TPU v7x, 256 devices: a whole 4x4x8 slice. The times are simulated.
256 devices in a mesh: tm: 16 (over x_lo, y, core), dp: 16 (over z, x_hi).
Axes of the slice: x: 4 (x_hi: 2, x_lo: 2; x = x_hi * 2 + x_lo), y: 4, z: 8, core: 2. Of those that a mesh axis runs over, the one named last changes fastest.
Arguments:
- tokens: bfloat16 [2, 32, 1024, 1536], P(None, 'tm', 'dp'), may hold values from -6 to 6
- space_gain: float32 [1536], replicated, may hold values from 0.25 to 1.75
- spatial_project: bfloat16 [1536, 2304], P('dp'), may hold values from -0.8164966 to 0.8164966
- spatial_output: bfloat16 [768, 1536], P('dp'), may hold values from -0.21875 to 0.21875
- time_gain: float32 [1536], replicated, may hold values from 0.25 to 1.75
- temporal_project: bfloat16 [1536, 2304], P('dp'), may hold values from -0.8164966 to 0.8164966
Outputs:
- spatial_branch: bfloat16 [2, 32, 1024, 1536], P(None, 'tm', 'dp')
- temporal_context: bfloat16 [2, 32, 1024, 768], P(None, 'tm', 'dp')
All inputs are finite; a program needn't handle non-finite values.
Results may differ from a plain program's by a relative error of at most 0.02.
Values may be sent and summed in bfloat16 or wider, within the bound.
No kernel may reach another device: no remote copies, remote signals or barrier semaphores. Data moves between devices by JAX's collectives and lax.ppermute only.
A program may use at most 128 MiB of HBM per device.

v0:
```python
import math

import jax
import jax.numpy as jnp
from jax import lax
from jax.sharding import PartitionSpec as P

HEADS = 8


EPSILON = 1e-05


def normalize(values, gain):
    factor = lax.rsqrt(jnp.mean(values * values, axis=-1, keepdims=True) + EPSILON)
    return (values * factor * gain).astype(jnp.bfloat16)


def row_folder(left, piece):
    return jnp.dot(left, piece, preferred_element_type=jnp.float32)


def temporal_attend(projected):
    batch, frames, columns, width3 = projected.shape
    inner = width3 // 3
    hsize = inner // HEADS
    query = projected[..., :inner].reshape(batch, frames, columns, HEADS, hsize)
    keys = projected[..., inner : 2 * inner].reshape(batch, frames, columns, HEADS, hsize)
    values = projected[..., 2 * inner :].reshape(batch, frames, columns, HEADS, hsize)
    scores = jnp.einsum("bfnhd,bgnhd->bnhfg", query, keys, preferred_element_type=jnp.float32) * (
        1.0 / math.sqrt(hsize)
    )
    causal = lax.broadcasted_iota(jnp.int32, (frames, frames), 0) >= lax.broadcasted_iota(
        jnp.int32, (frames, frames), 1
    )
    scores = jnp.where(causal, scores, -jnp.inf)
    peak = jnp.max(scores, axis=-1, keepdims=True)
    weights = jnp.exp(scores - peak)
    summed = jnp.sum(weights, axis=-1)
    context = jnp.einsum(
        "bnhfg,bgnhd->bfnhd",
        weights.astype(jnp.bfloat16),
        values,
        preferred_element_type=jnp.float32,
    )
    context = context / jnp.transpose(summed, (0, 3, 1, 2))[..., None]
    return context.astype(jnp.bfloat16).reshape(batch, frames, columns, inner)


def per_device(tokens, space_gain, spatial_project, spatial_output, time_gain, temporal_project):
    batch, frames_dev, per_frame, width = tokens.shape
    rows = batch * frames_dev * per_frame
    inner = spatial_project.shape[1] // 3
    hsize = inner // HEADS
    factor = 1.0 / math.sqrt(hsize)
    normed = normalize(tokens.astype(jnp.float32), space_gain).reshape(rows, width)
    projected = row_folder(normed, lax.all_gather(spatial_project, "dp", axis=0, tiled=True))
    projected = projected.astype(jnp.bfloat16).reshape(batch, frames_dev, per_frame, 3 * inner)
    query = projected[..., :inner].reshape(batch, frames_dev, per_frame, HEADS, hsize)
    keys_values = projected[..., inner:]
    start_peak = jnp.full((batch, frames_dev, HEADS, per_frame), -jnp.inf, jnp.float32)
    start_sum = jnp.zeros((batch, frames_dev, HEADS, per_frame), jnp.float32)
    start_accum = jnp.zeros((batch, frames_dev, per_frame, HEADS, hsize), jnp.float32)
    piece = lax.all_gather(keys_values, "dp", axis=2, tiled=True)
    summed = start_sum
    accum = start_accum
    count = piece.shape[2]
    keys = piece[..., :inner].reshape(batch, frames_dev, count, HEADS, hsize)
    values = piece[..., inner:].reshape(batch, frames_dev, count, HEADS, hsize)
    scores = (
        jnp.einsum("bfqhd,bfkhd->bfhqk", query, keys, preferred_element_type=jnp.float32) * factor
    )
    new_peak = jnp.max(scores, axis=-1)
    shrink = jnp.exp(start_peak - new_peak)
    weights = jnp.exp(scores - new_peak[..., None])
    summed = summed * shrink + jnp.sum(weights, axis=-1)
    update = jnp.einsum(
        "bfhqk,bfkhd->bfqhd",
        weights.astype(jnp.bfloat16),
        values,
        preferred_element_type=jnp.float32,
    )
    accum = accum * jnp.transpose(shrink, (0, 1, 3, 2))[..., None] + update
    final_peak, summed, accum = (new_peak, summed, accum)
    context = (
        (accum / jnp.transpose(summed, (0, 1, 3, 2))[..., None])
        .astype(jnp.bfloat16)
        .reshape(rows, inner)
    )
    branch = row_folder(context, lax.all_gather(spatial_output, "dp", axis=0, tiled=True))
    branch = branch.astype(jnp.bfloat16).reshape(batch, frames_dev, per_frame, width)
    mixed = tokens.astype(jnp.float32) + branch.astype(jnp.float32)
    normed_time = normalize(mixed, time_gain)
    flat_time = normed_time.reshape(rows, width)
    time_proj = row_folder(flat_time, lax.all_gather(temporal_project, "dp", axis=0, tiled=True))
    time_proj = time_proj.astype(jnp.bfloat16).reshape(batch, frames_dev, per_frame, 3 * inner)
    context_cols = temporal_attend(
        lax.all_to_all(time_proj, "tm", split_axis=2, concat_axis=1, tiled=True)
    )
    temporal_context = lax.all_to_all(context_cols, "tm", split_axis=1, concat_axis=2, tiled=True)
    return (branch, temporal_context)


def solution(mesh):
    in_specs = (P(None, "tm", "dp", None), P(), P("dp", None), P("dp", None), P(), P("dp", None))
    out_specs = (P(None, "tm", "dp", None), P(None, "tm", "dp", None))
    return jax.shard_map(
        per_device, mesh=mesh, in_specs=in_specs, out_specs=out_specs, check_vma=False
    )
```

profile of v0, /device:TPU:1, one launch (start us, length us, event | category | flops | bytes accessed | tf_op | source)
XLA Modules:
  0.0 581.5 jit_solution(15079823783434560837)
XLA Ops:
  7.2 0.7 all-gather.5.cloned.1.call-update
  7.9 1.4 fusion.6
  9.3 1.4 fusion.8
  10.7 126.3 %all-gather.5.cloned.1.call-done = bf16[1536,2304]{1,0:T(8,128)(2,1)} async-done(((bf16[96,2304]{1,0:T(8,128)(2,1)}), bf16[1536,2304]{1,0:T(8,128)(2,1)}) %all-gather.5.cloned.1.call-update) | async-done | bytes 7077904 | tf_op jit(solution)/shard_map/all_gather | solution.py:57
  137.0 5.0 convolution_convert_fusion.1
  142.0 0.9 slice.29
  143.0 0.7 all-gather.9.cloned.1.call-update
  144.3 0.6 reshape.68
  144.9 173.6 %all-gather.7.cloned.1.call-done = bf16[2,2,1024,1536]{3,2,1,0:T(8,128)(2,1)} async-done(((bf16[2,2,64,1536]{3,2,1,0:T(8,128)(2,1)}), bf16[2,2,1024,1536]{3,2,1,0:T(8,128)(2,1)}) %all-gather.7.cloned.1.call-update) | async-done | bytes 12582928 | tf_op jit(solution)/shard_map/all_gather | solution.py:64
  318.5 10.4 %fusion.34 = (bf16[2,2,1024,768]{3,2,1,0:T(8,128)(2,1)}, bf16[2,2,1024,768]{3,2,1,0:T(8,128)(2,1)}) fusion(bf16[2,2,1024,1536]{3,2,1,0:T(8,128)(2,1)} %all-gather.7.cloned.1.call-done), kind=kLoop, calls=%fused_computation.42 | loop fusion | bytes 25165824 | tf_op jit(solution)/shard_map/slice | solution.py:68
  328.9 8.6 %copy.41 = bf16[2,2,1024,768]{2,3,1,0:T(8,128)(2,1)} copy(bf16[2,2,1024,768]{3,2,1,0:T(8,128)(2,1)} %get-tuple-element.6) | data formatting | bytes 12582912 | tf_op jit(solution)/shard_map/slice | solution.py:68
  337.5 8.6 %copy.43 = bf16[2,2,1024,768]{2,3,1,0:T(8,128)(2,1)} copy(bf16[2,2,1024,768]{3,2,1,0:T(8,128)(2,1)} %get-tuple-element.7) | data formatting | bytes 12582912 | tf_op jit(solution)/shard_map/slice | solution.py:69
  346.2 4.3 multiply_reduce_fusion
  350.4 1.8 fusion
  352.3 5.0 fusion.21
  357.7 0.4 reshape.71
  358.1 44.3 %all-gather.9.cloned.1.call-done = bf16[768,1536]{1,0:T(8,128)(2,1)} async-done(((bf16[48,1536]{1,0:T(8,128)(2,1)}), bf16[768,1536]{1,0:T(8,128)(2,1)}) %all-gather.9.cloned.1.call-update) | async-done | bytes 2359312 | tf_op jit(solution)/shard_map/all_gather | solution.py:90
  402.4 2.4 convolution_convert_fusion.2
  405.5 122.4 %all-gather.11.cloned.1.call-done = bf16[1536,2304]{1,0:T(8,128)(2,1)} async-done(((bf16[96,2304]{1,0:T(8,128)(2,1)}), bf16[1536,2304]{1,0:T(8,128)(2,1)}) %all-gather.11.cloned.1.call-update) | async-done | bytes 7077904 | tf_op jit(solution)/shard_map/all_gather | solution.py:95
  527.9 5.0 convolution_convert_fusion
  532.9 2.2 copy.45
  535.1 5.4 all-to-all-start
  540.5 17.3 %all-to-all-done = bf16[2,2,64,2304]{3,1,0,2:T(2,128)(2,1)S(1)} async-done(((bf16[2,2,64,2304]{3,1,0,2:T(2,128)(2,1)}), bf16[2,2,64,2304]{3,1,0,2:T(2,128)(2,1)S(1)}, u32[]{:S(2)}, u32[]{:S(2)}) %all-to-all-start) | async-done | bytes 1179680 | tf_op jit(solution)/shard_map/all_to_all | solution.py:98
  557.8 0.5 copy.47
  558.2 0.4 fusion.35
  558.7 0.4 reshape.80
  559.4 0.4 reshape.79
  559.8 0.5 fusion.36
  560.6 0.6 fusion.17
  561.4 0.5 reshape.82
  562.0 11.9 %all_to_all.36 = bf16[2,32,4,768]{3,2,0,1:T(4,128)(2,1)S(1)} all-to-all(bf16[2,32,4,768]{3,2,0,1:T(4,128)(2,1)S(1)} %reshape.82), channel_id=1, replica_groups=mesh['tm'=16,'dp'=16] {'tm'}, dimensions={1} | all-to-all | bytes 786432 | tf_op jit(solution)/shard_map/all_to_all | solution.py:100
  574.2 0.8 copy.59
  (25 shorter events, 2.9 us)
Async XLA Ops:
  7.2 129.8 %all-gather.5.cloned.1.call-start = ((), (), s32[]{:S(2)}) async-start(), calls=%async_computation.2 | async-start | bytes 7520256 | tf_op jit(solution)/shard_map/all_gather | solution.py:57
  7.9 310.6 %all-gather.7.cloned.1.call-start = ((), (), s32[]{:S(2)}) async-start(), calls=%async_computation.3 | async-start | bytes 13369344 | tf_op jit(solution)/shard_map/all_gather | solution.py:64
  143.0 259.4 %all-gather.9.cloned.1.call-start = ((), (), s32[]{:S(2)}) async-start(), calls=%async_computation.4 | async-start | bytes 2506752 | tf_op jit(solution)/shard_map/all_gather | solution.py:90
  143.7 384.1 %all-gather.11.cloned.1.call-start = ((), (), s32[]{:S(2)}) async-start(), calls=%async_computation.5 | async-start | bytes 7520256 | tf_op jit(solution)/shard_map/all_gather | solution.py:95
  352.3 52.5 %copy-start = (bf16[2,2,64,1536]{3,2,1,0:T(8,128)(2,1)S(1)}, bf16[2,2,64,1536]{3,2,1,0:T(8,128)(2,1)}, u32[]{:S(2)}) copy-start(bf16[2,2,64,1536]{3,2,1,0:T(8,128)(2,1)} %param.6) | copy-start | bytes 2359300
  357.3 47.9 %copy-start.2 = (f32[1536]{0:T(1024)S(1)}, f32[1536]{0:T(1024)}, u32[]{:S(2)}) copy-start(f32[1536]{0:T(1024)} %param.10) | copy-start | bytes 18436
  404.8 128.1 %copy-start.1 = (bf16[256,1536]{1,0:T(8,128)(2,1)}, bf16[256,1536]{1,0:T(8,128)(2,1)S(1)}, u32[]{:S(2)}) copy-start(bf16[256,1536]{1,0:T(8,128)(2,1)S(1)} %convolution_convert_fusion.2) | copy-start | bytes 2359300
  535.1 22.7 %all-to-all-start = ((bf16[2,2,64,2304]{3,1,0,2:T(2,128)(2,1)}), bf16[2,2,64,2304]{3,1,0,2:T(2,128)(2,1)S(1)}, u32[]{:S(2)}, u32[]{:S(2)}) async-start(bf16[2,2,64,2304]{3,1,0,2:T(2,128)(2,1)} %copy.45), calls=%async_computation | async-start | bytes 2359296 | tf_op jit(solution)/shard_map/all_to_all | solution.py:98
Sparse Core Ops, SparseCore 0:
  10.6 126.3 all-gather.4
  143.1 175.3 all-gather.6
  321.1 81.1 all-gather.8
  404.8 123.0 all-gather.10
where the time goes:
time: 582 us
  waiting for transfers between devices  486 us (84%)
  local copies, waits for them, and re-layouts  35.9 us (6%)
  matrix products  22.8 us (4%)
  between operations  14 us (2%)
  blocking collectives  11.9 us (2%)
    all_gather x1, waiting for transfers between devices, per_device(): piece = lax.all_gather(keys_values, 'dp', axis=2, tiled=True)  174 us
    all_gather x1, waiting for transfers between devices, per_device(): lax.all_gather(spatial_project, 'dp', axis=0, tiled=True)  126 us
    all_gather x1, waiting for transfers between devices, per_device(): lax.all_gather(temporal_project, 'dp', axis=0, tiled=True)  122 us
    all_gather x1, waiting for transfers between devices, per_device(): lax.all_gather(spatial_output, 'dp', axis=0, tiled=True)  44.3 us
    slice x2, local copies, waits for them, and re-layouts, per_device(): keys = piece[..., :inner].reshape(batch, frames_dev, count, HEADS, hsize)  19 us
    all_to_all x1, waiting for transfers between devices, per_device(): lax.all_to_all(time_proj, 'tm', split_axis=2, concat_axis=1, tiled=True)  17.3 us
    dot_general x3, matrix products, row_folder(): return jnp.dot(left, piece, preferred_element_type=jnp.float32)  12.4 us
    all_to_all x1, blocking collectives, per_device(): lax.all_to_all(context_cols, 'tm', split_axis=1, concat_axis=2, tiled=True)  11.9 us
  transfers between devices with their start and end apart: 5, of which 5 were waited for; matrix products, arithmetic and copies ran while one was open for 8% of the time, Pallas kernels for 0%

commit v1 on v0

v1 whole, which is shorter than its diff:
```python
import math

import jax
import jax.numpy as jnp
from jax import lax
from jax.experimental import pallas as pl
from jax.experimental.pallas import tpu as pltpu
from jax.sharding import Mesh
from jax.sharding import PartitionSpec as P

HEADS = 8
HSIZE = 96
WIDTH = 1536
INNER = 768
HALF = INNER // 2
EPSILON = 1e-05
SCALE = math.log2(math.e) / math.sqrt(HSIZE)
TM = ("x_lo", "y", "core")
DP = ("z", "x_hi")
BF16 = jnp.bfloat16
F32 = jnp.float32


def params():
    return pltpu.CompilerParams(vmem_limit_bytes=56 * 1024 * 1024)


def dot(a, b):
    return jnp.dot(a, b, preferred_element_type=F32)


def dot_nt(a, b):
    return lax.dot_general(a, b, (((1,), (1,)), ((), ())), preferred_element_type=F32)


def shuffle(size, rows):
    column = lax.broadcasted_iota(jnp.int32, (1, size), 1)
    per = 16 * rows
    source = (column % per) // rows * per + column // per * rows + column % rows
    return (lax.broadcasted_iota(jnp.int32, (size, size), 0) == source).astype(BF16)


def norm_kernel(x_ref, gain_ref, shuffle_ref, out_ref):
    x = x_ref[...].astype(F32)
    factor = lax.rsqrt(jnp.mean(x * x, axis=-1, keepdims=True) + EPSILON)
    normed = (x * factor * gain_ref[...]).astype(BF16)
    out_ref[...] = dot(normed, shuffle_ref[...]).astype(BF16)


def project_kernel(own_ref, other_ref, w_ref, q_ref, kv_ref):
    step = pl.program_id(0)
    w = w_ref[...].reshape(WIDTH, HALF)
    rows = own_ref.shape[0]
    first = dot(own_ref[...], w).astype(BF16)
    second = dot(other_ref[...], w).astype(BF16)

    @pl.when(step == 0)
    def _():
        q_ref[:rows] = first
        q_ref[rows:] = second

    @pl.when(step > 0)
    def _():
        kv_ref[0, :rows] = first
        kv_ref[0, rows:] = second


def spatial_kernel(xh_ref, q_ref, kv_ref, kvo_ref, out_ref):
    rows = q_ref.shape[0]
    for h in range(HEADS // 2):
        lanes = slice(h * HSIZE, (h + 1) * HSIZE)
        q = q_ref[:, lanes]
        s0 = dot_nt(q, kv_ref[0, :, lanes])
        s1 = dot_nt(q, kvo_ref[0, :, lanes])
        peak = jnp.maximum(
            jnp.max(s0, axis=-1, keepdims=True), jnp.max(s1, axis=-1, keepdims=True)
        )
        e0 = jnp.exp2((s0 - peak) * SCALE)
        e1 = jnp.exp2((s1 - peak) * SCALE)
        summed = jnp.sum(e0, axis=-1, keepdims=True) + jnp.sum(e1, axis=-1, keepdims=True)
        acc = dot(e0.astype(BF16), kv_ref[1, :, lanes]) + dot(e1.astype(BF16), kvo_ref[1, :, lanes])
        out_ref[:, 0, :, lanes] = (acc / summed).astype(BF16).reshape(rows // 32, 32, HSIZE)


def output_kernel(ctx_ref, tok_ref, w_ref, gain_ref, sh3_ref, sh6_ref, branch_ref, out_ref):
    rows = tok_ref.shape[0]
    ctx = jnp.concatenate(
        [ctx_ref[:, 0].reshape(rows, HALF), ctx_ref[:, 1].reshape(rows, HALF)], axis=1
    )
    ctx = dot(ctx, sh3_ref[...]).astype(BF16)
    mixed = []
    total = jnp.zeros((rows, 1), F32)
    for cb in range(4):
        lanes = slice(cb * HALF, (cb + 1) * HALF)
        w = w_ref[:, cb * 48 : (cb + 1) * 48, :].reshape(INNER, HALF)
        branch = dot(ctx, w).astype(BF16)
        branch_ref[:, lanes] = branch
        mix = tok_ref[:, lanes].astype(F32) + branch.astype(F32)
        mixed.append(mix)
        total += jnp.sum(mix * mix, axis=-1, keepdims=True)
    factor = lax.rsqrt(total * (1.0 / WIDTH) + EPSILON)
    target = lax.broadcasted_iota(jnp.int32, (rows, rows), 0)
    source = (target % 32) // 4 * 32 + target // 32 * 4 + target % 4
    swap = (lax.broadcasted_iota(jnp.int32, (rows, rows), 1) == source).astype(BF16)
    normed = jnp.concatenate(
        [
            (mix * factor * gain_ref[:, cb * HALF : (cb + 1) * HALF]).astype(BF16)
            for cb, mix in enumerate(mixed)
        ],
        axis=1,
    )
    normed = dot(swap, normed).astype(BF16)
    out_ref[...] = dot(normed, sh6_ref[...]).astype(BF16)


def temporal_kernel(x_ref, w_ref, out_ref, q_scr, k_scr):
    step = pl.program_id(0)
    rows = x_ref.shape[0]
    projected = dot(x_ref[...], w_ref[...].reshape(WIDTH, HALF)).astype(BF16)
    kind = step % 3

    @pl.when(kind == 0)
    def _():
        q_scr[...] = projected

    @pl.when(kind == 1)
    def _():
        k_scr[...] = projected

    @pl.when(kind == 2)
    def _():
        r = lax.broadcasted_iota(jnp.int32, (rows, rows), 0)
        s = lax.broadcasted_iota(jnp.int32, (rows, rows), 1)
        same = (r % 4 == s % 4) & ((r // 8) % 2 == (s // 8) % 2)
        seen = (r // 16) * 2 + (r // 4) % 2 >= (s // 16) * 2 + (s // 4) % 2
        mask = same & seen
        for h in range(HEADS // 2):
            lanes = slice(h * HSIZE, (h + 1) * HSIZE)
            scores = dot_nt(q_scr[:, lanes], k_scr[:, lanes])
            scores = jnp.where(mask, scores, -jnp.inf)
            peak = jnp.max(scores, axis=-1, keepdims=True)
            weights = jnp.exp2((scores - peak) * SCALE)
            summed = jnp.sum(weights, axis=-1, keepdims=True)
            acc = dot(weights.astype(BF16), projected[:, lanes])
            out_ref[:, lanes] = (acc / summed).astype(BF16)


def whole(shape):
    return pl.BlockSpec(shape, lambda *_: (0,) * len(shape))


def pick(first, a, b, axis):
    return jnp.where(first, jnp.concatenate([a, b], axis), jnp.concatenate([b, a], axis))


def per_device(tokens, space_gain, spatial_project, spatial_output, time_gain, temporal_project):
    core = lax.axis_index("core")
    x_hi = lax.axis_index("x_hi")
    tm = lax.axis_index(TM)
    swap = [(0, 1), (1, 0)]
    sh6 = shuffle(WIDTH, 6)
    sh3 = shuffle(INNER, 3)

    wq = lax.dynamic_slice_in_dim(spatial_project, tm * 6, 6, 0)
    wq = wq.reshape(6, 3, 2, HALF).transpose(2, 1, 0, 3).reshape(2, 18, HALF)
    wo = lax.dynamic_slice_in_dim(spatial_output, tm * 3, 3, 0)
    wo = wo.reshape(3, 4, HALF).transpose(1, 0, 2).reshape(12, HALF)
    wt = lax.dynamic_slice_in_dim(temporal_project, tm * 6, 6, 0)
    wt = wt.reshape(6, 6, HALF).transpose(1, 0, 2).reshape(36, HALF)
    chunk = jnp.stack([jnp.concatenate([wo, wq[i], wt], 0) for i in range(2)])
    chunk = jnp.broadcast_to(chunk[None], (8, 2, 66, HALF)).reshape(16, 66, HALF)
    got = lax.all_to_all(chunk, DP, 0, 0, tiled=True)
    w1 = jnp.concatenate(
        [
            got[:, :12].reshape(16, 4, 3, HALF).transpose(1, 0, 2, 3).reshape(192, HALF),
            got[:, 12:30].reshape(16, 3, 6, HALF).transpose(1, 0, 2, 3).reshape(288, HALF),
        ],
        0,
    )
    w2 = got[:, 30:].reshape(16, 6, 6, HALF).transpose(1, 0, 2, 3).reshape(576, HALF)
    w1 = lax.all_gather(w1, TM, axis=0, tiled=False)
    w2 = lax.all_gather(w2, TM, axis=0, tiled=False)

    halves = tokens.reshape(4, 2, 32, WIDTH)
    keep = lax.dynamic_index_in_dim(halves, core, 1, keepdims=False)
    send = lax.dynamic_index_in_dim(halves, 1 - core, 1, keepdims=False)
    frames = pick(core == 0, keep, lax.ppermute(send, "core", swap), 0).reshape(256, WIDTH)
    normed = pl.pallas_call(
        norm_kernel,
        out_shape=jax.ShapeDtypeStruct((256, WIDTH), BF16),
        compiler_params=params(),
        name="space_norm",
    )(frames, space_gain.reshape(1, WIDTH), sh6)
    own = lax.all_to_all(normed.reshape(8, 32, WIDTH), "z", 0, 0, tiled=True)
    other = lax.ppermute(own, "x_hi", swap)
    q, kv = pl.pallas_call(
        project_kernel,
        grid=(3,),
        in_specs=[
            whole((256, WIDTH)),
            whole((256, WIDTH)),
            pl.BlockSpec((16, 96, HALF), lambda i: (0, i + 2, 0)),
        ],
        out_specs=[
            whole((512, HALF)),
            pl.BlockSpec((1, 512, HALF), lambda i: (jnp.maximum(i - 1, 0), 0, 0)),
        ],
        out_shape=[
            jax.ShapeDtypeStruct((512, HALF), BF16),
            jax.ShapeDtypeStruct((2, 512, HALF), BF16),
        ],
        compiler_params=params(),
        name="space_project",
    )(own.reshape(256, WIDTH), other.reshape(256, WIDTH), w1)
    kvo = lax.ppermute(kv, "core", swap)
    ctx = pl.pallas_call(
        spatial_kernel,
        grid_spec=pltpu.PrefetchScalarGridSpec(
            num_scalar_prefetch=1,
            grid=(2, 2),
            in_specs=[
                pl.BlockSpec((128, HALF), lambda i, j, xh: (i * 2 + j, 0)),
                whole((2, 512, HALF)),
                whole((2, 512, HALF)),
            ],
            out_specs=pl.BlockSpec(
                (4, 1, 32, HALF), lambda i, j, xh: (j, (i + xh[0]) % 2, 0, 0)
            ),
        ),
        out_shape=jax.ShapeDtypeStruct((8, 2, 32, HALF), BF16),
        compiler_params=params(),
        name="space_attend",
    )(x_hi.reshape(1).astype(jnp.int32), q, kv, kvo)
    ctx = lax.all_to_all(ctx.reshape(16, 32, HALF), DP, 0, 0, tiled=True)
    branch, normed_time = pl.pallas_call(
        output_kernel,
        grid=(1,),
        in_specs=[
            whole((8, 2, 32, HALF)),
            whole((256, WIDTH)),
            whole((16, 192, HALF)),
            whole((1, WIDTH)),
            whole((INNER, INNER)),
            whole((WIDTH, WIDTH)),
        ],
        out_specs=[whole((256, WIDTH)), whole((256, WIDTH))],
        out_shape=[
            jax.ShapeDtypeStruct((256, WIDTH), BF16),
            jax.ShapeDtypeStruct((256, WIDTH), BF16),
        ],
        compiler_params=params(),
        name="space_output",
    )(ctx.reshape(8, 2, 32, HALF), frames, w1, time_gain.reshape(1, WIDTH), sh3, sh6)
    branch = branch.reshape(8, 32, WIDTH)
    mine = lax.dynamic_slice_in_dim(branch, core * 4, 4, 0)
    theirs = lax.dynamic_slice_in_dim(branch, (1 - core) * 4, 4, 0)
    back = lax.ppermute(theirs, "core", swap)
    branch = pick(core == 0, mine[:, None], back[:, None], 1).reshape(tokens.shape)

    columns = lax.all_to_all(normed_time.reshape(8, 32, WIDTH), TM[:2], 0, 0, tiled=True)
    context = pl.pallas_call(
        temporal_kernel,
        grid=(6,),
        in_specs=[
            whole((256, WIDTH)),
            pl.BlockSpec((16, 96, HALF), lambda i: (0, i % 3 * 2 + i // 3, 0)),
        ],
        out_specs=pl.BlockSpec((256, HALF), lambda i: (0, i // 3)),
        out_shape=jax.ShapeDtypeStruct((256, INNER), BF16),
        scratch_shapes=[pltpu.VMEM((256, HALF), BF16), pltpu.VMEM((256, HALF), BF16)],
        compiler_params=params(),
        name="time_attend",
    )(columns.reshape(256, WIDTH), w2)
    context = lax.all_to_all(context.reshape(16, 16, INNER), TM, 0, 0, tiled=True)
    context = context.reshape(8, 2, 2, 2, 4, INNER).transpose(2, 3, 1, 0, 4, 5)
    return branch, context.reshape(2, 2, 64, INNER)


def solution(mesh):
    fine = Mesh(mesh.devices.reshape(2, 4, 2, 8, 2), TM + DP)
    in_specs = (P(None, TM, DP, None), P(), P(DP, None), P(DP, None), P(), P(DP, None))
    out_specs = (P(None, TM, DP, None), P(None, TM, DP, None))
    return jax.shard_map(
        per_device, mesh=fine, in_specs=in_specs, out_specs=out_specs, check_vma=False
    )
```

time: 582 us -> 214 us (0.37)
  waiting for transfers between devices: 486 us -> 50.7 us
  blocking collectives: 11.9 us -> 63.7 us
  Pallas kernels: 0 us -> 41.3 us
  local copies, waits for them, and re-layouts: 35.9 us -> 10.8 us
  matrix products: 22.8 us -> 0 us
  starting transfers between devices: 5.72 us -> 25 us
    all_gather x4 -> x2, waiting for transfers between devices: 467 us -> 0.01 us  [the longest x1 0.01 us: per_device(): w1 = lax.all_gather(w1, TM, axis=0, tiled=False)]
    all_to_all x1 -> x2, blocking collectives: 11.9 us -> 63.7 us  [the longest x1 36.7 us: per_device(): got = lax.all_to_all(chunk, DP, 0, 0, tiled=True)]
    pallas_call x0 -> x5, Pallas kernels: none -> 41.3 us  [the longest x1 12 us: per_device(): pl.pallas_call(spatial_kernel, grid_spec=pltpu.PrefetchScalarGridSpec(num...]
    slice x6, local copies, waits for them, and re-layouts: 29 us -> 0.32 us  [the longest x1 0.15 us: per_device(): got[:, 30:].reshape(16, 6, 6, HALF).transpose(1, 0, 2, 3).reshape(576, HALF)]
    ppermute x0 -> x4, waiting for transfers between devices: none -> 25.9 us  [the longest x1 23.7 us: per_device(): other = lax.ppermute(own, 'x_hi', swap)]
    dot_general x7 -> x0, matrix products: 22.8 us -> none  [the longest x3 12.4 us: row_folder(): return jnp.dot(left, piece, preferred_element_type=jnp.float32)]
    all_to_all x1 -> x3, starting transfers between devices: 5.39 us -> 16.5 us  [the longest x1 8.28 us: per_device(): lax.all_to_all(context.reshape(16, 16, INNER), TM, 0, 0, tiled=True)]
    ppermute x0 -> x4, starting transfers between devices: none -> 8.49 us  [the longest x1 3 us: per_device(): kvo = lax.ppermute(kv, 'core', swap)]
  transfers between devices with their start and end apart: 5 -> 9, of which waited for: 5 -> 5; matrix products, arithmetic and copies ran while one was open for 8% -> 5% of each run, Pallas kernels for 0% -> 19%
where the time goes in v1:
time: 214 us
  blocking collectives  63.7 us (30%)
  waiting for transfers between devices  50.7 us (24%)
  Pallas kernels  41.3 us (19%)
  starting transfers between devices  25 us (12%)
  between operations  14.3 us (7%)
  local copies, waits for them, and re-layouts  10.8 us (5%)
  other arithmetic  7.66 us (4%)
    all_to_all x1, blocking collectives, per_device(): got = lax.all_to_all(chunk, DP, 0, 0, tiled=True)  36.7 us
    all_to_all x1, blocking collectives, per_device(): own = lax.all_to_all(normed.reshape(8, 32, WIDTH), 'z', 0, 0, tiled=True)  27.1 us
    ppermute x1, waiting for transfers between devices, per_device(): other = lax.ppermute(own, 'x_hi', swap)  23.7 us
    all_to_all x1, waiting for transfers between devices, per_device(): ctx = lax.all_to_all(ctx.reshape(16, 32, HALF), DP, 0, 0, tiled=True)  13 us
    pallas_call x1, Pallas kernels, per_device(): pl.pallas_call(spatial_kernel, grid_spec=pltpu.PrefetchScalarGridSpec(num...  12 us
    pallas_call x1, Pallas kernels, per_device(): pl.pallas_call(temporal_kernel, grid=(6,), in_specs=[whole((256, WIDTH)),...  10.4 us
    all_to_all x1, starting transfers between devices, per_device(): lax.all_to_all(context.reshape(16, 16, INNER), TM, 0, 0, tiled=True)  8.28 us
    pallas_call x1, Pallas kernels, per_device(): pl.pallas_call(output_kernel, grid=(1,), in_specs=[whole((8, 2, 32, HALF)...  7.78 us
  transfers between devices with their start and end apart: 9, of which 5 were waited for; matrix products, arithmetic and copies ran while one was open for 5% of the time, Pallas kernels for 19%

profile of v1, /device:TPU:1, one launch (start us, length us, event | category | flops | bytes accessed | tf_op | source)
XLA Modules:
  0.0 213.6 jit_solution(7971404621070694009)
XLA Ops:
  7.2 1.0 constant_dynamic-slice_fusion.1
  8.6 36.7 %all_to_all.25 = bf16[16,66,384]{2,1,0:T(8,128)(2,1)S(1)} all-to-all(bf16[16,66,384]{2,1,0:T(8,128)(2,1)S(1)} %bitcast.49), channel_id=1, replica_groups=mesh['x_lo'=2,'y'=4,'core'=2,'z'=8,'x_hi'=2] {'z','x_hi'}, dimensions={0} | all-to-all | bytes 1622016 | tf_op jit(solution)/shard_map/all_to_all | solution.py:172
  45.8 0.8 pad_maximum_fusion
  47.0 0.9 all_gather_reshape.3
  48.1 2.3 %collective-permute-start = (bf16[4,32,1536]{2,1,0:T(8,128)(2,1)S(1)}, bf16[4,32,1536]{2,1,0:T(8,128)(2,1)S(1)}, u32[]{:S(2)}, u32[]{:S(2)}) collective-permute-start(bf16[4,32,1536]{2,1,0:T(8,128)(2,1)S(1)} %get-tuple-element.13), channel_id=1, source_target_pairs={{0,16},{16,0},{1,17},{17,1},{2,18},{18,2},{3,19},{19,3},{4,20},{20... | collective-permute-start | bytes 1179656 | tf_op jit(solution)/shard_map/ppermute | solution.py:187
  50.4 4.2 %fusion.shuffle_ref.sh6_ref = bf16[1536,1536]{1,0:T(8,128)(2,1)} fusion(s32[1536]{0:T(1024)S(1)} %fusion.24), kind=kLoop, calls=%fused_computation.1 | loop fusion | flops 4718592 | bytes 4724736 | tf_op jit(solution)/shard_map/convert_element_type | solution.py:40
  55.2 1.0 maximum_select_fusion
  56.2 5.0 %space_norm.1 = bf16[256,1536]{1,0:T(8,128)(2,1)} custom-call(bf16[256,1536]{1,0:T(8,128)(2,1)} %bitcast.47, f32[1,1536]{1,0:T(1,128)} %reshape.244.gain_ref, bf16[1536,1536]{1,0:T(8,128)(2,1)} %fusion.shuffle_ref.sh6_ref), custom_call_target="tpu_custom_call" | custom-call | tf_op jit(solution)/shard_map/space_norm/pallas_call | solution.py:188
  61.3 27.1 %all_to_all.26 = bf16[8,32,1536]{2,1,0:T(8,128)(2,1)S(1)} all-to-all(bf16[8,32,1536]{2,1,0:T(8,128)(2,1)} %bitcast.51), channel_id=1, replica_groups=mesh['x_lo'=2,'y'=4,'core'=2,'z'=8,'x_hi'=2] {'z'}, dimensions={0} | all-to-all | bytes 1572864 | tf_op jit(solution)/shard_map/all_to_all | solution.py:194
  88.8 23.7 %collective-permute-done.1 = bf16[8,32,1536]{2,1,0:T(8,128)(2,1)S(1)} collective-permute-done((bf16[8,32,1536]{2,1,0:T(8,128)(2,1)S(1)}, bf16[8,32,1536]{2,1,0:T(8,128)(2,1)S(1)}, u32[]{:S(2)}, u32[]{:S(2)}) %collective-permute-start.1) | collective-permute-done | bytes 786464 | tf_op jit(solution)/shard_map/ppermute | solution.py:195
  112.5 0.9 copy-done.5
  113.4 6.0 %space_project.1 = (bf16[512,384]{1,0:T(8,128)(2,1)}, bf16[2,512,384]{2,1,0:T(8,128)(2,1)}) custom-call(bf16[256,1536]{1,0:T(8,128)(2,1)} %bitcast.50, bf16[256,1536]{1,0:T(8,128)(2,1)} %bitcast.59, bf16[16,480,384]{2,1,0:T(8,128)(2,1)} %bitcast.45), custom_call_target="tpu_custom_call" | custom-call | tf_op jit(solution)/shard_map/space_project/pallas_call | solution.py:196
  119.5 3.0 %collective-permute-start.2 = (bf16[2,512,384]{2,1,0:T(8,128)(2,1)}, bf16[2,512,384]{2,1,0:T(8,128)(2,1)S(1)}, u32[]{:S(2)}, u32[]{:S(2)}) collective-permute-start(bf16[2,512,384]{2,1,0:T(8,128)(2,1)} %get-tuple-element.7.kv_ref), channel_id=1, source_target_pairs={{0,16},{16,0},{1,17},{17,1},{2,18},{18,2},{3,19},{19,3},{4,20},{20... | collective-permute-start | bytes 2359304 | tf_op jit(solution)/shard_map/ppermute | solution.py:215
  122.4 2.1 collective-permute-done.2.kvo_ref
  124.6 0.9 copy-done.4
  125.4 12.0 %space_attend.1 = bf16[8,2,32,384]{3,2,1,0:T(8,128)(2,1)} custom-call(s32[1]{0:T(128)} %bitcast.xh_ref, bf16[512,384]{1,0:T(8,128)(2,1)} %get-tuple-element.6.q_ref, bf16[2,512,384]{2,1,0:T(8,128)(2,1)} %get-tuple-element.7.kv_ref, bf16[2,512,384]{2,1,0:T(8,128)(2,1)} %copy-done.4), custom_call_target="tpu_custom_call" | custom-call | tf_op jit(solution)/shard_map/space_attend/pallas_call | solution.py:216
  137.5 3.7 %all-to-all-start.2 = ((bf16[16,32,384]{2,1,0:T(8,128)(2,1)}), bf16[16,32,384]{2,1,0:T(8,128)(2,1)S(1)}, u32[]{:S(2)}, u32[]{:S(2)}) async-start(bf16[16,32,384]{2,1,0:T(8,128)(2,1)} %bitcast.56), calls=%async_computation.2 | async-start | bytes 786432 | tf_op jit(solution)/shard_map/all_to_all | solution.py:234
  141.2 0.6 reshape.260.gain_ref
  141.9 1.4 fusion.1.sh3_ref
  143.3 13.0 %all-to-all-done.2 = bf16[16,32,384]{2,1,0:T(8,128)(2,1)S(1)} async-done(((bf16[16,32,384]{2,1,0:T(8,128)(2,1)}), bf16[16,32,384]{2,1,0:T(8,128)(2,1)S(1)}, u32[]{:S(2)}, u32[]{:S(2)}) %all-to-all-start.2) | async-done | bytes 393248 | tf_op jit(solution)/shard_map/all_to_all | solution.py:234
  156.2 0.7 copy-done.3
  157.0 7.8 %space_output.1 = (bf16[256,1536]{1,0:T(8,128)(2,1)}, bf16[256,1536]{1,0:T(8,128)(2,1)}) custom-call(bf16[8,2,32,384]{3,2,1,0:T(8,128)(2,1)} %bitcast.54, bf16[256,1536]{1,0:T(8,128)(2,1)} %bitcast.48, bf16[16,480,384]{2,1,0:T(8,128)(2,1)} %bitcast.46, f32[1,1536]{1,0:T(1,128)} %reshape.260.gain_ref, bf16[768,768]{1,0:T(8,128)(2,1)} %fusion.1.sh3_ref, ...), custom_call_target="tpu_custom_call" | custom-call | tf_op jit(solution)/shard_map/space_output/pallas_call | solution.py:235
  164.8 4.4 %all-to-all-start.3 = ((bf16[8,32,1536]{2,1,0:T(8,128)(2,1)}), bf16[8,32,1536]{2,1,0:T(8,128)(2,1)S(1)}, u32[]{:S(2)}, u32[]{:S(2)}) async-start(bf16[8,32,1536]{2,1,0:T(8,128)(2,1)} %bitcast.60), calls=%async_computation.3 | async-start | bytes 1572864 | tf_op jit(solution)/shard_map/all_to_all | solution.py:260
  169.2 1.2 dynamic-slice_bitcast_fusion
  170.4 2.7 %collective-permute-start.3 = (bf16[4,32,1536]{2,1,0:T(8,128)(2,1)S(1)}, bf16[4,32,1536]{2,1,0:T(8,128)(2,1)S(1)}, u32[]{:S(2)}, u32[]{:S(2)}) collective-permute-start(bf16[4,32,1536]{2,1,0:T(8,128)(2,1)S(1)} %get-tuple-element.11), channel_id=1, source_target_pairs={{0,16},{16,0},{1,17},{17,1},{2,18},{18,2},{3,19},{19,3},{4,20},{20... | collective-permute-start | bytes 1179656 | tf_op jit(solution)/shard_map/ppermute | solution.py:257
  173.1 4.4 %all-to-all-done.3 = bf16[8,32,1536]{2,1,0:T(8,128)(2,1)S(1)} async-done(((bf16[8,32,1536]{2,1,0:T(8,128)(2,1)}), bf16[8,32,1536]{2,1,0:T(8,128)(2,1)S(1)}, u32[]{:S(2)}, u32[]{:S(2)}) %all-to-all-start.3) | async-done | bytes 786464 | tf_op jit(solution)/shard_map/all_to_all | solution.py:260
  177.6 0.9 copy-done.2
  178.4 10.4 %time_attend.1 = bf16[256,768]{1,0:T(8,128)(2,1)} custom-call(bf16[256,1536]{1,0:T(8,128)(2,1)} %bitcast.52, bf16[16,576,384]{2,1,0:T(8,128)(2,1)} %all-gather.4.cloned.1.call-done.w_ref), custom_call_target="tpu_custom_call" | custom-call | tf_op jit(solution)/shard_map/time_attend/pallas_call | solution.py:261
  188.9 8.3 %all-to-all-start.4 = ((bf16[16,16,768]{2,1,0:T(8,128)(2,1)}), bf16[16,16,768]{2,1,0:T(8,128)(2,1)S(1)}, u32[]{:S(2)}, u32[]{:S(2)}) async-start(bf16[16,16,768]{2,1,0:T(8,128)(2,1)} %bitcast.55), calls=%async_computation.4 | async-start | bytes 786432 | tf_op jit(solution)/shard_map/all_to_all | solution.py:274
  197.3 1.0 copy.30
  198.3 7.4 %all-to-all-done.4 = bf16[16,16,768]{2,1,0:T(8,128)(2,1)S(1)} async-done(((bf16[16,16,768]{2,1,0:T(8,128)(2,1)}), bf16[16,16,768]{2,1,0:T(8,128)(2,1)S(1)}, u32[]{:S(2)}, u32[]{:S(2)}) %all-to-all-start.4) | async-done | bytes 393248 | tf_op jit(solution)/shard_map/all_to_all | solution.py:274
  205.9 0.8 reshape.267
  (53 shorter events, 2.8 us)
Async XLA Ops:
  7.2 1.2 copy-start
  7.2 105.3 %all-gather.6.cloned.1.call-start = ((), (), s32[]{:S(2)}) async-start(), calls=%async_computation.6 | async-start | bytes 6266880 | tf_op jit(solution)/shard_map/all_gather | solution.py:181
  45.3 2.7 %copy-start.6 = (bf16[2,2,64,1536]{3,2,1,0:T(8,128)(2,1)S(1)}, bf16[2,2,64,1536]{3,2,1,0:T(8,128)(2,1)}, u32[]{:S(2)}) copy-start(bf16[2,2,64,1536]{3,2,1,0:T(8,128)(2,1)} %param.6) | copy-start | bytes 2359300
  46.6 130.9 %all-gather.4.cloned.1.call-start = ((), (), s32[]{:S(2)}) async-start(), calls=%async_computation.5 | async-start | bytes 7520256 | tf_op jit(solution)/shard_map/all_gather | solution.py:182
  46.8 7.8 %copy-start.7 = (f32[1536]{0:T(1024)S(1)}, f32[1536]{0:T(1024)}, u32[]{:S(2)}) copy-start(f32[1536]{0:T(1024)} %param.7) | copy-start | bytes 18436
  48.1 7.2 %collective-permute-start = (bf16[4,32,1536]{2,1,0:T(8,128)(2,1)S(1)}, bf16[4,32,1536]{2,1,0:T(8,128)(2,1)S(1)}, u32[]{:S(2)}, u32[]{:S(2)}) collective-permute-start(bf16[4,32,1536]{2,1,0:T(8,128)(2,1)S(1)} %get-tuple-element.13), channel_id=1, source_target_pairs={{0,16},{16,0},{1,17},{17,1},{2,18},{18,2},{3,19},{19,3},{4,20},{20... | collective-permute-start | bytes 1179656 | tf_op jit(solution)/shard_map/ppermute | solution.py:187
  88.4 24.2 %copy-start.1 = (bf16[8,32,1536]{2,1,0:T(8,128)(2,1)}, bf16[8,32,1536]{2,1,0:T(8,128)(2,1)S(1)}, u32[]{:S(2)}) copy-start(bf16[8,32,1536]{2,1,0:T(8,128)(2,1)S(1)} %all_to_all.26) | copy-start | bytes 2359300
  88.4 24.2 %collective-permute-start.1 = (bf16[8,32,1536]{2,1,0:T(8,128)(2,1)S(1)}, bf16[8,32,1536]{2,1,0:T(8,128)(2,1)S(1)}, u32[]{:S(2)}, u32[]{:S(2)}) collective-permute-start(bf16[8,32,1536]{2,1,0:T(8,128)(2,1)S(1)} %all_to_all.26), channel_id=1, source_target_pairs={{0,1},{1,0},{2,3},{3,2},{4,5},{5,4},{6,7},{7,6},{8,9},{9,8},{10,11... | collective-permute-start | bytes 2359304 | tf_op jit(solution)/shard_map/ppermute | solution.py:195
  112.5 0.9 copy-start.5
  113.4 27.8 %copy-start.8 = (f32[1536]{0:T(1024)S(1)}, f32[1536]{0:T(1024)}, u32[]{:S(2)}) copy-start(f32[1536]{0:T(1024)} %param.10) | copy-start | bytes 18436
  119.5 5.1 %collective-permute-start.2 = (bf16[2,512,384]{2,1,0:T(8,128)(2,1)}, bf16[2,512,384]{2,1,0:T(8,128)(2,1)S(1)}, u32[]{:S(2)}, u32[]{:S(2)}) collective-permute-start(bf16[2,512,384]{2,1,0:T(8,128)(2,1)} %get-tuple-element.7.kv_ref), channel_id=1, source_target_pairs={{0,16},{16,0},{1,17},{17,1},{2,18},{18,2},{3,19},{19,3},{4,20},{20... | collective-permute-start | bytes 2359304 | tf_op jit(solution)/shard_map/ppermute | solution.py:215
  124.6 0.9 copy-start.4
  137.5 18.8 %all-to-all-start.2 = ((bf16[16,32,384]{2,1,0:T(8,128)(2,1)}), bf16[16,32,384]{2,1,0:T(8,128)(2,1)S(1)}, u32[]{:S(2)}, u32[]{:S(2)}) async-start(bf16[16,32,384]{2,1,0:T(8,128)(2,1)} %bitcast.56), calls=%async_computation.2 | async-start | bytes 786432 | tf_op jit(solution)/shard_map/all_to_all | solution.py:234
  156.2 0.7 copy-start.3
  164.8 12.8 %all-to-all-start.3 = ((bf16[8,32,1536]{2,1,0:T(8,128)(2,1)}), bf16[8,32,1536]{2,1,0:T(8,128)(2,1)S(1)}, u32[]{:S(2)}, u32[]{:S(2)}) async-start(bf16[8,32,1536]{2,1,0:T(8,128)(2,1)} %bitcast.60), calls=%async_computation.3 | async-start | bytes 1572864 | tf_op jit(solution)/shard_map/all_to_all | solution.py:260
  170.4 26.7 %collective-permute-start.3 = (bf16[4,32,1536]{2,1,0:T(8,128)(2,1)S(1)}, bf16[4,32,1536]{2,1,0:T(8,128)(2,1)S(1)}, u32[]{:S(2)}, u32[]{:S(2)}) collective-permute-start(bf16[4,32,1536]{2,1,0:T(8,128)(2,1)S(1)} %get-tuple-element.11), channel_id=1, source_target_pairs={{0,16},{16,0},{1,17},{17,1},{2,18},{18,2},{3,19},{19,3},{4,20},{20... | collective-permute-start | bytes 1179656 | tf_op jit(solution)/shard_map/ppermute | solution.py:257
  177.6 0.9 copy-start.2
  188.9 16.8 %all-to-all-start.4 = ((bf16[16,16,768]{2,1,0:T(8,128)(2,1)}), bf16[16,16,768]{2,1,0:T(8,128)(2,1)S(1)}, u32[]{:S(2)}, u32[]{:S(2)}) async-start(bf16[16,16,768]{2,1,0:T(8,128)(2,1)} %bitcast.55), calls=%async_computation.4 | async-start | bytes 786432 | tf_op jit(solution)/shard_map/all_to_all | solution.py:274
Sparse Core Ops, SparseCore 0:
  46.8 40.3 all-gather.5
  89.0 53.0 all-gather.3

commit v2 on v1

v2 whole, which is shorter than its diff:
```python
import functools
import math

import jax
import jax.numpy as jnp
from jax import lax
from jax.experimental import pallas as pl
from jax.experimental.pallas import tpu as pltpu
from jax.sharding import Mesh
from jax.sharding import PartitionSpec as P

HEADS = 8
HSIZE = 96
WIDTH = 1536
INNER = 768
HALF = INNER // 2
EPSILON = 1e-05
SCALE = math.log2(math.e) / math.sqrt(HSIZE)
TM = ("x_lo", "y", "core")
DP = ("z", "x_hi")
BF16 = jnp.bfloat16
F32 = jnp.float32


def params():
    return pltpu.CompilerParams(vmem_limit_bytes=56 * 1024 * 1024)


def dot(a, b):
    return jnp.dot(a, b, preferred_element_type=F32)


def dot_nt(a, b):
    return lax.dot_general(a, b, (((1,), (1,)), ((), ())), preferred_element_type=F32)


def shuffle(size, rows):
    column = lax.broadcasted_iota(jnp.int32, (1, size), 1)
    per = 16 * rows
    source = (column % per) // rows * per + column // per * rows + column % rows
    return (lax.broadcasted_iota(jnp.int32, (size, size), 0) == source).astype(BF16)


def norm_kernel(xh_ref, own_ref, other_ref, gain_ref, shuffle_ref, out_ref):
    swapped = xh_ref[0] == 1
    for slot in range(2):
        here, there = (own_ref, other_ref) if slot == 0 else (other_ref, own_ref)
        x = jnp.where(swapped, there[...], here[...]).astype(F32)
        factor = lax.rsqrt(jnp.mean(x * x, axis=-1, keepdims=True) + EPSILON)
        normed = (x * factor * gain_ref[...]).astype(BF16)
        out_ref[:, slot] = dot(normed, shuffle_ref[...]).astype(BF16).reshape(8, 32, WIDTH)


def project_kernel(x_ref, w_ref, q_ref, kv_ref):
    step = pl.program_id(0)
    projected = dot(x_ref[...], w_ref[...].reshape(WIDTH, HALF)).astype(BF16)

    @pl.when(step == 0)
    def _():
        q_ref[...] = projected

    @pl.when(step > 0)
    def _():
        kv_ref[0] = projected


def attend(queries, keys, values, mask=None):
    outs = []
    for h, (first, last) in enumerate(((0, 128), (0, 256), (128, 384), (256, 384))):
        lane = lax.broadcasted_iota(jnp.int32, (1, last - first), 1) + first
        head = (lane >= h * HSIZE) & (lane < (h + 1) * HSIZE)
        q = jnp.where(head, queries[:, first:last], jnp.zeros((), BF16))
        scores = [dot_nt(q, k[:, first:last]) for k in keys]
        if mask is not None:
            scores = [jnp.where(mask, s, -jnp.inf) for s in scores]
        peak = functools.reduce(
            jnp.maximum, [jnp.max(s, axis=-1, keepdims=True) for s in scores]
        )
        terms = [jnp.exp2((s - peak) * SCALE) for s in scores]
        summed = sum(jnp.sum(t, axis=-1, keepdims=True) for t in terms)
        acc = sum(dot(t.astype(BF16), v[:, first:last]) for t, v in zip(terms, values))
        outs.append(acc * (1.0 / summed))
    lane = lax.broadcasted_iota(jnp.int32, (1, 128), 1)
    return (
        jnp.where(lane < 96, outs[0], outs[1][:, :128]),
        jnp.where(lane < 64, outs[1][:, 128:], outs[2][:, :128]),
        jnp.where(lane < 32, outs[2][:, 128:], outs[3]),
    )


def spatial_kernel(q_ref, kv_ref, kvo_ref, out_ref):
    blocks = attend(q_ref[...], (kv_ref[0], kvo_ref[0]), (kv_ref[1], kvo_ref[1]))
    for i, block in enumerate(blocks):
        out_ref[:, i * 128 : (i + 1) * 128] = block.astype(BF16)


def output_kernel(ctx_ref, tok_ref, w_ref, gain_ref, sh3_ref, sh6_ref, branch_ref, out_ref):
    rows = tok_ref.shape[0]
    ctx = jnp.concatenate(
        [ctx_ref[:, 0].reshape(rows, HALF), ctx_ref[:, 1].reshape(rows, HALF)], axis=1
    )
    ctx = dot(ctx, sh3_ref[...]).astype(BF16)
    mixed = []
    total = jnp.zeros((rows, 1), F32)
    for cb in range(4):
        lanes = slice(cb * HALF, (cb + 1) * HALF)
        w = w_ref[:, cb * 48 : (cb + 1) * 48, :].reshape(INNER, HALF)
        branch = dot(ctx, w).astype(BF16)
        branch_ref[:, lanes] = branch
        mix = tok_ref[:, lanes].astype(F32) + branch.astype(F32)
        mixed.append(mix)
        total += jnp.sum(mix * mix, axis=-1, keepdims=True)
    factor = lax.rsqrt(total * (1.0 / WIDTH) + EPSILON)
    target = lax.broadcasted_iota(jnp.int32, (rows, rows), 0)
    source = (target % 32) // 4 * 32 + target // 32 * 4 + target % 4
    swap = (lax.broadcasted_iota(jnp.int32, (rows, rows), 1) == source).astype(BF16)
    normed = jnp.concatenate(
        [
            (mix * factor * gain_ref[:, cb * HALF : (cb + 1) * HALF]).astype(BF16)
            for cb, mix in enumerate(mixed)
        ],
        axis=1,
    )
    normed = dot(swap, normed).astype(BF16)
    out_ref[...] = dot(normed, sh6_ref[...]).astype(BF16)


def temporal_kernel(x_ref, w_ref, out_ref):
    rows = x_ref.shape[0]
    query, key, value = (
        dot(x_ref[...], w_ref[:, 96 * i : 96 * (i + 1), :].reshape(WIDTH, HALF)).astype(BF16)
        for i in range(3)
    )
    r = lax.broadcasted_iota(jnp.int32, (rows, rows), 0)
    s = lax.broadcasted_iota(jnp.int32, (rows, rows), 1)
    same = (r % 4 == s % 4) & ((r // 8) % 2 == (s // 8) % 2)
    seen = (r // 16) * 2 + (r // 4) % 2 >= (s // 16) * 2 + (s // 4) % 2
    for i, block in enumerate(attend(query, (key,), (value,), same & seen)):
        out_ref[:, i * 128 : (i + 1) * 128] = block.astype(BF16)


def whole(shape):
    return pl.BlockSpec(shape, lambda *_: (0,) * len(shape))


def pick(first, a, b, axis):
    return jnp.where(first, jnp.concatenate([a, b], axis), jnp.concatenate([b, a], axis))


def per_device(tokens, space_gain, spatial_project, spatial_output, time_gain, temporal_project):
    core = lax.axis_index("core")
    x_hi = lax.axis_index("x_hi")
    tm = lax.axis_index(TM)
    swap = [(0, 1), (1, 0)]
    sh6 = shuffle(WIDTH, 6)
    sh3 = shuffle(INNER, 3)

    wq = lax.dynamic_slice_in_dim(spatial_project, tm * 6, 6, 0)
    wq = wq.reshape(6, 3, 2, HALF).transpose(2, 1, 0, 3).reshape(2, 18, HALF)
    wo = lax.dynamic_slice_in_dim(spatial_output, tm * 3, 3, 0)
    wo = wo.reshape(3, 4, HALF).transpose(1, 0, 2).reshape(12, HALF)
    wt = lax.dynamic_slice_in_dim(temporal_project, tm * 6, 6, 0)
    wt = wt.reshape(6, 3, 2, HALF).transpose(2, 1, 0, 3).reshape(36, HALF)
    chunk = jnp.stack([jnp.concatenate([wo, wq[i], wt], 0) for i in range(2)])
    chunk = jnp.broadcast_to(chunk[None], (8, 2, 66, HALF)).reshape(16, 66, HALF)
    got = lax.all_to_all(chunk, DP, 0, 0, tiled=True)
    across = lax.ppermute(tokens, "x_hi", swap)

    def both_cores(block):
        halves = block.reshape(4, 2, 32, WIDTH)
        keep = lax.dynamic_index_in_dim(halves, core, 1, keepdims=False)
        send = lax.dynamic_index_in_dim(halves, 1 - core, 1, keepdims=False)
        moved = lax.ppermute(send, "core", swap)
        return pick(core == 0, keep, moved, 0).reshape(256, WIDTH)

    frames = both_cores(tokens)
    normed = pl.pallas_call(
        norm_kernel,
        grid_spec=pltpu.PrefetchScalarGridSpec(
            num_scalar_prefetch=1,
            grid=(1,),
            in_specs=[
                whole((256, WIDTH)),
                whole((256, WIDTH)),
                whole((1, WIDTH)),
                whole((WIDTH, WIDTH)),
            ],
            out_specs=whole((8, 2, 32, WIDTH)),
        ),
        out_shape=jax.ShapeDtypeStruct((8, 2, 32, WIDTH), BF16),
        compiler_params=params(),
        name="space_norm",
    )(
        x_hi.reshape(1).astype(jnp.int32),
        frames,
        both_cores(across),
        space_gain.reshape(1, WIDTH),
        sh6,
    )
    got, _ = lax.optimization_barrier((got, normed))
    w1 = jnp.concatenate(
        [
            got[:, :12].reshape(16, 4, 3, HALF).transpose(1, 0, 2, 3).reshape(192, HALF),
            got[:, 12:30].reshape(16, 3, 6, HALF).transpose(1, 0, 2, 3).reshape(288, HALF),
        ],
        0,
    )
    w2 = got[:, 30:].reshape(16, 6, 6, HALF).transpose(1, 0, 2, 3).reshape(576, HALF)
    w1 = lax.all_gather(w1, TM, axis=0, tiled=False)
    frame = lax.all_to_all(normed.reshape(8, 64, WIDTH), "z", 0, 0, tiled=True)
    w2, frame = lax.optimization_barrier((w2, frame))
    w2 = lax.all_gather(w2, TM, axis=0, tiled=False)
    q, kv = pl.pallas_call(
        project_kernel,
        grid=(3,),
        in_specs=[
            whole((512, WIDTH)),
            pl.BlockSpec((16, 96, HALF), lambda i: (0, i + 2, 0)),
        ],
        out_specs=[
            whole((512, HALF)),
            pl.BlockSpec((1, 512, HALF), lambda i: (jnp.maximum(i - 1, 0), 0, 0)),
        ],
        out_shape=[
            jax.ShapeDtypeStruct((512, HALF), BF16),
            jax.ShapeDtypeStruct((2, 512, HALF), BF16),
        ],
        compiler_params=params(),
        name="space_project",
    )(frame.reshape(512, WIDTH), w1)
    kvo = lax.ppermute(kv, "core", swap)
    ctx = pl.pallas_call(
        spatial_kernel,
        grid=(2,),
        in_specs=[
            pl.BlockSpec((256, HALF), lambda i: (i, 0)),
            whole((2, 512, HALF)),
            whole((2, 512, HALF)),
        ],
        out_specs=pl.BlockSpec((256, HALF), lambda i: (i, 0)),
        out_shape=jax.ShapeDtypeStruct((512, HALF), BF16),
        compiler_params=params(),
        name="space_attend",
    )(q, kv, kvo)
    ctx = lax.all_to_all(ctx.reshape(16, 32, HALF), DP, 0, 0, tiled=True)
    branch, normed_time = pl.pallas_call(
        output_kernel,
        grid=(1,),
        in_specs=[
            whole((8, 2, 32, HALF)),
            whole((256, WIDTH)),
            whole((16, 192, HALF)),
            whole((1, WIDTH)),
            whole((INNER, INNER)),
            whole((WIDTH, WIDTH)),
        ],
        out_specs=[whole((256, WIDTH)), whole((256, WIDTH))],
        out_shape=[
            jax.ShapeDtypeStruct((256, WIDTH), BF16),
            jax.ShapeDtypeStruct((256, WIDTH), BF16),
        ],
        compiler_params=params(),
        name="space_output",
    )(ctx.reshape(8, 2, 32, HALF), frames, w1, time_gain.reshape(1, WIDTH), sh3, sh6)
    branch = branch.reshape(8, 32, WIDTH)
    mine = lax.dynamic_slice_in_dim(branch, core * 4, 4, 0)
    theirs = lax.dynamic_slice_in_dim(branch, (1 - core) * 4, 4, 0)
    back = lax.ppermute(theirs, "core", swap)
    branch = pick(core == 0, mine[:, None], back[:, None], 1).reshape(tokens.shape)

    columns = lax.all_to_all(normed_time.reshape(8, 32, WIDTH), TM[:2], 0, 0, tiled=True)
    context = pl.pallas_call(
        temporal_kernel,
        grid=(2,),
        in_specs=[
            whole((256, WIDTH)),
            pl.BlockSpec((16, 288, HALF), lambda i: (0, i, 0)),
        ],
        out_specs=pl.BlockSpec((256, HALF), lambda i: (0, i)),
        out_shape=jax.ShapeDtypeStruct((256, INNER), BF16),
        compiler_params=params(),
        name="time_attend",
    )(columns.reshape(256, WIDTH), w2)
    context = lax.all_to_all(context.reshape(16, 16, INNER), TM, 0, 0, tiled=True)
    context = context.reshape(8, 2, 2, 2, 4, INNER).transpose(2, 3, 1, 0, 4, 5)
    return branch, context.reshape(2, 2, 64, INNER)


def solution(mesh):
    fine = Mesh(mesh.devices.reshape(2, 4, 2, 8, 2), TM + DP)
    in_specs = (P(None, TM, DP, None), P(), P(DP, None), P(DP, None), P(), P(DP, None))
    out_specs = (P(None, TM, DP, None), P(None, TM, DP, None))
    return jax.shard_map(
        per_device, mesh=fine, in_specs=in_specs, out_specs=out_specs, check_vma=False
    )
```

time: 214 us -> 188 us (0.88)
  blocking collectives: 63.7 us -> 0 us
  starting transfers between devices: 25 us -> 46.6 us
  waiting for transfers between devices: 50.7 us -> 71.6 us
  Pallas kernels: 41.3 us -> 33.3 us
    all_to_all x2 -> x0, blocking collectives: 63.7 us -> none  [the longest x1 36.7 us: per_device(): got = lax.all_to_all(chunk, DP, 0, 0, tiled=True)]
    all_to_all x0 -> x2, waiting for transfers between devices: none -> 39.7 us  [the longest x1 39.3 us: per_device(): frame = lax.all_to_all(normed.reshape(8, 64, WIDTH), 'z', 0, 0, tiled=True)]
    ppermute x2 -> x3, waiting for transfers between devices: 23.7 us -> 4.39 us  [the longest x1 4.38 us: per_device(): across = lax.ppermute(tokens, 'x_hi', swap)]
    all_to_all x0 -> x2, starting transfers between devices: none -> 17.5 us  [the longest x1 9.23 us: per_device(): frame = lax.all_to_all(normed.reshape(8, 64, WIDTH), 'z', 0, 0, tiled=True)]
    pallas_call x4, Pallas kernels: 33.6 us -> 25.3 us  [the longest x1 6.91 us: per_device(): pl.pallas_call(norm_kernel, grid_spec=pltpu.PrefetchScalarGridSpec(num_sc...]
    ppermute x2 -> x3, starting transfers between devices: 2.77 us -> 7.81 us  [the longest x2 4.15 us: both_cores(): moved = lax.ppermute(send, 'core', swap)]
    all_to_all x1, starting transfers between devices: 3.73 us -> 6.79 us  [per_device(): ctx = lax.all_to_all(ctx.reshape(16, 32, HALF), DP, 0, 0, tiled=True)]
    ppermute x1, starting transfers between devices: 3 us -> 0.47 us  [per_device(): kvo = lax.ppermute(kv, 'core', swap)]
  transfers between devices with their start and end apart: 9 -> 12, of which waited for: 5 -> 7; matrix products, arithmetic and copies ran while one was open for 5% -> 8% of each run, Pallas kernels for 19% -> 18%
where the time goes in v2:
time: 188 us; the launch traced here: 187 us
  waiting for transfers between devices  71.6 us (38%)
  starting transfers between devices  46.6 us (25%)
  Pallas kernels  33.3 us (18%)
  between operations  14.3 us (8%)
  local copies, waits for them, and re-layouts  12.6 us (7%)
  other arithmetic  8.66 us (5%)
    all_to_all x1, waiting for transfers between devices, per_device(): frame = lax.all_to_all(normed.reshape(8, 64, WIDTH), 'z', 0, 0, tiled=True)  39.3 us
    all_to_all x1, waiting for transfers between devices, per_device(): ctx = lax.all_to_all(ctx.reshape(16, 32, HALF), DP, 0, 0, tiled=True)  13 us
    all_to_all x1, starting transfers between devices, per_device(): frame = lax.all_to_all(normed.reshape(8, 64, WIDTH), 'z', 0, 0, tiled=True)  9.23 us
    all_to_all x1, starting transfers between devices, per_device(): got = lax.all_to_all(chunk, DP, 0, 0, tiled=True)  8.29 us
    all_to_all x1, starting transfers between devices, per_device(): lax.all_to_all(context.reshape(16, 16, INNER), TM, 0, 0, tiled=True)  8.02 us
    pallas_call x1, Pallas kernels, per_device(): pl.pallas_call(output_kernel, grid=(1,), in_specs=[whole((8, 2, 32, HALF)...  7.99 us
    all_to_all x1, waiting for transfers between devices, per_device(): lax.all_to_all(context.reshape(16, 16, INNER), TM, 0, 0, tiled=True)  7.37 us
    pallas_call x1, Pallas kernels, per_device(): pl.pallas_call(norm_kernel, grid_spec=pltpu.PrefetchScalarGridSpec(num_sc...  6.91 us
  transfers between devices with their start and end apart: 12, of which 7 were waited for; matrix products, arithmetic and copies ran while one was open for 8% of the time, Pallas kernels for 18%

profile of v2, /device:TPU:1, one launch (start us, length us, event | category | flops | bytes accessed | tf_op | source)
XLA Modules:
  0.0 187.1 jit_solution(4996988203988116651)
XLA Ops:
  7.2 3.7 %collective-permute-start.1 = (bf16[2,2,64,1536]{3,2,1,0:T(8,128)(2,1)}, bf16[2,2,64,1536]{3,2,1,0:T(8,128)(2,1)S(1)}, u32[]{:S(2)}, u32[]{:S(2)}) collective-permute-start(bf16[2,2,64,1536]{3,2,1,0:T(8,128)(2,1)} %param.6), channel_id=1, source_target_pairs={{0,1},{1,0},{2,3},{3,2},{4,5},{5,4},{6,7},{7,6},{8,9},{9,8},{10,11... | collective-permute-start | bytes 2359304 | tf_op jit(solution)/shard_map/ppermute | solution.py:167
  10.8 0.9 constant_dynamic-slice_fusion.1
  12.2 1.0 broadcast_in_dim.12
  13.2 8.3 %all-to-all-start = ((bf16[16,66,384]{2,1,0:T(8,128)(2,1)}), bf16[16,66,384]{2,1,0:T(8,128)(2,1)S(1)}, u32[]{:S(2)}, u32[]{:S(2)}) async-start(bf16[16,66,384]{2,1,0:T(8,128)(2,1)} %bitcast.6), calls=%async_computation | async-start | bytes 1769472 | tf_op jit(solution)/shard_map/all_to_all | solution.py:166
  21.6 1.3 collective-permute-start
  22.9 4.4 %collective-permute-done.1 = bf16[2,2,64,1536]{3,2,1,0:T(8,128)(2,1)S(1)} collective-permute-done((bf16[2,2,64,1536]{3,2,1,0:T(8,128)(2,1)}, bf16[2,2,64,1536]{3,2,1,0:T(8,128)(2,1)S(1)}, u32[]{:S(2)}, u32[]{:S(2)}) %collective-permute-start.1) | collective-permute-done | bytes 786464 | tf_op jit(solution)/shard_map/ppermute | solution.py:167
  28.1 2.8 %collective-permute-start.2 = (bf16[4,32,1536]{2,1,0:T(8,128)(2,1)}, bf16[4,32,1536]{2,1,0:T(8,128)(2,1)S(1)}, u32[]{:S(2)}, u32[]{:S(2)}) collective-permute-start(bf16[4,32,1536]{2,1,0:T(8,128)(2,1)} %get-tuple-element.19), channel_id=1, source_target_pairs={{0,16},{16,0},{1,17},{17,1},{2,18},{18,2},{3,19},{19,3},{4,20},{20... | collective-permute-start | bytes 1179656 | tf_op jit(solution)/shard_map/ppermute | solution.py:173
  31.0 4.2 %fusion.shuffle_ref.sh6_ref = bf16[1536,1536]{1,0:T(8,128)(2,1)} fusion(s32[1536]{0:T(1024)S(1)} %fusion.24), kind=kLoop, calls=%fused_computation.1 | loop fusion | flops 4718592 | bytes 4724736 | tf_op jit(solution)/shard_map/convert_element_type | solution.py:41
  35.8 1.0 maximum_select_fusion
  36.8 1.0 maximum_select_fusion.1
  37.8 6.9 %space_norm.1 = bf16[8,2,32,1536]{3,2,1,0:T(8,128)(2,1)} custom-call(s32[1]{0:T(128)} %bitcast.7.xh_ref, bf16[256,1536]{1,0:T(8,128)(2,1)} %bitcast.51, bf16[256,1536]{1,0:T(8,128)(2,1)} %bitcast.55, f32[1,1536]{1,0:T(1,128)} %reshape.259.gain_ref, bf16[1536,1536]{1,0:T(8,128)(2,1)} %fusion.shuffle_ref.sh6_ref), custom_call_target="tpu_custom_call" | custom-call | tf_op jit(solution)/shard_map/space_norm/pallas_call | solution.py:177
  46.4 9.2 %all-to-all-start.1 = ((bf16[8,64,1536]{2,1,0:T(8,128)(2,1)}), bf16[8,64,1536]{2,1,0:T(8,128)(2,1)S(1)}, u32[]{:S(2)}, u32[]{:S(2)}) async-start(bf16[8,64,1536]{2,1,0:T(8,128)(2,1)} %bitcast.18), calls=%async_computation.1 | async-start | bytes 3145728 | tf_op jit(solution)/shard_map/all_to_all | solution.py:210
  55.9 0.9 reshape.261
  56.8 39.3 %all-to-all-done.1 = bf16[8,64,1536]{2,1,0:T(8,128)(2,1)S(1)} async-done(((bf16[8,64,1536]{2,1,0:T(8,128)(2,1)}), bf16[8,64,1536]{2,1,0:T(8,128)(2,1)S(1)}, u32[]{:S(2)}, u32[]{:S(2)}) %all-to-all-start.1) | async-done | bytes 1572896 | tf_op jit(solution)/shard_map/all_to_all | solution.py:210
  96.2 1.1 copy-done.1
  97.3 6.0 %space_project.1 = (bf16[512,384]{1,0:T(8,128)(2,1)}, bf16[2,512,384]{2,1,0:T(8,128)(2,1)}) custom-call(bf16[512,1536]{1,0:T(8,128)(2,1)} %bitcast.54, bf16[16,480,384]{2,1,0:T(8,128)(2,1)} %bitcast.49), custom_call_target="tpu_custom_call" | custom-call | tf_op jit(solution)/shard_map/space_project/pallas_call | solution.py:213
  103.7 2.1 %collective-permute-done.3.kvo_ref = bf16[2,512,384]{2,1,0:T(8,128)(2,1)S(1)} collective-permute-done((bf16[2,512,384]{2,1,0:T(8,128)(2,1)}, bf16[2,512,384]{2,1,0:T(8,128)(2,1)S(1)}, u32[]{:S(2)}, u32[]{:S(2)}) %collective-permute-start.3) | collective-permute-done | bytes 786464 | tf_op jit(solution)/shard_map/ppermute | solution.py:231
  105.9 0.9 copy-done.5
  106.8 5.7 %space_attend.1 = bf16[512,384]{1,0:T(8,128)(2,1)} custom-call(bf16[512,384]{1,0:T(8,128)(2,1)} %get-tuple-element.11.q_ref, bf16[2,512,384]{2,1,0:T(8,128)(2,1)} %get-tuple-element.12.kv_ref, bf16[2,512,384]{2,1,0:T(8,128)(2,1)} %copy-done.5), custom_call_target="tpu_custom_call" | custom-call | tf_op jit(solution)/shard_map/space_attend/pallas_call | solution.py:232
  112.5 6.8 %all-to-all-start.2 = ((bf16[16,32,384]{2,1,0:T(8,128)(2,1)}), bf16[16,32,384]{2,1,0:T(8,128)(2,1)S(1)}, u32[]{:S(2)}, u32[]{:S(2)}) async-start(bf16[16,32,384]{2,1,0:T(8,128)(2,1)} %bitcast.60), calls=%async_computation.2 | async-start | bytes 786432 | tf_op jit(solution)/shard_map/all_to_all | solution.py:245
  119.9 1.4 fusion.1.sh3_ref
  121.3 13.0 %all-to-all-done.2 = bf16[16,32,384]{2,1,0:T(8,128)(2,1)S(1)} async-done(((bf16[16,32,384]{2,1,0:T(8,128)(2,1)}), bf16[16,32,384]{2,1,0:T(8,128)(2,1)S(1)}, u32[]{:S(2)}, u32[]{:S(2)}) %all-to-all-start.2) | async-done | bytes 393248 | tf_op jit(solution)/shard_map/all_to_all | solution.py:245
  135.1 8.0 %space_output.1 = (bf16[256,1536]{1,0:T(8,128)(2,1)}, bf16[256,1536]{1,0:T(8,128)(2,1)}) custom-call(bf16[8,2,32,384]{3,2,1,0:T(8,128)(2,1)} %bitcast.58, bf16[256,1536]{1,0:T(8,128)(2,1)} %bitcast.52, bf16[16,480,384]{2,1,0:T(8,128)(2,1)} %bitcast.50, f32[1,1536]{1,0:T(1,128)} %reshape.270.gain_ref, bf16[768,768]{1,0:T(8,128)(2,1)} %fusion.1.sh3_ref, ...), custom_call_target="tpu_custom_call" | custom-call | tf_op jit(solution)/shard_map/space_output/pallas_call | solution.py:246
  143.1 3.5 %all-to-all-start.3 = ((bf16[8,32,1536]{2,1,0:T(8,128)(2,1)}), bf16[8,32,1536]{2,1,0:T(8,128)(2,1)S(1)}, u32[]{:S(2)}, u32[]{:S(2)}) async-start(bf16[8,32,1536]{2,1,0:T(8,128)(2,1)} %bitcast.63), calls=%async_computation.3 | async-start | bytes 1572864 | tf_op jit(solution)/shard_map/all_to_all | solution.py:271
  146.7 1.2 dynamic-slice_bitcast_fusion
  147.8 2.4 %collective-permute-start.4 = (bf16[4,32,1536]{2,1,0:T(8,128)(2,1)S(1)}, bf16[4,32,1536]{2,1,0:T(8,128)(2,1)S(1)}, u32[]{:S(2)}, u32[]{:S(2)}) collective-permute-start(bf16[4,32,1536]{2,1,0:T(8,128)(2,1)S(1)} %get-tuple-element.17), channel_id=1, source_target_pairs={{0,16},{16,0},{1,17},{17,1},{2,18},{18,2},{3,19},{19,3},{4,20},{20... | collective-permute-start | bytes 1179656 | tf_op jit(solution)/shard_map/ppermute | solution.py:268
  150.2 4.9 %all-to-all-done.3 = bf16[8,32,1536]{2,1,0:T(8,128)(2,1)S(1)} async-done(((bf16[8,32,1536]{2,1,0:T(8,128)(2,1)}), bf16[8,32,1536]{2,1,0:T(8,128)(2,1)S(1)}, u32[]{:S(2)}, u32[]{:S(2)}) %all-to-all-start.3) | async-done | bytes 786464 | tf_op jit(solution)/shard_map/all_to_all | solution.py:271
  155.2 0.9 copy-done.2
  156.0 6.7 %time_attend.1 = bf16[256,768]{1,0:T(8,128)(2,1)} custom-call(bf16[256,1536]{1,0:T(8,128)(2,1)} %bitcast.56, bf16[16,576,384]{2,1,0:T(8,128)(2,1)} %bitcast.53), custom_call_target="tpu_custom_call" | custom-call | tf_op jit(solution)/shard_map/time_attend/pallas_call | solution.py:272
  162.7 8.0 %all-to-all-start.4 = ((bf16[16,16,768]{2,1,0:T(8,128)(2,1)}), bf16[16,16,768]{2,1,0:T(8,128)(2,1)S(1)}, u32[]{:S(2)}, u32[]{:S(2)}) async-start(bf16[16,16,768]{2,1,0:T(8,128)(2,1)} %bitcast.59), calls=%async_computation.4 | async-start | bytes 786432 | tf_op jit(solution)/shard_map/all_to_all | solution.py:284
  170.9 1.0 copy.34
  171.8 7.4 %all-to-all-done.4 = bf16[16,16,768]{2,1,0:T(8,128)(2,1)S(1)} async-done(((bf16[16,16,768]{2,1,0:T(8,128)(2,1)}), bf16[16,16,768]{2,1,0:T(8,128)(2,1)S(1)}, u32[]{:S(2)}, u32[]{:S(2)}) %all-to-all-start.4) | async-done | bytes 393248 | tf_op jit(solution)/shard_map/all_to_all | solution.py:284
  (57 shorter events, 6.8 us)
Async XLA Ops:
  7.2 4.7 %copy-start = (bf16[48,1536]{1,0:T(8,128)(2,1)S(1)}, bf16[48,1536]{1,0:T(8,128)(2,1)}, u32[]{:S(2)}) copy-start(bf16[48,1536]{1,0:T(8,128)(2,1)} %param.9) | copy-start | bytes 442372
  7.2 14.3 %copy-start.4 = (bf16[2,2,64,1536]{3,2,1,0:T(8,128)(2,1)S(1)}, bf16[2,2,64,1536]{3,2,1,0:T(8,128)(2,1)}, u32[]{:S(2)}) copy-start(bf16[2,2,64,1536]{3,2,1,0:T(8,128)(2,1)} %param.6) | copy-start | bytes 2359300
  7.2 20.1 %collective-permute-start.1 = (bf16[2,2,64,1536]{3,2,1,0:T(8,128)(2,1)}, bf16[2,2,64,1536]{3,2,1,0:T(8,128)(2,1)S(1)}, u32[]{:S(2)}, u32[]{:S(2)}) collective-permute-start(bf16[2,2,64,1536]{3,2,1,0:T(8,128)(2,1)} %param.6), channel_id=1, source_target_pairs={{0,1},{1,0},{2,3},{3,2},{4,5},{5,4},{6,7},{7,6},{8,9},{9,8},{10,11... | collective-permute-start | bytes 2359304 | tf_op jit(solution)/shard_map/ppermute | solution.py:167
  13.2 31.9 %all-to-all-start = ((bf16[16,66,384]{2,1,0:T(8,128)(2,1)}), bf16[16,66,384]{2,1,0:T(8,128)(2,1)S(1)}, u32[]{:S(2)}, u32[]{:S(2)}) async-start(bf16[16,66,384]{2,1,0:T(8,128)(2,1)} %bitcast.6), calls=%async_computation | async-start | bytes 1769472 | tf_op jit(solution)/shard_map/all_to_all | solution.py:166
  21.5 74.7 %all-gather.5.cloned.1.call-start = ((), (), s32[]{:S(2)}) async-start(), calls=%async_computation.5 | async-start | bytes 6266880 | tf_op jit(solution)/shard_map/all_gather | solution.py:209
  21.6 14.2 %collective-permute-start = (bf16[4,32,1536]{2,1,0:T(8,128)(2,1)S(1)}, bf16[4,32,1536]{2,1,0:T(8,128)(2,1)S(1)}, u32[]{:S(2)}, u32[]{:S(2)}) collective-permute-start(bf16[4,32,1536]{2,1,0:T(8,128)(2,1)S(1)} %get-tuple-element.21), channel_id=1, source_target_pairs={{0,16},{16,0},{1,17},{17,1},{2,18},{18,2},{3,19},{19,3},{4,20},{20... | collective-permute-start | bytes 1179656 | tf_op jit(solution)/shard_map/ppermute | solution.py:173
  28.1 7.1 %copy-start.6 = (f32[1536]{0:T(1024)S(1)}, f32[1536]{0:T(1024)}, u32[]{:S(2)}) copy-start(f32[1536]{0:T(1024)} %param.7) | copy-start | bytes 18436
  28.1 8.7 %collective-permute-start.2 = (bf16[4,32,1536]{2,1,0:T(8,128)(2,1)}, bf16[4,32,1536]{2,1,0:T(8,128)(2,1)S(1)}, u32[]{:S(2)}, u32[]{:S(2)}) collective-permute-start(bf16[4,32,1536]{2,1,0:T(8,128)(2,1)} %get-tuple-element.19), channel_id=1, source_target_pairs={{0,16},{16,0},{1,17},{17,1},{2,18},{18,2},{3,19},{19,3},{4,20},{20... | collective-permute-start | bytes 1179656 | tf_op jit(solution)/shard_map/ppermute | solution.py:173
  46.4 49.7 %all-to-all-start.1 = ((bf16[8,64,1536]{2,1,0:T(8,128)(2,1)}), bf16[8,64,1536]{2,1,0:T(8,128)(2,1)S(1)}, u32[]{:S(2)}, u32[]{:S(2)}) async-start(bf16[8,64,1536]{2,1,0:T(8,128)(2,1)} %bitcast.18), calls=%async_computation.1 | async-start | bytes 3145728 | tf_op jit(solution)/shard_map/all_to_all | solution.py:210
  55.7 99.5 %all-gather.7.cloned.1.call-start = ((), (), s32[]{:S(2)}) async-start(), calls=%async_computation.6 | async-start | bytes 7520256 | tf_op jit(solution)/shard_map/all_gather | solution.py:212
  96.1 1.1 copy-start.1
  103.3 16.0 %copy-start.7 = (f32[1536]{0:T(1024)S(1)}, f32[1536]{0:T(1024)}, u32[]{:S(2)}) copy-start(f32[1536]{0:T(1024)} %param.10) | copy-start | bytes 18436
  103.3 2.6 %collective-permute-start.3 = (bf16[2,512,384]{2,1,0:T(8,128)(2,1)}, bf16[2,512,384]{2,1,0:T(8,128)(2,1)S(1)}, u32[]{:S(2)}, u32[]{:S(2)}) collective-permute-start(bf16[2,512,384]{2,1,0:T(8,128)(2,1)} %get-tuple-element.12.kv_ref), channel_id=1, source_target_pairs={{0,16},{16,0},{1,17},{17,1},{2,18},{18,2},{3,19},{19,3},{4,20},{20... | collective-permute-start | bytes 2359304 | tf_op jit(solution)/shard_map/ppermute | solution.py:231
  105.9 0.9 copy-start.5
  112.5 21.9 %all-to-all-start.2 = ((bf16[16,32,384]{2,1,0:T(8,128)(2,1)}), bf16[16,32,384]{2,1,0:T(8,128)(2,1)S(1)}, u32[]{:S(2)}, u32[]{:S(2)}) async-start(bf16[16,32,384]{2,1,0:T(8,128)(2,1)} %bitcast.60), calls=%async_computation.2 | async-start | bytes 786432 | tf_op jit(solution)/shard_map/all_to_all | solution.py:245
  134.4 0.7 copy-start.3
  143.1 12.1 %all-to-all-start.3 = ((bf16[8,32,1536]{2,1,0:T(8,128)(2,1)}), bf16[8,32,1536]{2,1,0:T(8,128)(2,1)S(1)}, u32[]{:S(2)}, u32[]{:S(2)}) async-start(bf16[8,32,1536]{2,1,0:T(8,128)(2,1)} %bitcast.63), calls=%async_computation.3 | async-start | bytes 1572864 | tf_op jit(solution)/shard_map/all_to_all | solution.py:271
  147.8 22.9 %collective-permute-start.4 = (bf16[4,32,1536]{2,1,0:T(8,128)(2,1)S(1)}, bf16[4,32,1536]{2,1,0:T(8,128)(2,1)S(1)}, u32[]{:S(2)}, u32[]{:S(2)}) collective-permute-start(bf16[4,32,1536]{2,1,0:T(8,128)(2,1)S(1)} %get-tuple-element.17), channel_id=1, source_target_pairs={{0,16},{16,0},{1,17},{17,1},{2,18},{18,2},{3,19},{19,3},{4,20},{20... | collective-permute-start | bytes 1179656 | tf_op jit(solution)/shard_map/ppermute | solution.py:268
  155.2 0.9 copy-start.2
  162.7 16.5 %all-to-all-start.4 = ((bf16[16,16,768]{2,1,0:T(8,128)(2,1)}), bf16[16,16,768]{2,1,0:T(8,128)(2,1)S(1)}, u32[]{:S(2)}, u32[]{:S(2)}) async-start(bf16[16,16,768]{2,1,0:T(8,128)(2,1)} %bitcast.59), calls=%async_computation.4 | async-start | bytes 786432 | tf_op jit(solution)/shard_map/all_to_all | solution.py:284
Sparse Core Ops, SparseCore 0:
  46.6 48.5 all-gather.4
  97.0 52.9 all-gather.6

commit v3 on v2

v3 whole, which is shorter than its diff:
```python
import functools
import math

import jax
import jax.numpy as jnp
import numpy as np
from jax import lax
from jax.experimental import pallas as pl
from jax.experimental.pallas import tpu as pltpu
from jax.sharding import Mesh
from jax.sharding import PartitionSpec as P

HEADS = 8
HSIZE = 96
WIDTH = 1536
INNER = 768
HALF = INNER // 2
EPSILON = 1e-05
SCALE = math.log2(math.e) / math.sqrt(HSIZE)
TM = ("x_lo", "y", "core")
DP = ("z", "x_hi")
BF16 = jnp.bfloat16
F32 = jnp.float32


def dot(a, b):
    return jnp.dot(a, b, preferred_element_type=F32)


def dot_nt(a, b):
    return lax.dot_general(a, b, (((1,), (1,)), ((), ())), preferred_element_type=F32)


def one_hot(shape, order):
    size = math.prod(shape)
    source = np.arange(size).reshape(shape).transpose(order).reshape(-1)
    return (np.arange(size)[:, None] == source[None]).astype(jnp.bfloat16)


def fetch(pairs, sems):
    copies = [pltpu.make_async_copy(a, b, sems.at[i]) for i, (a, b) in enumerate(pairs)]
    for copy in copies:
        copy.start()
    return copies


def gather_frames(core, block_ref, moved_ref, frames_vmem):
    frames_vmem[pl.ds(core * 4, 4)] = block_ref[:, pl.ds(core, 1)].reshape(4, 32, WIDTH)
    frames_vmem[pl.ds((1 - core) * 4, 4)] = moved_ref[...]


def normalize(frames_vmem, gain_ref):
    x = frames_vmem[...].reshape(256, WIDTH).astype(F32)
    factor = lax.rsqrt(jnp.mean(x * x, axis=-1, keepdims=True) + EPSILON)
    return (x * factor * gain_ref[...]).astype(BF16)


def own_kernel(
    core_ref, block_ref, moved_ref, gain_ref, order_ref,
    frames_ref, out_ref, frames_vmem, out_vmem, order_vmem, sems,
):
    copies = fetch([(order_ref, order_vmem)], sems)
    gather_frames(core_ref[0], block_ref, moved_ref, frames_vmem)
    copies += fetch([(frames_vmem, frames_ref)], sems.at[pl.ds(1, 1)])
    normed = normalize(frames_vmem, gain_ref)
    copies[0].wait()
    out_vmem[...] = dot(normed, order_vmem[...]).astype(BF16).reshape(8, 1, 32, WIDTH)
    copies += fetch([(out_vmem, out_ref)], sems.at[pl.ds(2, 1)])
    copies[1].wait()
    copies[2].wait()


def other_kernel(
    core_ref, xh_ref, block_ref, moved_ref, gain_ref, own_ref, order_ref,
    out_ref, frames_vmem, own_vmem, order_vmem, sems,
):
    copies = fetch([(order_ref, order_vmem), (own_ref, own_vmem)], sems)
    xh = xh_ref[0]
    gather_frames(core_ref[0], block_ref, moved_ref, frames_vmem)
    normed = normalize(frames_vmem, gain_ref)
    copies[0].wait()
    other = dot(normed, order_vmem[...]).astype(BF16)
    out_ref[:, pl.ds(1 - xh, 1)] = other.reshape(8, 1, 32, WIDTH)
    copies[1].wait()
    out_ref[:, pl.ds(xh, 1)] = own_vmem[...]


def project_kernel(x_ref, w_ref, q_ref, kv_ref, w_vmem, sems):
    copies = fetch(
        [(w_ref.at[:, pl.ds(192 + 96 * i, 96)], w_vmem.at[i]) for i in range(3)], sems
    )
    for copy, i in zip(copies, range(3)):
        copy.wait()
        projected = dot(x_ref[...], w_vmem[i].reshape(WIDTH, HALF)).astype(BF16)
        if i == 0:
            q_ref[...] = projected
        else:
            kv_ref[i - 1] = projected


def attend(queries, keys, values, mask=None):
    outs = []
    for h, (first, last) in enumerate(((0, 128), (0, 256), (128, 384), (256, 384))):
        lane = lax.broadcasted_iota(jnp.int32, (1, last - first), 1) + first
        head = (lane >= h * HSIZE) & (lane < (h + 1) * HSIZE)
        q = jnp.where(head, queries[:, first:last], jnp.zeros((), BF16))
        scores = [dot_nt(q, k[:, first:last]) for k in keys]
        if mask is not None:
            scores = [jnp.where(mask, s, -jnp.inf) for s in scores]
        peak = functools.reduce(
            jnp.maximum, [jnp.max(s, axis=-1, keepdims=True) for s in scores]
        )
        terms = [jnp.exp2((s - peak) * SCALE) for s in scores]
        summed = sum(jnp.sum(t, axis=-1, keepdims=True) for t in terms)
        acc = sum(dot(t.astype(BF16), v[:, first:last]) for t, v in zip(terms, values))
        outs.append(acc * (1.0 / summed))
    lane = lax.broadcasted_iota(jnp.int32, (1, 128), 1)
    return (
        jnp.where(lane < 96, outs[0], outs[1][:, :128]),
        jnp.where(lane < 64, outs[1][:, 128:], outs[2][:, :128]),
        jnp.where(lane < 32, outs[2][:, 128:], outs[3]),
    )


def spatial_kernel(q_ref, kv_ref, kvo_ref, out_ref):
    for first in (0, 256):
        rows = slice(first, first + 256)
        blocks = attend(q_ref[rows], (kv_ref[0], kvo_ref[0]), (kv_ref[1], kvo_ref[1]))
        for i, block in enumerate(blocks):
            out_ref[rows, i * 128 : (i + 1) * 128] = block.astype(BF16)


def weights_kernel(
    w_ref, inner_ref, time_ref,
    plain_ref, mixed_ref, w_vmem, inner_vmem, time_vmem, plain_vmem, mixed_vmem, sems,
):
    copies = fetch(
        [
            (inner_ref, inner_vmem),
            (w_ref.at[:, pl.ds(0, 192)], w_vmem),
            (time_ref, time_vmem),
        ],
        sems,
    )
    copies[0].wait()
    copies[1].wait()
    for cb in range(4):
        w = w_vmem[:, cb * 48 : (cb + 1) * 48, :].reshape(INNER, HALF)
        plain_vmem[:, cb * HALF : (cb + 1) * HALF] = dot(inner_vmem[...], w).astype(BF16)
    copies[2].wait()
    out = fetch([(plain_vmem, plain_ref)], sems.at[pl.ds(3, 1)])
    for cb in range(4):
        lanes = slice(cb * HALF, (cb + 1) * HALF)
        mixed_vmem[cb] = dot(plain_vmem[...], time_vmem[:, lanes]).astype(BF16)
        out += fetch([(mixed_vmem.at[cb], mixed_ref.at[cb])], sems.at[pl.ds(4 + cb, 1)])
    for copy in out:
        copy.wait()


def tokens_kernel(tok_ref, time_ref, out_ref, tok_vmem, time_vmem, out_vmem, sems):
    for copy in fetch([(tok_ref, tok_vmem), (time_ref, time_vmem)], sems):
        copy.wait()
    out_vmem[...] = dot(tok_vmem[...], time_vmem[...]).astype(BF16)
    fetch([(out_vmem, out_ref)], sems.at[pl.ds(2, 1)])[0].wait()


def join(ctx_ref):
    rows = 256
    return jnp.concatenate(
        [ctx_ref[:, 0].reshape(rows, HALF), ctx_ref[:, 1].reshape(rows, HALF)], axis=1
    )


def output_kernel(ctx_ref, tok_ref, w_ref, gain_ref, out_ref, w_vmem, tok_vmem, sems):
    copies = fetch(
        [(w_ref.at[cb], w_vmem.at[cb]) for cb in range(4)] + [(tok_ref, tok_vmem)], sems
    )
    rows = tok_ref.shape[0]
    ctx = join(ctx_ref)
    target = lax.broadcasted_iota(jnp.int32, (rows, rows), 0)
    source = (target % 32) // 4 * 32 + target // 32 * 4 + target % 4
    swap = (lax.broadcasted_iota(jnp.int32, (rows, rows), 1) == source).astype(BF16)
    branches = []
    for cb in range(4):
        copies[cb].wait()
        branches.append(dot(ctx, w_vmem[cb]).astype(BF16))
    copies[4].wait()
    mixed = []
    total = jnp.zeros((rows, 1), F32)
    for cb, branch in enumerate(branches):
        mix = tok_vmem[:, cb * HALF : (cb + 1) * HALF].astype(F32) + branch.astype(F32)
        mixed.append(mix)
        total += jnp.sum(mix * mix, axis=-1, keepdims=True)
    factor = lax.rsqrt(total * (1.0 / WIDTH) + EPSILON)
    for cb, mix in enumerate(mixed):
        lanes = slice(cb * HALF, (cb + 1) * HALF)
        normed = (mix * factor * gain_ref[:, lanes]).astype(BF16)
        out_ref[:, lanes] = dot(swap, normed).astype(BF16)


def branch_kernel(ctx_ref, w_ref, out_ref, w_vmem, sems):
    copies = fetch([(w_ref, w_vmem)], sems)
    ctx = join(ctx_ref)
    copies[0].wait()
    for cb in range(4):
        lanes = slice(cb * HALF, (cb + 1) * HALF)
        out_ref[:, lanes] = dot(ctx, w_vmem[:, lanes]).astype(BF16)


def temporal_kernel(x_ref, w_ref, out_ref, w_vmem, sems):
    copies = fetch([(w_ref.at[:, pl.ds(96 * i, 96)], w_vmem.at[i]) for i in range(6)], sems)
    rows = x_ref.shape[0]
    r = lax.broadcasted_iota(jnp.int32, (rows, rows), 0)
    s = lax.broadcasted_iota(jnp.int32, (rows, rows), 1)
    same = (r % 4 == s % 4) & ((r // 8) % 2 == (s // 8) % 2)
    seen = (r // 16) * 2 + (r // 4) % 2 >= (s // 16) * 2 + (s // 4) % 2
    for half in range(2):
        parts = []
        for i in range(3 * half, 3 * half + 3):
            copies[i].wait()
            parts.append(dot(x_ref[...], w_vmem[i].reshape(WIDTH, HALF)).astype(BF16))
        query, key, value = parts
        for i, block in enumerate(attend(query, (key,), (value,), same & seen)):
            lanes = slice(half * HALF + i * 128, half * HALF + (i + 1) * 128)
            out_ref[:, lanes] = block.astype(BF16)


SMEM = pl.BlockSpec(memory_space=pltpu.SMEM)
VMEM = pl.BlockSpec(memory_space=pltpu.VMEM)
HBM = pl.BlockSpec(memory_space=pltpu.HBM)


def call(kernel, name, specs, out_shapes, scratch, copies, mib=32, cost=None):
    if copies:
        scratch = scratch + [pltpu.SemaphoreType.DMA((copies,))]
    return pl.pallas_call(
        kernel,
        in_specs=specs,
        out_specs=[pl.BlockSpec(memory_space=space) for space, _ in out_shapes],
        out_shape=[
            pltpu.HBM(shape, BF16) if space is pltpu.HBM else jax.ShapeDtypeStruct(shape, BF16)
            for space, shape in out_shapes
        ],
        scratch_shapes=scratch,
        compiler_params=pltpu.CompilerParams(vmem_limit_bytes=mib * 1024 * 1024),
        cost_estimate=cost,
        name=name,
    )


def hbm(x):
    return pltpu.with_memory_space_constraint(x, pltpu.HBM)


def vmem(*shape):
    return pltpu.VMEM(shape, BF16)


def pick(first, a, b, axis):
    return jnp.where(first, jnp.concatenate([a, b], axis), jnp.concatenate([b, a], axis))


def per_device(tokens, space_gain, spatial_project, spatial_output, time_gain, temporal_project):
    core = lax.axis_index("core")
    x_hi = lax.axis_index("x_hi")
    tm = lax.axis_index(TM)
    swap = [(0, 1), (1, 0)]
    space_order = jnp.asarray(one_hot((16, 16, 6), (1, 0, 2)))
    inner_order = jnp.asarray(one_hot((16, 16, 3), (1, 0, 2)))
    time_order = jnp.asarray(one_hot((16, 16, 2, 3), (1, 2, 0, 3)))

    wq = lax.dynamic_slice_in_dim(spatial_project, tm * 6, 6, 0)
    wq = wq.reshape(6, 3, 2, HALF).transpose(2, 1, 0, 3).reshape(2, 18, HALF)
    wo = lax.dynamic_slice_in_dim(spatial_output, tm * 3, 3, 0)
    wo = wo.reshape(3, 4, HALF).transpose(1, 0, 2).reshape(12, HALF)
    wt = lax.dynamic_slice_in_dim(temporal_project, tm * 6, 6, 0)
    wt = wt.reshape(2, 3, 3, 2, HALF).transpose(0, 3, 2, 1, 4).reshape(2, 18, HALF)
    chunk = jnp.stack([jnp.concatenate([wo, wq[i], wt[i]], 0) for i in range(2)])
    chunk = jnp.broadcast_to(chunk[None], (8, 2, 48, HALF)).reshape(16, 48, HALF)
    got = lax.all_to_all(chunk, DP, 0, 0, tiled=True)
    across = lax.ppermute(tokens, "x_hi", swap)

    def moved(block):
        return lax.ppermute(
            lax.dynamic_index_in_dim(block, 1 - core, 1, keepdims=False), "core", swap
        )

    core_id = core.reshape(1).astype(jnp.int32)
    xh_id = x_hi.reshape(1).astype(jnp.int32)
    gain = space_gain.reshape(1, WIDTH)
    halves = tokens.reshape(4, 2, 32, WIDTH)
    frames, own = call(
        own_kernel,
        "space_norm_own",
        [SMEM] + [VMEM] * 3 + [HBM],
        [(pltpu.HBM, (8, 32, WIDTH)), (pltpu.HBM, (8, 1, 32, WIDTH))],
        [vmem(8, 32, WIDTH), vmem(8, 1, 32, WIDTH), vmem(WIDTH, WIDTH)],
        3,
        20,
        cost=pl.CostEstimate(flops=1, bytes_accessed=1, transcendentals=0),
    )(core_id, halves, moved(halves), gain, hbm(space_order))
    across, own = lax.optimization_barrier((across, own))
    halves = across.reshape(4, 2, 32, WIDTH)
    (normed,) = call(
        other_kernel,
        "space_norm_other",
        [SMEM] * 2 + [VMEM] * 3 + [HBM] * 2,
        [(pltpu.VMEM, (8, 2, 32, WIDTH))],
        [vmem(8, 32, WIDTH), vmem(8, 1, 32, WIDTH), vmem(WIDTH, WIDTH)],
        2,
        20,
    )(core_id, xh_id, halves, moved(halves), gain, hbm(own), hbm(space_order))
    got, normed = lax.optimization_barrier((got, normed))
    w1 = jnp.concatenate(
        [
            got[:, :12].reshape(16, 4, 3, HALF).transpose(1, 0, 2, 3).reshape(192, HALF),
            got[:, 12:30].reshape(16, 3, 6, HALF).transpose(1, 0, 2, 3).reshape(288, HALF),
        ],
        0,
    )
    w2 = got[:, 30:].reshape(16, 6, 3, HALF).transpose(1, 0, 2, 3).reshape(6, 1, 48, HALF)
    w2 = pick(x_hi == 0, w2, lax.ppermute(w2, "x_hi", swap), 1).reshape(576, HALF)
    w1 = lax.all_gather(w1, TM, axis=0, tiled=False)
    (tokens_time,) = call(
        tokens_kernel,
        "time_tokens",
        [HBM] * 2,
        [(pltpu.HBM, (256, WIDTH))],
        [vmem(256, WIDTH), vmem(WIDTH, WIDTH), vmem(256, WIDTH)],
        3,
        16,
    )(hbm(frames.reshape(256, WIDTH)), hbm(time_order))
    frame = lax.all_to_all(normed.reshape(8, 64, WIDTH), "z", 0, 0, tiled=True)
    w2, frame, tokens_time = lax.optimization_barrier((w2, frame, tokens_time))
    w2 = lax.all_gather(w2, TM, axis=0, tiled=False)
    q, kv = call(
        project_kernel,
        "space_project",
        [VMEM, HBM],
        [(pltpu.VMEM, (512, HALF)), (pltpu.VMEM, (2, 512, HALF))],
        [vmem(3, 16, 96, HALF)],
        3,
    )(frame.reshape(512, WIDTH), hbm(w1))
    kvo = lax.ppermute(kv, "core", swap)
    (ctx,) = call(spatial_kernel, "space_attend", [VMEM] * 3, [(pltpu.VMEM, (512, HALF))], [], 0, 20)(
        q, kv, kvo
    )
    w1, ctx = lax.optimization_barrier((w1, ctx))
    plain, mixed = call(
        weights_kernel,
        "output_weights",
        [HBM] * 3,
        [(pltpu.HBM, (INNER, WIDTH)), (pltpu.HBM, (4, INNER, HALF))],
        [
            vmem(16, 192, HALF),
            vmem(INNER, INNER),
            vmem(WIDTH, WIDTH),
            vmem(INNER, WIDTH),
            vmem(4, INNER, HALF),
        ],
        8,
        24,
        cost=pl.CostEstimate(flops=5_400_000_000, bytes_accessed=15_000_000, transcendentals=0),
    )(hbm(w1), hbm(inner_order), hbm(time_order))
    gain = time_gain.reshape(16, 16, 2, 3).transpose(1, 2, 0, 3).reshape(1, WIDTH)
    ctx = lax.all_to_all(ctx.reshape(16, 32, HALF), DP, 0, 0, tiled=True).reshape(8, 2, 32, HALF)
    (normed_time,) = call(
        output_kernel,
        "space_output",
        [VMEM, HBM, HBM, VMEM],
        [(pltpu.VMEM, (256, WIDTH))],
        [vmem(4, INNER, HALF), vmem(256, WIDTH)],
        5,
        20,
    )(ctx, hbm(tokens_time), hbm(mixed), gain)
    ctx, normed_time = lax.optimization_barrier((ctx, normed_time))
    (branch,) = call(
        branch_kernel,
        "space_branch",
        [VMEM, HBM],
        [(pltpu.VMEM, (256, WIDTH))],
        [vmem(INNER, WIDTH)],
        1,
        12,
    )(ctx, hbm(plain))
    branch = branch.reshape(8, 32, WIDTH)
    mine = lax.dynamic_slice_in_dim(branch, core * 4, 4, 0)
    theirs = lax.dynamic_slice_in_dim(branch, (1 - core) * 4, 4, 0)
    back = lax.ppermute(theirs, "core", swap)
    branch = pick(core == 0, mine[:, None], back[:, None], 1).reshape(tokens.shape)

    columns = lax.all_to_all(normed_time.reshape(8, 32, WIDTH), TM[:2], 0, 0, tiled=True)
    (context,) = call(
        temporal_kernel,
        "time_attend",
        [VMEM, HBM],
        [(pltpu.VMEM, (256, INNER))],
        [vmem(6, 16, 96, HALF)],
        6,
    )(columns.reshape(256, WIDTH), hbm(w2))
    context = lax.all_to_all(context.reshape(16, 16, INNER), TM, 0, 0, tiled=True)
    context = context.reshape(8, 2, 2, 2, 4, INNER).transpose(2, 3, 1, 0, 4, 5)
    return branch, context.reshape(2, 2, 64, INNER)


def solution(mesh):
    fine = Mesh(mesh.devices.reshape(2, 4, 2, 8, 2), TM + DP)
    in_specs = (P(None, TM, DP, None), P(), P(DP, None), P(DP, None), P(), P(DP, None))
    out_specs = (P(None, TM, DP, None), P(None, TM, DP, None))
    return jax.shard_map(
        per_device, mesh=fine, in_specs=in_specs, out_specs=out_specs, check_vma=False
    )
```

time: 188 us -> 181 us (0.963)
  Pallas kernels: 33.3 us -> 47.3 us
  waiting for transfers between devices: 71.6 us -> 62.8 us
  other arithmetic: 8.66 us -> 1.03 us
  local copies, waits for them, and re-layouts: 12.6 us -> 6.69 us
    pallas_call x5 -> x9, Pallas kernels: 33.3 us -> 47.3 us  [the longest x1 10.6 us: per_device(): call(weights_kernel, 'output_weights', [HBM] * 3, [(pltpu.HBM, (INNER, WI...]
    all_to_all x1, waiting for transfers between devices: 39.3 us -> 28.1 us  [per_device(): frame = lax.all_to_all(normed.reshape(8, 64, WIDTH), 'z', 0, 0, tiled=True)]
    all_to_all x1, waiting for transfers between devices: 13 us -> 3.67 us  [per_device(): lax.all_to_all(ctx.reshape(16, 32, HALF), DP, 0, 0, tiled=True)]
    all_to_all x1, waiting for transfers between devices: 4.92 us -> 12.2 us  [per_device(): lax.all_to_all(normed_time.reshape(8, 32, WIDTH), TM[:2], 0, 0, tiled=True)]
    convert_element_type x2 -> x0, other arithmetic: 5.64 us -> none  [shuffle(): (lax.broadcasted_iota(jnp.int32, (size, size), 0) == source).astype(BF16)]
    ppermute x1, waiting for transfers between devices: 4.38 us -> 0.01 us  [per_device(): across = lax.ppermute(tokens, 'x_hi', swap)]
    unnamed x16 -> x8, local copies, waits for them, and re-layouts: 3.61 us -> 0.02 us
    all_to_all x1, waiting for transfers between devices: 0.4 us -> 3.68 us  [per_device(): got = lax.all_to_all(chunk, DP, 0, 0, tiled=True)]
  transfers between devices with their start and end apart: 12 -> 13, of which waited for: 7 -> 11; matrix products, arithmetic and copies ran while one was open for 8% -> 3% of each run, Pallas kernels for 18% -> 26%
where the time goes in v3:
time: 181 us; the launch traced here: 180 us
  waiting for transfers between devices  62.8 us (35%)
  starting transfers between devices  48 us (27%)
  Pallas kernels  47.3 us (26%)
  between operations  14.4 us (8%)
  local copies, waits for them, and re-layouts  6.69 us (4%)
    all_to_all x1, waiting for transfers between devices, per_device(): frame = lax.all_to_all(normed.reshape(8, 64, WIDTH), 'z', 0, 0, tiled=True)  28.1 us
    all_to_all x1, waiting for transfers between devices, per_device(): lax.all_to_all(normed_time.reshape(8, 32, WIDTH), TM[:2], 0, 0, tiled=True)  12.2 us
    pallas_call x1, Pallas kernels, per_device(): call(weights_kernel, 'output_weights', [HBM] * 3, [(pltpu.HBM, (INNER, WI...  10.6 us
    all_to_all x1, starting transfers between devices, per_device(): frame = lax.all_to_all(normed.reshape(8, 64, WIDTH), 'z', 0, 0, tiled=True)  9.22 us
    all_to_all x1, starting transfers between devices, per_device(): got = lax.all_to_all(chunk, DP, 0, 0, tiled=True)  8.8 us
    all_to_all x1, starting transfers between devices, per_device(): lax.all_to_all(ctx.reshape(16, 32, HALF), DP, 0, 0, tiled=True)  7.79 us
    all_to_all x1, waiting for transfers between devices, per_device(): lax.all_to_all(context.reshape(16, 16, INNER), TM, 0, 0, tiled=True)  7.29 us
    pallas_call x1, Pallas kernels, per_device(): call(temporal_kernel, 'time_attend', [VMEM, HBM], [(pltpu.VMEM, (256, INN...  6.48 us
  transfers between devices with their start and end apart: 13, of which 11 were waited for; matrix products, arithmetic and copies ran while one was open for 3% of the time, Pallas kernels for 26%

profile of v3, /device:TPU:1, one launch (start us, length us, event | category | flops | bytes accessed | tf_op | source)
XLA Modules:
  0.0 180.3 jit_solution(13886367741253772440)
XLA Ops:
  7.2 3.7 %collective-permute-start = (bf16[2,2,64,1536]{3,2,1,0:T(8,128)(2,1)}, bf16[2,2,64,1536]{3,2,1,0:T(8,128)(2,1)S(1)}, u32[]{:S(2)}, u32[]{:S(2)}) collective-permute-start(bf16[2,2,64,1536]{3,2,1,0:T(8,128)(2,1)} %param.9), channel_id=1, source_target_pairs={{0,1},{1,0},{2,3},{3,2},{4,5},{5,4},{6,7},{7,6},{8,9},{9,8},{10,11... | collective-permute-start | bytes 2359304 | tf_op jit(solution)/shard_map/ppermute | solution.py:281
  10.9 1.0 constant_dynamic-slice_fusion.1
  12.3 0.9 broadcast_in_dim.12
  13.1 8.8 %all-to-all-start = ((bf16[16,48,384]{2,1,0:T(8,128)(2,1)}), bf16[16,48,384]{2,1,0:T(8,128)(2,1)S(1)}, u32[]{:S(2)}, u32[]{:S(2)}) async-start(bf16[16,48,384]{2,1,0:T(8,128)(2,1)} %bitcast.6), calls=%async_computation | async-start | bytes 1179648 | tf_op jit(solution)/shard_map/all_to_all | solution.py:280
  22.0 1.0 collective-permute-start.1
  23.1 1.3 collective-permute-done.1.moved_ref
  24.4 4.9 %space_norm_own.1 = (bf16[8,32,1536]{2,1,0:T(8,128)(2,1)}, bf16[8,1,32,1536]{3,2,1,0:T(8,128)(2,1)}) custom-call(s32[1]{0:T(128)} %bitcast.7.core_ref, bf16[4,2,32,1536]{3,2,1,0:T(8,128)(2,1)S(1)} %bitcast.55, bf16[4,32,1536]{2,1,0:T(8,128)(2,1)S(1)} %collective-permute-done.1.moved_ref, f32[1,1536]{1,0:T(1,128)S(1)} %reshape.120.gain_ref, ...), custom_call_target="tpu_custom_call" | custom-call | flops 1 | bytes 1 | tf_op jit(solution)/shard_map/space_norm_own/pallas_call | solution.py:292
  30.3 1.3 collective-permute-done.2.moved_ref
  31.6 5.0 %space_norm_other.1 = bf16[8,2,32,1536]{3,2,1,0:T(8,128)(2,1)} custom-call(s32[1]{0:T(128)} %bitcast.7.core_ref, s32[1]{0:T(128)} %bitcast.8.xh_ref, bf16[4,2,32,1536]{3,2,1,0:T(8,128)(2,1)S(1)} %bitcast.57, bf16[4,32,1536]{2,1,0:T(8,128)(2,1)S(1)} %collective-permute-done.2.moved_ref, f32[1,1536]{1,0:T(1,128)S(1)} %reshape.120.gain_ref, ...), custom_call_target="tpu_custom_call" | custom-call | tf_op jit(solution)/shard_map/space_norm_other/pallas_call | solution.py:304
  36.7 3.7 %all-to-all-done = bf16[16,48,384]{2,1,0:T(8,128)(2,1)S(1)} async-done(((bf16[16,48,384]{2,1,0:T(8,128)(2,1)}), bf16[16,48,384]{2,1,0:T(8,128)(2,1)S(1)}, u32[]{:S(2)}, u32[]{:S(2)}) %all-to-all-start) | async-done | bytes 589856 | tf_op jit(solution)/shard_map/all_to_all | solution.py:280
  41.7 9.2 %all-to-all-start.1 = ((bf16[8,64,1536]{2,1,0:T(8,128)(2,1)}), bf16[8,64,1536]{2,1,0:T(8,128)(2,1)S(1)}, u32[]{:S(2)}, u32[]{:S(2)}) async-start(bf16[8,64,1536]{2,1,0:T(8,128)(2,1)} %bitcast.21), calls=%async_computation.1 | async-start | bytes 3145728 | tf_op jit(solution)/shard_map/all_to_all | solution.py:333
  51.3 3.7 %collective-permute-start.3 = (bf16[6,1,48,384]{3,2,0,1:T(8,128)(2,1)S(1)}, bf16[6,1,48,384]{3,2,0,1:T(8,128)(2,1)S(1)}, u32[]{:S(2)}, u32[]{:S(2)}) collective-permute-start(bf16[6,1,48,384]{3,2,0,1:T(8,128)(2,1)S(1)} %reshape.127), channel_id=1, source_target_pairs={{0,1},{1,0},{2,3},{3,2},{4,5},{5,4},{6,7},{7,6},{8,9},{9,8},{10,11... | collective-permute-start | bytes 663560 | tf_op jit(solution)/shard_map/ppermute | solution.py:322
  55.0 4.9 %time_tokens.1.tok_ref = bf16[256,1536]{1,0:T(8,128)(2,1)} custom-call(bf16[256,1536]{1,0:T(8,128)(2,1)} %bitcast.66, bf16[1536,1536]{1,0:T(8,128)(2,1)} %constant.51.clone.time_ref), custom_call_target="tpu_custom_call" | custom-call | tf_op jit(solution)/shard_map/time_tokens/pallas_call | solution.py:324
  61.1 28.1 %all-to-all-done.1 = bf16[8,64,1536]{2,1,0:T(8,128)(2,1)S(1)} async-done(((bf16[8,64,1536]{2,1,0:T(8,128)(2,1)}), bf16[8,64,1536]{2,1,0:T(8,128)(2,1)S(1)}, u32[]{:S(2)}, u32[]{:S(2)}) %all-to-all-start.1) | async-done | bytes 1572896 | tf_op jit(solution)/shard_map/all_to_all | solution.py:333
  89.2 1.9 %all-gather.5.cloned.1.call-done = bf16[7680,384]{1,0:T(8,128)(2,1)} async-done(((bf16[480,384]{1,0:T(8,128)(2,1)}), bf16[7680,384]{1,0:T(8,128)(2,1)}) %all-gather.5.cloned.1.call-update) | async-done | bytes 5898256 | tf_op jit(solution)/shard_map/all_gather | solution.py:323
  91.2 4.2 %space_project.1 = (bf16[512,384]{1,0:T(8,128)(2,1)S(1)}, bf16[2,512,384]{2,1,0:T(8,128)(2,1)S(1)}) custom-call(bf16[512,1536]{1,0:T(8,128)(2,1)S(1)} %bitcast.49, bf16[16,480,384]{2,1,0:T(8,128)(2,1)} %bitcast.59), custom_call_target="tpu_custom_call" | custom-call | tf_op jit(solution)/shard_map/space_project/pallas_call | solution.py:336
  95.4 1.0 collective-permute-start.4
  96.4 1.9 %collective-permute-done.4.kvo_ref = bf16[2,512,384]{2,1,0:T(8,128)(2,1)S(1)} collective-permute-done((bf16[2,512,384]{2,1,0:T(8,128)(2,1)S(1)}, bf16[2,512,384]{2,1,0:T(8,128)(2,1)S(1)}, u32[]{:S(2)}, u32[]{:S(2)}) %collective-permute-start.4) | collective-permute-done | bytes 786464 | tf_op jit(solution)/shard_map/ppermute | solution.py:344
  98.4 4.2 %space_attend.1 = bf16[512,384]{1,0:T(8,128)(2,1)} custom-call(bf16[512,384]{1,0:T(8,128)(2,1)S(1)} %get-tuple-element.26.q_ref, bf16[2,512,384]{2,1,0:T(8,128)(2,1)S(1)} %get-tuple-element.27.kv_ref, bf16[2,512,384]{2,1,0:T(8,128)(2,1)S(1)} %collective-permute-done.4.kvo_ref), custom_call_target="tpu_custom_call" | custom-call | tf_op jit(solution)/shard_map/space_attend/pallas_call | solution.py:345
  102.6 7.8 %all-to-all-start.2 = ((bf16[16,32,384]{2,1,0:T(8,128)(2,1)}), bf16[16,32,384]{2,1,0:T(8,128)(2,1)S(1)}, u32[]{:S(2)}, u32[]{:S(2)}) async-start(bf16[16,32,384]{2,1,0:T(8,128)(2,1)} %bitcast.24), calls=%async_computation.2 | async-start | bytes 786432 | tf_op jit(solution)/shard_map/all_to_all | solution.py:366
  111.1 10.6 %output_weights.1 = (bf16[768,1536]{1,0:T(8,128)(2,1)}, bf16[4,768,384]{2,1,0:T(8,128)(2,1)}) custom-call(bf16[16,480,384]{2,1,0:T(8,128)(2,1)} %bitcast.60, bf16[768,768]{1,0:T(8,128)(2,1)} %constant.50.clone.inner_ref, bf16[1536,1536]{1,0:T(8,128)(2,1)} %constant.51.clone.time_ref), custom_call_target="tpu_custom_call" | custom-call | flops 5400000000 | bytes 15000000 | tf_op jit(solution)/shard_map/output_weights/pallas_call | solution.py:349
  121.7 3.7 %all-to-all-done.2 = bf16[16,32,384]{2,1,0:T(8,128)(2,1)S(1)} async-done(((bf16[16,32,384]{2,1,0:T(8,128)(2,1)}), bf16[16,32,384]{2,1,0:T(8,128)(2,1)S(1)}, u32[]{:S(2)}, u32[]{:S(2)}) %all-to-all-start.2) | async-done | bytes 393248 | tf_op jit(solution)/shard_map/all_to_all | solution.py:366
  125.4 4.2 %space_output.1 = bf16[256,1536]{1,0:T(8,128)(2,1)} custom-call(bf16[8,2,32,384]{3,2,1,0:T(8,128)(2,1)S(1)} %bitcast.50, bf16[256,1536]{1,0:T(8,128)(2,1)} %time_tokens.1.tok_ref, bf16[4,768,384]{2,1,0:T(8,128)(2,1)} %get-tuple-element.31.w_ref, f32[1,1536]{1,0:T(1,128)S(1)} %reshape.134.gain_ref), custom_call_target="tpu_custom_call" | custom-call | tf_op jit(solution)/shard_map/space_output/pallas_call | solution.py:367
  129.7 3.6 %all-to-all-start.3 = ((bf16[8,32,1536]{2,1,0:T(8,128)(2,1)}), bf16[8,32,1536]{2,1,0:T(8,128)(2,1)S(1)}, u32[]{:S(2)}, u32[]{:S(2)}) async-start(bf16[8,32,1536]{2,1,0:T(8,128)(2,1)} %bitcast.31), calls=%async_computation.3 | async-start | bytes 1572864 | tf_op jit(solution)/shard_map/all_to_all | solution.py:392
  133.2 2.7 %space_branch.1 = bf16[256,1536]{1,0:T(8,128)(2,1)S(1)} custom-call(bf16[8,2,32,384]{3,2,1,0:T(8,128)(2,1)S(1)} %bitcast.51, bf16[768,1536]{1,0:T(8,128)(2,1)} %get-tuple-element.33.w_ref), custom_call_target="tpu_custom_call" | custom-call | tf_op jit(solution)/shard_map/space_branch/pallas_call | solution.py:377
  136.0 2.8 %collective-permute-start.5 = (bf16[4,32,1536]{2,1,0:T(8,128)(2,1)S(1)}, bf16[4,32,1536]{2,1,0:T(8,128)(2,1)S(1)}, u32[]{:S(2)}, u32[]{:S(2)}) collective-permute-start(bf16[4,32,1536]{2,1,0:T(8,128)(2,1)S(1)} %get-tuple-element.37), channel_id=1, source_target_pairs={{0,16},{16,0},{1,17},{17,1},{2,18},{18,2},{3,19},{19,3},{4,20},{20... | collective-permute-start | bytes 1179656 | tf_op jit(solution)/shard_map/ppermute | solution.py:389
  138.8 12.2 %all-to-all-done.3 = bf16[8,32,1536]{2,1,0:T(8,128)(2,1)S(1)} async-done(((bf16[8,32,1536]{2,1,0:T(8,128)(2,1)}), bf16[8,32,1536]{2,1,0:T(8,128)(2,1)S(1)}, u32[]{:S(2)}, u32[]{:S(2)}) %all-to-all-start.3) | async-done | bytes 786464 | tf_op jit(solution)/shard_map/all_to_all | solution.py:392
  150.9 1.0 all-gather.7.cloned.1.call-done
  151.9 6.5 %time_attend.1 = bf16[256,768]{1,0:T(8,128)(2,1)} custom-call(bf16[256,1536]{1,0:T(8,128)(2,1)S(1)} %bitcast.53, bf16[16,576,384]{2,1,0:T(8,128)(2,1)} %bitcast.58), custom_call_target="tpu_custom_call" | custom-call | tf_op jit(solution)/shard_map/time_attend/pallas_call | solution.py:393
  158.4 5.5 %all-to-all-start.4 = ((bf16[16,16,768]{2,1,0:T(8,128)(2,1)}), bf16[16,16,768]{2,1,0:T(8,128)(2,1)S(1)}, u32[]{:S(2)}, u32[]{:S(2)}) async-start(bf16[16,16,768]{2,1,0:T(8,128)(2,1)} %bitcast.34), calls=%async_computation.4 | async-start | bytes 786432 | tf_op jit(solution)/shard_map/all_to_all | solution.py:401
  164.1 1.0 copy.44
  165.1 7.3 %all-to-all-done.4 = bf16[16,16,768]{2,1,0:T(8,128)(2,1)S(1)} async-done(((bf16[16,16,768]{2,1,0:T(8,128)(2,1)}), bf16[16,16,768]{2,1,0:T(8,128)(2,1)S(1)}, u32[]{:S(2)}, u32[]{:S(2)}) %all-to-all-start.4) | async-done | bytes 393248 | tf_op jit(solution)/shard_map/all_to_all | solution.py:401
  (55 shorter events, 6.2 us)
Async XLA Ops:
  7.2 3.7 %copy-start = (bf16[48,1536]{1,0:T(8,128)(2,1)S(1)}, bf16[48,1536]{1,0:T(8,128)(2,1)}, u32[]{:S(2)}) copy-start(bf16[48,1536]{1,0:T(8,128)(2,1)} %param.12) | copy-start | bytes 442372
  7.2 14.8 %copy-start.1 = (bf16[2,2,64,1536]{3,2,1,0:T(8,128)(2,1)S(1)}, bf16[2,2,64,1536]{3,2,1,0:T(8,128)(2,1)}, u32[]{:S(2)}) copy-start(bf16[2,2,64,1536]{3,2,1,0:T(8,128)(2,1)} %param.9) | copy-start | bytes 2359300
  7.2 15.9 %copy-start.3 = (f32[1536]{0:T(1024)S(1)}, f32[1536]{0:T(1024)}, u32[]{:S(2)}) copy-start(f32[1536]{0:T(1024)} %param.10) | copy-start | bytes 18436
  7.2 22.2 %collective-permute-start = (bf16[2,2,64,1536]{3,2,1,0:T(8,128)(2,1)}, bf16[2,2,64,1536]{3,2,1,0:T(8,128)(2,1)S(1)}, u32[]{:S(2)}, u32[]{:S(2)}) collective-permute-start(bf16[2,2,64,1536]{3,2,1,0:T(8,128)(2,1)} %param.9), channel_id=1, source_target_pairs={{0,1},{1,0},{2,3},{3,2},{4,5},{5,4},{6,7},{7,6},{8,9},{9,8},{10,11... | collective-permute-start | bytes 2359304 | tf_op jit(solution)/shard_map/ppermute | solution.py:281
  13.1 27.2 %all-to-all-start = ((bf16[16,48,384]{2,1,0:T(8,128)(2,1)}), bf16[16,48,384]{2,1,0:T(8,128)(2,1)S(1)}, u32[]{:S(2)}, u32[]{:S(2)}) async-start(bf16[16,48,384]{2,1,0:T(8,128)(2,1)} %bitcast.6), calls=%async_computation | async-start | bytes 1179648 | tf_op jit(solution)/shard_map/all_to_all | solution.py:280
  21.9 69.2 %all-gather.5.cloned.1.call-start = ((), (), s32[]{:S(2)}) async-start(), calls=%async_computation.5 | async-start | bytes 6266880 | tf_op jit(solution)/shard_map/all_gather | solution.py:323
  22.0 2.4 %collective-permute-start.1 = (bf16[4,32,1536]{2,1,0:T(8,128)(2,1)S(1)}, bf16[4,32,1536]{2,1,0:T(8,128)(2,1)S(1)}, u32[]{:S(2)}, u32[]{:S(2)}) collective-permute-start(bf16[4,32,1536]{2,1,0:T(8,128)(2,1)S(1)} %dynamic-slice_bitcast_fusion.2), channel_id=1, source_target_pairs={{0,16},{16,0},{1,17},{17,1},{2,18},{18,2},{3,19},{19,3},{4,20},{20... | collective-permute-start | bytes 1179656 | tf_op jit(solution)/shard_map/ppermute | solution.py:284
  29.4 2.2 %collective-permute-start.2 = (bf16[4,32,1536]{2,1,0:T(8,128)(2,1)S(1)}, bf16[4,32,1536]{2,1,0:T(8,128)(2,1)S(1)}, u32[]{:S(2)}, u32[]{:S(2)}) collective-permute-start(bf16[4,32,1536]{2,1,0:T(8,128)(2,1)S(1)} %dynamic-slice_bitcast_fusion.1), channel_id=1, source_target_pairs={{0,16},{16,0},{1,17},{17,1},{2,18},{18,2},{3,19},{19,3},{4,20},{20... | collective-permute-start | bytes 1179656 | tf_op jit(solution)/shard_map/ppermute | solution.py:284
  41.7 47.5 %all-to-all-start.1 = ((bf16[8,64,1536]{2,1,0:T(8,128)(2,1)}), bf16[8,64,1536]{2,1,0:T(8,128)(2,1)S(1)}, u32[]{:S(2)}, u32[]{:S(2)}) async-start(bf16[8,64,1536]{2,1,0:T(8,128)(2,1)} %bitcast.21), calls=%async_computation.1 | async-start | bytes 3145728 | tf_op jit(solution)/shard_map/all_to_all | solution.py:333
  50.9 101.0 %all-gather.7.cloned.1.call-start = ((), (), s32[]{:S(2)}) async-start(), calls=%async_computation.6 | async-start | bytes 7520256 | tf_op jit(solution)/shard_map/all_gather | solution.py:335
  51.3 8.9 %collective-permute-start.3 = (bf16[6,1,48,384]{3,2,0,1:T(8,128)(2,1)S(1)}, bf16[6,1,48,384]{3,2,0,1:T(8,128)(2,1)S(1)}, u32[]{:S(2)}, u32[]{:S(2)}) collective-permute-start(bf16[6,1,48,384]{3,2,0,1:T(8,128)(2,1)S(1)} %reshape.127), channel_id=1, source_target_pairs={{0,1},{1,0},{2,3},{3,2},{4,5},{5,4},{6,7},{7,6},{8,9},{9,8},{10,11... | collective-permute-start | bytes 663560 | tf_op jit(solution)/shard_map/ppermute | solution.py:322
  95.4 15.0 %copy-start.2 = (f32[1536]{0:T(1024)S(1)}, f32[1536]{0:T(1024)}, u32[]{:S(2)}) copy-start(f32[1536]{0:T(1024)} %param.13) | copy-start | bytes 18436
  95.4 2.9 %collective-permute-start.4 = (bf16[2,512,384]{2,1,0:T(8,128)(2,1)S(1)}, bf16[2,512,384]{2,1,0:T(8,128)(2,1)S(1)}, u32[]{:S(2)}, u32[]{:S(2)}) collective-permute-start(bf16[2,512,384]{2,1,0:T(8,128)(2,1)S(1)} %get-tuple-element.27.kv_ref), channel_id=1, source_target_pairs={{0,16},{16,0},{1,17},{17,1},{2,18},{18,2},{3,19},{19,3},{4,20},{20... | collective-permute-start | bytes 2359304 | tf_op jit(solution)/shard_map/ppermute | solution.py:344
  102.6 22.9 %all-to-all-start.2 = ((bf16[16,32,384]{2,1,0:T(8,128)(2,1)}), bf16[16,32,384]{2,1,0:T(8,128)(2,1)S(1)}, u32[]{:S(2)}, u32[]{:S(2)}) async-start(bf16[16,32,384]{2,1,0:T(8,128)(2,1)} %bitcast.24), calls=%async_computation.2 | async-start | bytes 786432 | tf_op jit(solution)/shard_map/all_to_all | solution.py:366
  129.7 21.3 %all-to-all-start.3 = ((bf16[8,32,1536]{2,1,0:T(8,128)(2,1)}), bf16[8,32,1536]{2,1,0:T(8,128)(2,1)S(1)}, u32[]{:S(2)}, u32[]{:S(2)}) async-start(bf16[8,32,1536]{2,1,0:T(8,128)(2,1)} %bitcast.31), calls=%async_computation.3 | async-start | bytes 1572864 | tf_op jit(solution)/shard_map/all_to_all | solution.py:392
  136.0 28.0 %collective-permute-start.5 = (bf16[4,32,1536]{2,1,0:T(8,128)(2,1)S(1)}, bf16[4,32,1536]{2,1,0:T(8,128)(2,1)S(1)}, u32[]{:S(2)}, u32[]{:S(2)}) collective-permute-start(bf16[4,32,1536]{2,1,0:T(8,128)(2,1)S(1)} %get-tuple-element.37), channel_id=1, source_target_pairs={{0,16},{16,0},{1,17},{17,1},{2,18},{18,2},{3,19},{19,3},{4,20},{20... | collective-permute-start | bytes 1179656 | tf_op jit(solution)/shard_map/ppermute | solution.py:389
  158.4 13.9 %all-to-all-start.4 = ((bf16[16,16,768]{2,1,0:T(8,128)(2,1)}), bf16[16,16,768]{2,1,0:T(8,128)(2,1)S(1)}, u32[]{:S(2)}, u32[]{:S(2)}) async-start(bf16[16,16,768]{2,1,0:T(8,128)(2,1)} %bitcast.34), calls=%async_computation.4 | async-start | bytes 786432 | tf_op jit(solution)/shard_map/all_to_all | solution.py:401
Sparse Core Ops, SparseCore 0:
  41.8 49.2 all-gather.4
  93.0 58.8 all-gather.6

commit v4 on v3

--- a/solution.py
+++ b/solution.py
@@ -127,7 +127,10 @@
         rows = slice(first, first + 256)
         blocks = attend(q_ref[rows], (kv_ref[0], kvo_ref[0]), (kv_ref[1], kvo_ref[1]))
         for i, block in enumerate(blocks):
-            out_ref[rows, i * 128 : (i + 1) * 128] = block.astype(BF16)
+            block = block.astype(BF16).reshape(4, 2, 32, 128)
+            for xh in range(2):
+                z = slice(first // 64, first // 64 + 4)
+                out_ref[xh, z, :, i * 128 : (i + 1) * 128] = block[:, xh]
 
 
 def weights_kernel(
@@ -164,21 +167,14 @@
     fetch([(out_vmem, out_ref)], sems.at[pl.ds(2, 1)])[0].wait()
 
 
-def join(ctx_ref):
-    rows = 256
-    return jnp.concatenate(
-        [ctx_ref[:, 0].reshape(rows, HALF), ctx_ref[:, 1].reshape(rows, HALF)], axis=1
-    )
-
-
 def output_kernel(ctx_ref, tok_ref, w_ref, gain_ref, out_ref, w_vmem, tok_vmem, sems):
     copies = fetch(
         [(w_ref.at[cb], w_vmem.at[cb]) for cb in range(4)] + [(tok_ref, tok_vmem)], sems
     )
     rows = tok_ref.shape[0]
-    ctx = join(ctx_ref)
+    ctx = jnp.concatenate([ctx_ref[0], ctx_ref[1]], axis=1)
     target = lax.broadcasted_iota(jnp.int32, (rows, rows), 0)
-    source = (target % 32) // 4 * 32 + target // 32 * 4 + target % 4
+    source = (target % 64) // 8 * 32 + target // 64 * 8 + target % 8
     swap = (lax.broadcasted_iota(jnp.int32, (rows, rows), 1) == source).astype(BF16)
     branches = []
     for cb in range(4):
@@ -195,12 +191,14 @@
     for cb, mix in enumerate(mixed):
         lanes = slice(cb * HALF, (cb + 1) * HALF)
         normed = (mix * factor * gain_ref[:, lanes]).astype(BF16)
-        out_ref[:, lanes] = dot(swap, normed).astype(BF16)
+        normed = dot(swap, normed).astype(BF16)
+        out_ref[0, :, lanes] = normed
+        out_ref[1, :, lanes] = normed
 
 
 def branch_kernel(ctx_ref, w_ref, out_ref, w_vmem, sems):
     copies = fetch([(w_ref, w_vmem)], sems)
-    ctx = join(ctx_ref)
+    ctx = jnp.concatenate([ctx_ref[0], ctx_ref[1]], axis=1)
     copies[0].wait()
     for cb in range(4):
         lanes = slice(cb * HALF, (cb + 1) * HALF)
@@ -208,21 +206,20 @@
 
 
 def temporal_kernel(x_ref, w_ref, out_ref, w_vmem, sems):
-    copies = fetch([(w_ref.at[:, pl.ds(96 * i, 96)], w_vmem.at[i]) for i in range(6)], sems)
-    rows = x_ref.shape[0]
-    r = lax.broadcasted_iota(jnp.int32, (rows, rows), 0)
-    s = lax.broadcasted_iota(jnp.int32, (rows, rows), 1)
-    same = (r % 4 == s % 4) & ((r // 8) % 2 == (s // 8) % 2)
-    seen = (r // 16) * 2 + (r // 4) % 2 >= (s // 16) * 2 + (s // 4) % 2
-    for half in range(2):
-        parts = []
-        for i in range(3 * half, 3 * half + 3):
-            copies[i].wait()
-            parts.append(dot(x_ref[...], w_vmem[i].reshape(WIDTH, HALF)).astype(BF16))
-        query, key, value = parts
-        for i, block in enumerate(attend(query, (key,), (value,), same & seen)):
-            lanes = slice(half * HALF + i * 128, half * HALF + (i + 1) * 128)
-            out_ref[:, lanes] = block.astype(BF16)
+    copies = fetch([(w_ref.at[:, pl.ds(192 * i, 192)], w_vmem.at[i]) for i in range(3)], sems)
+    r = lax.broadcasted_iota(jnp.int32, (256, 256), 0)
+    s = lax.broadcasted_iota(jnp.int32, (256, 256), 1)
+    mask = (r % 8 == s % 8) & (r // 8 >= s // 8)
+    parts = []
+    for i in range(3):
+        copies[i].wait()
+        part = dot(x_ref[...], w_vmem[i].reshape(WIDTH, HALF)).astype(BF16)
+        parts.append(part.reshape(16, 2, 16, HALF))
+    for history in range(2):
+        query, key, value = (part[:, history].reshape(256, HALF) for part in parts)
+        for i, block in enumerate(attend(query, (key,), (value,), mask)):
+            block = block.astype(BF16).reshape(16, 16, 128)
+            out_ref[:, history, :, i * 128 : (i + 1) * 128] = block
 
 
 SMEM = pl.BlockSpec(memory_space=pltpu.SMEM)
@@ -262,19 +259,22 @@
 
 def per_device(tokens, space_gain, spatial_project, spatial_output, time_gain, temporal_project):
     core = lax.axis_index("core")
+    x_lo = lax.axis_index("x_lo")
     x_hi = lax.axis_index("x_hi")
     tm = lax.axis_index(TM)
     swap = [(0, 1), (1, 0)]
     space_order = jnp.asarray(one_hot((16, 16, 6), (1, 0, 2)))
     inner_order = jnp.asarray(one_hot((16, 16, 3), (1, 0, 2)))
-    time_order = jnp.asarray(one_hot((16, 16, 2, 3), (1, 2, 0, 3)))
+    time_order = jnp.asarray(one_hot((16, 4, 2, 2, 6), (1, 2, 3, 0, 4)))
 
     wq = lax.dynamic_slice_in_dim(spatial_project, tm * 6, 6, 0)
     wq = wq.reshape(6, 3, 2, HALF).transpose(2, 1, 0, 3).reshape(2, 18, HALF)
     wo = lax.dynamic_slice_in_dim(spatial_output, tm * 3, 3, 0)
     wo = wo.reshape(3, 4, HALF).transpose(1, 0, 2).reshape(12, HALF)
-    wt = lax.dynamic_slice_in_dim(temporal_project, tm * 6, 6, 0)
-    wt = wt.reshape(2, 3, 3, 2, HALF).transpose(0, 3, 2, 1, 4).reshape(2, 18, HALF)
+    row = lax.axis_index(TM[1:]) * 12
+    wt = lax.dynamic_slice_in_dim(temporal_project, row, 12, 0).reshape(2, 6, 3, 2, HALF)
+    wt = lax.dynamic_index_in_dim(wt, x_lo, 3, keepdims=False)
+    wt = wt.transpose(0, 2, 1, 3).reshape(2, 18, HALF)
     chunk = jnp.stack([jnp.concatenate([wo, wq[i], wt[i]], 0) for i in range(2)])
     chunk = jnp.broadcast_to(chunk[None], (8, 2, 48, HALF)).reshape(16, 48, HALF)
     got = lax.all_to_all(chunk, DP, 0, 0, tiled=True)
@@ -318,7 +318,7 @@
         ],
         0,
     )
-    w2 = got[:, 30:].reshape(16, 6, 3, HALF).transpose(1, 0, 2, 3).reshape(6, 1, 48, HALF)
+    w2 = got[:, 30:].reshape(16, 3, 6, HALF).transpose(1, 0, 2, 3).reshape(3, 1, 96, HALF)
     w2 = pick(x_hi == 0, w2, lax.ppermute(w2, "x_hi", swap), 1).reshape(576, HALF)
     w1 = lax.all_gather(w1, TM, axis=0, tiled=False)
     (tokens_time,) = call(
@@ -332,7 +332,7 @@
     )(hbm(frames.reshape(256, WIDTH)), hbm(time_order))
     frame = lax.all_to_all(normed.reshape(8, 64, WIDTH), "z", 0, 0, tiled=True)
     w2, frame, tokens_time = lax.optimization_barrier((w2, frame, tokens_time))
-    w2 = lax.all_gather(w2, TM, axis=0, tiled=False)
+    w2 = lax.all_gather(w2, TM[1:], axis=0, tiled=False)
     q, kv = call(
         project_kernel,
         "space_project",
@@ -342,7 +342,7 @@
         3,
     )(frame.reshape(512, WIDTH), hbm(w1))
     kvo = lax.ppermute(kv, "core", swap)
-    (ctx,) = call(spatial_kernel, "space_attend", [VMEM] * 3, [(pltpu.VMEM, (512, HALF))], [], 0, 20)(
+    (ctx,) = call(spatial_kernel, "space_attend", [VMEM] * 3, [(pltpu.VMEM, (2, 8, 32, HALF))], [], 0, 20)(
         q, kv, kvo
     )
     w1, ctx = lax.optimization_barrier((w1, ctx))
@@ -362,13 +362,14 @@
         24,
         cost=pl.CostEstimate(flops=5_400_000_000, bytes_accessed=15_000_000, transcendentals=0),
     )(hbm(w1), hbm(inner_order), hbm(time_order))
-    gain = time_gain.reshape(16, 16, 2, 3).transpose(1, 2, 0, 3).reshape(1, WIDTH)
-    ctx = lax.all_to_all(ctx.reshape(16, 32, HALF), DP, 0, 0, tiled=True).reshape(8, 2, 32, HALF)
+    gain = time_gain.reshape(16, 4, 2, 2, 6).transpose(1, 2, 3, 0, 4).reshape(1, WIDTH)
+    ctx = lax.all_to_all(ctx.reshape(16, 32, HALF), DP[::-1], 0, 0, tiled=True)
+    ctx = ctx.reshape(2, 256, HALF)
     (normed_time,) = call(
         output_kernel,
         "space_output",
         [VMEM, HBM, HBM, VMEM],
-        [(pltpu.VMEM, (256, WIDTH))],
+        [(pltpu.VMEM, (2, 256, WIDTH))],
         [vmem(4, INNER, HALF), vmem(256, WIDTH)],
         5,
         20,
@@ -389,17 +390,17 @@
     back = lax.ppermute(theirs, "core", swap)
     branch = pick(core == 0, mine[:, None], back[:, None], 1).reshape(tokens.shape)
 
-    columns = lax.all_to_all(normed_time.reshape(8, 32, WIDTH), TM[:2], 0, 0, tiled=True)
+    columns = lax.all_to_all(normed_time.reshape(8, 64, WIDTH), TM[:2], 0, 0, tiled=True)
     (context,) = call(
         temporal_kernel,
         "time_attend",
         [VMEM, HBM],
-        [(pltpu.VMEM, (256, INNER))],
-        [vmem(6, 16, 96, HALF)],
-        6,
-    )(columns.reshape(256, WIDTH), hbm(w2))
-    context = lax.all_to_all(context.reshape(16, 16, INNER), TM, 0, 0, tiled=True)
-    context = context.reshape(8, 2, 2, 2, 4, INNER).transpose(2, 3, 1, 0, 4, 5)
+        [(pltpu.VMEM, (16, 2, 16, HALF))],
+        [vmem(3, 8, 192, HALF)],
+        3,
+    )(columns.reshape(512, WIDTH), hbm(w2))
+    context = lax.all_to_all(context.reshape(16, 32, HALF), TM, 0, 0, tiled=True)
+    context = context.reshape(2, 4, 2, 2, 2, 8, HALF).transpose(3, 4, 2, 1, 5, 0, 6)
     return branch, context.reshape(2, 2, 64, INNER)
 
 

time: 181 us -> 179 us (0.989)
  waiting for transfers between devices: 62.8 us -> 59.7 us
    all_to_all x3, waiting for transfers between devices: 23.1 us -> 21.2 us  [the longest x1 12.3 us: per_device(): lax.all_to_all(normed_time.reshape(8, 64, WIDTH), TM[:2], 0, 0, tiled=True)]
  transfers between devices with their start and end apart: 13 -> 13, of which waited for: 11 -> 10; matrix products, arithmetic and copies ran while one was open for 3% -> 3% of each run, Pallas kernels for 26% -> 26%
where the time goes in v4:
time: 179 us; the launch traced here: 178 us
  waiting for transfers between devices  59.7 us (33%)
  starting transfers between devices  49.1 us (27%)
  Pallas kernels  45.6 us (25%)
  between operations  14.5 us (8%)
  local copies, waits for them, and re-layouts  7.94 us (4%)
    all_to_all x1, waiting for transfers between devices, per_device(): frame = lax.all_to_all(normed.reshape(8, 64, WIDTH), 'z', 0, 0, tiled=True)  28.3 us
    all_to_all x1, waiting for transfers between devices, per_device(): lax.all_to_all(normed_time.reshape(8, 64, WIDTH), TM[:2], 0, 0, tiled=True)  12.3 us
    pallas_call x1, Pallas kernels, per_device(): call(weights_kernel, 'output_weights', [HBM] * 3, [(pltpu.HBM, (INNER, WI...  10.6 us
    all_to_all x1, starting transfers between devices, per_device(): frame = lax.all_to_all(normed.reshape(8, 64, WIDTH), 'z', 0, 0, tiled=True)  8.99 us
    all_to_all x1, starting transfers between devices, per_device(): got = lax.all_to_all(chunk, DP, 0, 0, tiled=True)  8.29 us
    all_to_all x1, starting transfers between devices, per_device(): ctx = lax.all_to_all(ctx.reshape(16, 32, HALF), DP[::-1], 0, 0, tiled=True)  7.82 us
    all_to_all x1, waiting for transfers between devices, per_device(): lax.all_to_all(context.reshape(16, 32, HALF), TM, 0, 0, tiled=True)  7.29 us
    all_to_all x1, starting transfers between devices, per_device(): lax.all_to_all(context.reshape(16, 32, HALF), TM, 0, 0, tiled=True)  6.77 us
  transfers between devices with their start and end apart: 13, of which 10 were waited for; matrix products, arithmetic and copies ran while one was open for 3% of the time, Pallas kernels for 26%

profile of v4, /device:TPU:1, one launch (start us, length us, event | category | flops | bytes accessed | tf_op | source)
XLA Modules:
  0.0 177.9 jit_solution(12073657565193075894)
XLA Ops:
  7.2 3.7 %collective-permute-start = (bf16[2,2,64,1536]{3,2,1,0:T(8,128)(2,1)}, bf16[2,2,64,1536]{3,2,1,0:T(8,128)(2,1)S(1)}, u32[]{:S(2)}, u32[]{:S(2)}) collective-permute-start(bf16[2,2,64,1536]{3,2,1,0:T(8,128)(2,1)} %param.9), channel_id=1, source_target_pairs={{0,1},{1,0},{2,3},{3,2},{4,5},{5,4},{6,7},{7,6},{8,9},{9,8},{10,11... | collective-permute-start | bytes 2359304 | tf_op jit(solution)/shard_map/ppermute | solution.py:281
  12.0 0.9 constant_dynamic-slice_fusion.3
  13.1 0.9 broadcast_in_dim.12
  14.0 8.3 %all-to-all-start = ((bf16[16,48,384]{2,1,0:T(8,128)(2,1)}), bf16[16,48,384]{2,1,0:T(8,128)(2,1)S(1)}, u32[]{:S(2)}, u32[]{:S(2)}) async-start(bf16[16,48,384]{2,1,0:T(8,128)(2,1)} %bitcast.8), calls=%async_computation | async-start | bytes 1179648 | tf_op jit(solution)/shard_map/all_to_all | solution.py:280
  22.4 1.3 collective-permute-start.1
  23.8 1.3 collective-permute-done.1.moved_ref
  25.1 4.9 %space_norm_own.1 = (bf16[8,32,1536]{2,1,0:T(8,128)(2,1)}, bf16[8,1,32,1536]{3,2,1,0:T(8,128)(2,1)}) custom-call(s32[1]{0:T(128)} %bitcast.9.core_ref, bf16[4,2,32,1536]{3,2,1,0:T(8,128)(2,1)S(1)} %bitcast.61, bf16[4,32,1536]{2,1,0:T(8,128)(2,1)S(1)} %collective-permute-done.1.moved_ref, f32[1,1536]{1,0:T(1,128)S(1)} %reshape.120.gain_ref, ...), custom_call_target="tpu_custom_call" | custom-call | flops 1 | bytes 1 | tf_op jit(solution)/shard_map/space_norm_own/pallas_call | solution.py:292
  30.6 1.3 collective-permute-done.2.moved_ref
  31.9 5.0 %space_norm_other.1 = bf16[8,2,32,1536]{3,2,1,0:T(8,128)(2,1)} custom-call(s32[1]{0:T(128)} %bitcast.9.core_ref, s32[1]{0:T(128)} %bitcast.10.xh_ref, bf16[4,2,32,1536]{3,2,1,0:T(8,128)(2,1)S(1)} %bitcast.63, bf16[4,32,1536]{2,1,0:T(8,128)(2,1)S(1)} %collective-permute-done.2.moved_ref, f32[1,1536]{1,0:T(1,128)S(1)} %reshape.120.gain_ref, ...), custom_call_target="tpu_custom_call" | custom-call | tf_op jit(solution)/shard_map/space_norm_other/pallas_call | solution.py:304
  36.9 3.7 %all-to-all-done = bf16[16,48,384]{2,1,0:T(8,128)(2,1)S(1)} async-done(((bf16[16,48,384]{2,1,0:T(8,128)(2,1)}), bf16[16,48,384]{2,1,0:T(8,128)(2,1)S(1)}, u32[]{:S(2)}, u32[]{:S(2)}) %all-to-all-start) | async-done | bytes 589856 | tf_op jit(solution)/shard_map/all_to_all | solution.py:280
  42.0 9.0 %all-to-all-start.1 = ((bf16[8,64,1536]{2,1,0:T(8,128)(2,1)}), bf16[8,64,1536]{2,1,0:T(8,128)(2,1)S(1)}, u32[]{:S(2)}, u32[]{:S(2)}) async-start(bf16[8,64,1536]{2,1,0:T(8,128)(2,1)} %bitcast.23), calls=%async_computation.1 | async-start | bytes 3145728 | tf_op jit(solution)/shard_map/all_to_all | solution.py:333
  51.2 3.7 %collective-permute-start.3 = (bf16[3,1,96,384]{3,2,0,1:T(8,128)(2,1)S(1)}, bf16[3,1,96,384]{3,2,0,1:T(8,128)(2,1)S(1)}, u32[]{:S(2)}, u32[]{:S(2)}) collective-permute-start(bf16[3,1,96,384]{3,2,0,1:T(8,128)(2,1)S(1)} %reshape.127), channel_id=1, source_target_pairs={{0,1},{1,0},{2,3},{3,2},{4,5},{5,4},{6,7},{7,6},{8,9},{9,8},{10,11... | collective-permute-start | bytes 663560 | tf_op jit(solution)/shard_map/ppermute | solution.py:322
  54.8 4.9 %time_tokens.1.tok_ref = bf16[256,1536]{1,0:T(8,128)(2,1)} custom-call(bf16[256,1536]{1,0:T(8,128)(2,1)} %bitcast.71, bf16[1536,1536]{1,0:T(8,128)(2,1)} %constant.53.clone.order_ref.time_ref), custom_call_target="tpu_custom_call" | custom-call | tf_op jit(solution)/shard_map/time_tokens/pallas_call | solution.py:324
  60.9 28.3 %all-to-all-done.1 = bf16[8,64,1536]{2,1,0:T(8,128)(2,1)S(1)} async-done(((bf16[8,64,1536]{2,1,0:T(8,128)(2,1)}), bf16[8,64,1536]{2,1,0:T(8,128)(2,1)S(1)}, u32[]{:S(2)}, u32[]{:S(2)}) %all-to-all-start.1) | async-done | bytes 1572896 | tf_op jit(solution)/shard_map/all_to_all | solution.py:333
  89.2 1.6 all-gather.5.cloned.1.call-done
  90.8 4.2 %space_project.1 = (bf16[512,384]{1,0:T(8,128)(2,1)S(1)}, bf16[2,512,384]{2,1,0:T(8,128)(2,1)S(1)}) custom-call(bf16[512,1536]{1,0:T(8,128)(2,1)S(1)} %bitcast.54, bf16[16,480,384]{2,1,0:T(8,128)(2,1)} %bitcast.64), custom_call_target="tpu_custom_call" | custom-call | tf_op jit(solution)/shard_map/space_project/pallas_call | solution.py:336
  95.1 1.4 collective-permute-start.4
  96.5 1.9 %collective-permute-done.4.kvo_ref = bf16[2,512,384]{2,1,0:T(8,128)(2,1)S(1)} collective-permute-done((bf16[2,512,384]{2,1,0:T(8,128)(2,1)S(1)}, bf16[2,512,384]{2,1,0:T(8,128)(2,1)S(1)}, u32[]{:S(2)}, u32[]{:S(2)}) %collective-permute-start.4) | collective-permute-done | bytes 786464 | tf_op jit(solution)/shard_map/ppermute | solution.py:344
  98.4 4.2 %space_attend.1 = bf16[2,8,32,384]{3,2,1,0:T(8,128)(2,1)} custom-call(bf16[512,384]{1,0:T(8,128)(2,1)S(1)} %get-tuple-element.26.q_ref, bf16[2,512,384]{2,1,0:T(8,128)(2,1)S(1)} %get-tuple-element.27.kv_ref, bf16[2,512,384]{2,1,0:T(8,128)(2,1)S(1)} %collective-permute-done.4.kvo_ref), custom_call_target="tpu_custom_call" | custom-call | tf_op jit(solution)/shard_map/space_attend/pallas_call | solution.py:345
  102.6 7.8 %all-to-all-start.2 = ((bf16[16,32,384]{2,1,0:T(8,128)(2,1)}), bf16[16,32,384]{2,1,0:T(8,128)(2,1)S(1)}, u32[]{:S(2)}, u32[]{:S(2)}) async-start(bf16[16,32,384]{2,1,0:T(8,128)(2,1)} %bitcast.26), calls=%async_computation.2 | async-start | bytes 786432 | tf_op jit(solution)/shard_map/all_to_all | solution.py:366
  110.8 10.6 %output_weights.1 = (bf16[768,1536]{1,0:T(8,128)(2,1)}, bf16[4,768,384]{2,1,0:T(8,128)(2,1)}) custom-call(bf16[16,480,384]{2,1,0:T(8,128)(2,1)} %bitcast.65, bf16[768,768]{1,0:T(8,128)(2,1)} %constant.54.clone.inner_ref, bf16[1536,1536]{1,0:T(8,128)(2,1)} %constant.53.clone.order_ref.time_ref), custom_call_target="tpu_custom_call" | custom-call | flops 5400000000 | bytes 15000000 | tf_op jit(solution)/shard_map/output_weights/pallas_call | solution.py:349
  121.5 1.6 all-to-all-done.2
  123.1 3.4 %space_output.1 = bf16[2,256,1536]{2,1,0:T(8,128)(2,1)S(1)} custom-call(bf16[2,256,384]{2,1,0:T(8,128)(2,1)S(1)} %bitcast.57, bf16[256,1536]{1,0:T(8,128)(2,1)} %time_tokens.1.tok_ref, bf16[4,768,384]{2,1,0:T(8,128)(2,1)} %get-tuple-element.31.w_ref, f32[1,1536]{1,0:T(1,128)S(1)} %reshape.134.gain_ref), custom_call_target="tpu_custom_call" | custom-call | tf_op jit(solution)/shard_map/space_output/pallas_call | solution.py:368
  126.4 1.2 copy-done.1
  127.6 3.6 %all-to-all-start.3 = ((bf16[8,64,1536]{2,1,0:T(8,128)(2,1)}), bf16[8,64,1536]{2,1,0:T(8,128)(2,1)S(1)}, u32[]{:S(2)}, u32[]{:S(2)}) async-start(bf16[8,64,1536]{2,1,0:T(8,128)(2,1)} %bitcast.56), calls=%async_computation.3 | async-start | bytes 3145728 | tf_op jit(solution)/shard_map/all_to_all | solution.py:393
  131.2 2.7 %space_branch.1 = bf16[256,1536]{1,0:T(8,128)(2,1)S(1)} custom-call(bf16[2,256,384]{2,1,0:T(8,128)(2,1)S(1)} %bitcast.58, bf16[768,1536]{1,0:T(8,128)(2,1)} %get-tuple-element.33.w_ref), custom_call_target="tpu_custom_call" | custom-call | tf_op jit(solution)/shard_map/space_branch/pallas_call | solution.py:378
  133.9 3.1 %collective-permute-start.5 = (bf16[4,32,1536]{2,1,0:T(8,128)(2,1)S(1)}, bf16[4,32,1536]{2,1,0:T(8,128)(2,1)S(1)}, u32[]{:S(2)}, u32[]{:S(2)}) collective-permute-start(bf16[4,32,1536]{2,1,0:T(8,128)(2,1)S(1)} %get-tuple-element.37), channel_id=1, source_target_pairs={{0,16},{16,0},{1,17},{17,1},{2,18},{18,2},{3,19},{19,3},{4,20},{20... | collective-permute-start | bytes 1179656 | tf_op jit(solution)/shard_map/ppermute | solution.py:390
  137.0 12.3 %all-to-all-done.3 = bf16[8,64,1536]{2,1,0:T(8,128)(2,1)S(1)} async-done(((bf16[8,64,1536]{2,1,0:T(8,128)(2,1)}), bf16[8,64,1536]{2,1,0:T(8,128)(2,1)S(1)}, u32[]{:S(2)}, u32[]{:S(2)}) %all-to-all-start.3) | async-done | bytes 1572896 | tf_op jit(solution)/shard_map/all_to_all | solution.py:393
  149.4 5.8 %time_attend.1 = bf16[16,2,16,384]{3,2,1,0:T(8,128)(2,1)} custom-call(bf16[512,1536]{1,0:T(8,128)(2,1)S(1)} %bitcast.55, bf16[8,576,384]{2,1,0:T(8,128)(2,1)} %bitcast.66), custom_call_target="tpu_custom_call" | custom-call | tf_op jit(solution)/shard_map/time_attend/pallas_call | solution.py:394
  155.1 6.8 %all-to-all-start.4 = ((bf16[16,32,384]{2,1,0:T(8,128)(2,1)}), bf16[16,32,384]{2,1,0:T(8,128)(2,1)S(1)}, u32[]{:S(2)}, u32[]{:S(2)}) async-start(bf16[16,32,384]{2,1,0:T(8,128)(2,1)} %bitcast.36), calls=%async_computation.4 | async-start | bytes 786432 | tf_op jit(solution)/shard_map/all_to_all | solution.py:402
  162.0 1.0 copy.48
  163.0 7.3 %all-to-all-done.4 = bf16[16,32,384]{2,1,0:T(8,128)(2,1)S(1)} async-done(((bf16[16,32,384]{2,1,0:T(8,128)(2,1)}), bf16[16,32,384]{2,1,0:T(8,128)(2,1)S(1)}, u32[]{:S(2)}, u32[]{:S(2)}) %all-to-all-start.4) | async-done | bytes 393248 | tf_op jit(solution)/shard_map/all_to_all | solution.py:402
  (58 shorter events, 5.9 us)
Async XLA Ops:
  7.2 4.5 %copy-start = (bf16[96,2304]{1,0:T(8,128)(2,1)S(1)}, bf16[96,2304]{1,0:T(8,128)(2,1)}, u32[]{:S(2)}) copy-start(bf16[96,2304]{1,0:T(8,128)(2,1)} %param.14) | copy-start | bytes 1327108
  7.2 15.2 %copy-start.2 = (bf16[2,2,64,1536]{3,2,1,0:T(8,128)(2,1)S(1)}, bf16[2,2,64,1536]{3,2,1,0:T(8,128)(2,1)}, u32[]{:S(2)}) copy-start(bf16[2,2,64,1536]{3,2,1,0:T(8,128)(2,1)} %param.9) | copy-start | bytes 2359300
  7.2 16.6 %copy-start.4 = (f32[1536]{0:T(1024)S(1)}, f32[1536]{0:T(1024)}, u32[]{:S(2)}) copy-start(f32[1536]{0:T(1024)} %param.10) | copy-start | bytes 18436
  7.2 22.8 %collective-permute-start = (bf16[2,2,64,1536]{3,2,1,0:T(8,128)(2,1)}, bf16[2,2,64,1536]{3,2,1,0:T(8,128)(2,1)S(1)}, u32[]{:S(2)}, u32[]{:S(2)}) collective-permute-start(bf16[2,2,64,1536]{3,2,1,0:T(8,128)(2,1)} %param.9), channel_id=1, source_target_pairs={{0,1},{1,0},{2,3},{3,2},{4,5},{5,4},{6,7},{7,6},{8,9},{9,8},{10,11... | collective-permute-start | bytes 2359304 | tf_op jit(solution)/shard_map/ppermute | solution.py:281
  14.0 26.6 %all-to-all-start = ((bf16[16,48,384]{2,1,0:T(8,128)(2,1)}), bf16[16,48,384]{2,1,0:T(8,128)(2,1)S(1)}, u32[]{:S(2)}, u32[]{:S(2)}) async-start(bf16[16,48,384]{2,1,0:T(8,128)(2,1)} %bitcast.8), calls=%async_computation | async-start | bytes 1179648 | tf_op jit(solution)/shard_map/all_to_all | solution.py:280
  22.3 68.5 %all-gather.5.cloned.1.call-start = ((), (), s32[]{:S(2)}) async-start(), calls=%async_computation.5 | async-start | bytes 6266880 | tf_op jit(solution)/shard_map/all_gather | solution.py:323
  22.4 2.7 %collective-permute-start.1 = (bf16[4,32,1536]{2,1,0:T(8,128)(2,1)S(1)}, bf16[4,32,1536]{2,1,0:T(8,128)(2,1)S(1)}, u32[]{:S(2)}, u32[]{:S(2)}) collective-permute-start(bf16[4,32,1536]{2,1,0:T(8,128)(2,1)S(1)} %dynamic-slice_bitcast_fusion.2), channel_id=1, source_target_pairs={{0,16},{16,0},{1,17},{17,1},{2,18},{18,2},{3,19},{19,3},{4,20},{20... | collective-permute-start | bytes 1179656 | tf_op jit(solution)/shard_map/ppermute | solution.py:284
  30.1 1.8 %collective-permute-start.2 = (bf16[4,32,1536]{2,1,0:T(8,128)(2,1)S(1)}, bf16[4,32,1536]{2,1,0:T(8,128)(2,1)S(1)}, u32[]{:S(2)}, u32[]{:S(2)}) collective-permute-start(bf16[4,32,1536]{2,1,0:T(8,128)(2,1)S(1)} %dynamic-slice_bitcast_fusion.1), channel_id=1, source_target_pairs={{0,16},{16,0},{1,17},{17,1},{2,18},{18,2},{3,19},{19,3},{4,20},{20... | collective-permute-start | bytes 1179656 | tf_op jit(solution)/shard_map/ppermute | solution.py:284
  42.0 47.3 %all-to-all-start.1 = ((bf16[8,64,1536]{2,1,0:T(8,128)(2,1)}), bf16[8,64,1536]{2,1,0:T(8,128)(2,1)S(1)}, u32[]{:S(2)}, u32[]{:S(2)}) async-start(bf16[8,64,1536]{2,1,0:T(8,128)(2,1)} %bitcast.23), calls=%async_computation.1 | async-start | bytes 3145728 | tf_op jit(solution)/shard_map/all_to_all | solution.py:333
  51.0 86.1 %all-gather.7.cloned.1.call-start = ((), (), s32[]{:S(2)}) async-start(), calls=%async_computation.6 | async-start | bytes 3981312 | tf_op jit(solution)/shard_map/all_gather | solution.py:335
  51.2 8.8 %collective-permute-start.3 = (bf16[3,1,96,384]{3,2,0,1:T(8,128)(2,1)S(1)}, bf16[3,1,96,384]{3,2,0,1:T(8,128)(2,1)S(1)}, u32[]{:S(2)}, u32[]{:S(2)}) collective-permute-start(bf16[3,1,96,384]{3,2,0,1:T(8,128)(2,1)S(1)} %reshape.127), channel_id=1, source_target_pairs={{0,1},{1,0},{2,3},{3,2},{4,5},{5,4},{6,7},{7,6},{8,9},{9,8},{10,11... | collective-permute-start | bytes 663560 | tf_op jit(solution)/shard_map/ppermute | solution.py:322
  95.0 15.4 %copy-start.3 = (f32[1536]{0:T(1024)S(1)}, f32[1536]{0:T(1024)}, u32[]{:S(2)}) copy-start(f32[1536]{0:T(1024)} %param.13) | copy-start | bytes 18436
  95.1 3.3 %collective-permute-start.4 = (bf16[2,512,384]{2,1,0:T(8,128)(2,1)S(1)}, bf16[2,512,384]{2,1,0:T(8,128)(2,1)S(1)}, u32[]{:S(2)}, u32[]{:S(2)}) collective-permute-start(bf16[2,512,384]{2,1,0:T(8,128)(2,1)S(1)} %get-tuple-element.27.kv_ref), channel_id=1, source_target_pairs={{0,16},{16,0},{1,17},{17,1},{2,18},{18,2},{3,19},{19,3},{4,20},{20... | collective-permute-start | bytes 2359304 | tf_op jit(solution)/shard_map/ppermute | solution.py:344
  102.6 20.5 %all-to-all-start.2 = ((bf16[16,32,384]{2,1,0:T(8,128)(2,1)}), bf16[16,32,384]{2,1,0:T(8,128)(2,1)S(1)}, u32[]{:S(2)}, u32[]{:S(2)}) async-start(bf16[16,32,384]{2,1,0:T(8,128)(2,1)} %bitcast.26), calls=%async_computation.2 | async-start | bytes 786432 | tf_op jit(solution)/shard_map/all_to_all | solution.py:366
  126.4 1.2 copy-start.1
  127.6 21.8 %all-to-all-start.3 = ((bf16[8,64,1536]{2,1,0:T(8,128)(2,1)}), bf16[8,64,1536]{2,1,0:T(8,128)(2,1)S(1)}, u32[]{:S(2)}, u32[]{:S(2)}) async-start(bf16[8,64,1536]{2,1,0:T(8,128)(2,1)} %bitcast.56), calls=%async_computation.3 | async-start | bytes 3145728 | tf_op jit(solution)/shard_map/all_to_all | solution.py:393
  133.9 28.0 %collective-permute-start.5 = (bf16[4,32,1536]{2,1,0:T(8,128)(2,1)S(1)}, bf16[4,32,1536]{2,1,0:T(8,128)(2,1)S(1)}, u32[]{:S(2)}, u32[]{:S(2)}) collective-permute-start(bf16[4,32,1536]{2,1,0:T(8,128)(2,1)S(1)} %get-tuple-element.37), channel_id=1, source_target_pairs={{0,16},{16,0},{1,17},{17,1},{2,18},{18,2},{3,19},{19,3},{4,20},{20... | collective-permute-start | bytes 1179656 | tf_op jit(solution)/shard_map/ppermute | solution.py:390
  155.1 15.2 %all-to-all-start.4 = ((bf16[16,32,384]{2,1,0:T(8,128)(2,1)}), bf16[16,32,384]{2,1,0:T(8,128)(2,1)S(1)}, u32[]{:S(2)}, u32[]{:S(2)}) async-start(bf16[16,32,384]{2,1,0:T(8,128)(2,1)} %bitcast.36), calls=%async_computation.4 | async-start | bytes 786432 | tf_op jit(solution)/shard_map/all_to_all | solution.py:402
Sparse Core Ops, SparseCore 0:
  42.1 48.6 all-gather.4
  93.2 31.9 all-gather.6

commit v5 on v4

--- a/solution.py
+++ b/solution.py
@@ -42,6 +42,26 @@
     for copy in copies:
         copy.start()
     return copies
+
+
+def chunk_kernel(tm_ref, wq_ref, wo_ref, wt_ref, out_ref):
+    tm = tm_ref[0]
+    half = pl.multiple_of(tm // 8 * HALF, HALF)
+    for h in range(2):
+        pieces = [(wo_ref[:, cb * HALF : (cb + 1) * HALF], 3 * cb, 3, tm * 3) for cb in range(4)]
+        for kind in range(3):
+            first = kind * INNER + h * HALF
+            pieces.append((wq_ref[:, first : first + HALF], 12 + 6 * kind, 6, tm * 6))
+            lanes = pl.ds(pl.multiple_of(kind * INNER + half, HALF), HALF)
+            pieces.append((wt_ref[:, lanes], 30 + 6 * kind, 6, tm % 8 * 12 + h * 6))
+        total = jnp.zeros((48, HALF), F32)
+        for block, place, count, source in pieces:
+            row = lax.broadcasted_iota(jnp.int32, (48, block.shape[0]), 0) - place
+            column = lax.broadcasted_iota(jnp.int32, (48, block.shape[0]), 1) - source
+            picked = (row == column) & (row >= 0) & (row < count)
+            total += dot(picked.astype(BF16), block)
+        for z in range(8):
+            out_ref[z, h] = total.astype(BF16)
 
 
 def gather_frames(core, block_ref, moved_ref, frames_vmem):
@@ -72,30 +92,34 @@
 
 def other_kernel(
     core_ref, xh_ref, block_ref, moved_ref, gain_ref, own_ref, order_ref,
-    out_ref, frames_vmem, own_vmem, order_vmem, sems,
+    out_ref, frames_vmem, order_vmem, sems,
 ):
-    copies = fetch([(order_ref, order_vmem), (own_ref, own_vmem)], sems)
     xh = xh_ref[0]
+    pairs = [
+        (order_ref.at[:, pl.ds(cb * HALF, HALF)], order_vmem.at[cb]) for cb in range(4)
+    ]
+    copies = fetch(pairs + [(own_ref, out_ref.at[:, pl.ds(xh, 1)])], sems)
     gather_frames(core_ref[0], block_ref, moved_ref, frames_vmem)
     normed = normalize(frames_vmem, gain_ref)
-    copies[0].wait()
-    other = dot(normed, order_vmem[...]).astype(BF16)
-    out_ref[:, pl.ds(1 - xh, 1)] = other.reshape(8, 1, 32, WIDTH)
-    copies[1].wait()
-    out_ref[:, pl.ds(xh, 1)] = own_vmem[...]
-
-
-def project_kernel(x_ref, w_ref, q_ref, kv_ref, w_vmem, sems):
+    for cb in range(4):
+        copies[cb].wait()
+        other = dot(normed, order_vmem[cb]).astype(BF16).reshape(8, 1, 32, HALF)
+        out_ref[:, pl.ds(1 - xh, 1), :, cb * HALF : (cb + 1) * HALF] = other
+    copies[4].wait()
+
+
+def keys_values_kernel(x_ref, w_ref, kv_ref, w_vmem, sems):
     copies = fetch(
-        [(w_ref.at[:, pl.ds(192 + 96 * i, 96)], w_vmem.at[i]) for i in range(3)], sems
-    )
-    for copy, i in zip(copies, range(3)):
-        copy.wait()
-        projected = dot(x_ref[...], w_vmem[i].reshape(WIDTH, HALF)).astype(BF16)
-        if i == 0:
-            q_ref[...] = projected
-        else:
-            kv_ref[i - 1] = projected
+        [(w_ref.at[:, pl.ds(192 + 96 * i, 96)], w_vmem.at[i - 1]) for i in (1, 2)], sems
+    )
+    for i in range(2):
+        copies[i].wait()
+        kv_ref[i] = dot(x_ref[...], w_vmem[i].reshape(WIDTH, HALF)).astype(BF16)
+
+
+def queries_kernel(x_ref, w_ref, q_ref, w_vmem, sems):
+    fetch([(w_ref.at[:, pl.ds(192, 96)], w_vmem)], sems)[0].wait()
+    q_ref[...] = dot(x_ref[...], w_vmem[...].reshape(WIDTH, HALF)).astype(BF16)
 
 
 def attend(queries, keys, values, mask=None):
@@ -167,7 +191,9 @@
     fetch([(out_vmem, out_ref)], sems.at[pl.ds(2, 1)])[0].wait()
 
 
-def output_kernel(ctx_ref, tok_ref, w_ref, gain_ref, out_ref, w_vmem, tok_vmem, sems):
+def output_kernel(
+    ctx_ref, tok_ref, w_ref, gain_ref, out_ref, w_vmem, tok_vmem, out_vmem, sems
+):
     copies = fetch(
         [(w_ref.at[cb], w_vmem.at[cb]) for cb in range(4)] + [(tok_ref, tok_vmem)], sems
     )
@@ -191,9 +217,12 @@
     for cb, mix in enumerate(mixed):
         lanes = slice(cb * HALF, (cb + 1) * HALF)
         normed = (mix * factor * gain_ref[:, lanes]).astype(BF16)
-        normed = dot(swap, normed).astype(BF16)
-        out_ref[0, :, lanes] = normed
-        out_ref[1, :, lanes] = normed
+        out_vmem[cb] = dot(swap, normed).astype(BF16)
+        for i in range(2):
+            place = out_ref.at[i, :, pl.ds(cb * HALF, HALF)]
+            copies += fetch([(out_vmem.at[cb], place)], sems.at[pl.ds(5 + 2 * cb + i, 1)])
+    for copy in copies[5:]:
+        copy.wait()
 
 
 def branch_kernel(ctx_ref, w_ref, out_ref, w_vmem, sems):
@@ -267,16 +296,16 @@
     inner_order = jnp.asarray(one_hot((16, 16, 3), (1, 0, 2)))
     time_order = jnp.asarray(one_hot((16, 4, 2, 2, 6), (1, 2, 3, 0, 4)))
 
-    wq = lax.dynamic_slice_in_dim(spatial_project, tm * 6, 6, 0)
-    wq = wq.reshape(6, 3, 2, HALF).transpose(2, 1, 0, 3).reshape(2, 18, HALF)
-    wo = lax.dynamic_slice_in_dim(spatial_output, tm * 3, 3, 0)
-    wo = wo.reshape(3, 4, HALF).transpose(1, 0, 2).reshape(12, HALF)
-    row = lax.axis_index(TM[1:]) * 12
-    wt = lax.dynamic_slice_in_dim(temporal_project, row, 12, 0).reshape(2, 6, 3, 2, HALF)
-    wt = lax.dynamic_index_in_dim(wt, x_lo, 3, keepdims=False)
-    wt = wt.transpose(0, 2, 1, 3).reshape(2, 18, HALF)
-    chunk = jnp.stack([jnp.concatenate([wo, wq[i], wt[i]], 0) for i in range(2)])
-    chunk = jnp.broadcast_to(chunk[None], (8, 2, 48, HALF)).reshape(16, 48, HALF)
+    (chunk,) = call(
+        chunk_kernel,
+        "weight_rows",
+        [SMEM] + [VMEM] * 3,
+        [(pltpu.VMEM, (8, 2, 48, HALF))],
+        [],
+        0,
+        12,
+    )(tm.reshape(1).astype(jnp.int32), spatial_project, spatial_output, temporal_project)
+    chunk = chunk.reshape(16, 48, HALF)
     got = lax.all_to_all(chunk, DP, 0, 0, tiled=True)
     across = lax.ppermute(tokens, "x_hi", swap)
 
@@ -306,8 +335,8 @@
         "space_norm_other",
         [SMEM] * 2 + [VMEM] * 3 + [HBM] * 2,
         [(pltpu.VMEM, (8, 2, 32, WIDTH))],
-        [vmem(8, 32, WIDTH), vmem(8, 1, 32, WIDTH), vmem(WIDTH, WIDTH)],
-        2,
+        [vmem(8, 32, WIDTH), vmem(4, WIDTH, HALF)],
+        5,
         20,
     )(core_id, xh_id, halves, moved(halves), gain, hbm(own), hbm(space_order))
     got, normed = lax.optimization_barrier((got, normed))
@@ -333,15 +362,27 @@
     frame = lax.all_to_all(normed.reshape(8, 64, WIDTH), "z", 0, 0, tiled=True)
     w2, frame, tokens_time = lax.optimization_barrier((w2, frame, tokens_time))
     w2 = lax.all_gather(w2, TM[1:], axis=0, tiled=False)
-    q, kv = call(
-        project_kernel,
-        "space_project",
+    frame = frame.reshape(512, WIDTH)
+    (kv,) = call(
+        keys_values_kernel,
+        "space_keys_values",
         [VMEM, HBM],
-        [(pltpu.VMEM, (512, HALF)), (pltpu.VMEM, (2, 512, HALF))],
-        [vmem(3, 16, 96, HALF)],
-        3,
-    )(frame.reshape(512, WIDTH), hbm(w1))
+        [(pltpu.VMEM, (2, 512, HALF))],
+        [vmem(2, 16, 96, HALF)],
+        2,
+        24,
+    )(frame, hbm(w1))
     kvo = lax.ppermute(kv, "core", swap)
+    frame, kv = lax.optimization_barrier((frame, kv))
+    (q,) = call(
+        queries_kernel,
+        "space_queries",
+        [VMEM, HBM],
+        [(pltpu.VMEM, (512, HALF))],
+        [vmem(16, 96, HALF)],
+        1,
+        16,
+    )(frame, hbm(w1))
     (ctx,) = call(spatial_kernel, "space_attend", [VMEM] * 3, [(pltpu.VMEM, (2, 8, 32, HALF))], [], 0, 20)(
         q, kv, kvo
     )
@@ -369,9 +410,9 @@
         output_kernel,
         "space_output",
         [VMEM, HBM, HBM, VMEM],
-        [(pltpu.VMEM, (2, 256, WIDTH))],
-        [vmem(4, INNER, HALF), vmem(256, WIDTH)],
-        5,
+        [(pltpu.HBM, (2, 256, WIDTH))],
+        [vmem(4, INNER, HALF), vmem(256, WIDTH), vmem(4, 256, HALF)],
+        13,
         20,
     )(ctx, hbm(tokens_time), hbm(mixed), gain)
     ctx, normed_time = lax.optimization_barrier((ctx, normed_time))

time: 179 us -> 176 us (0.983)
  Pallas kernels: 45.6 us -> 49 us
  starting transfers between devices: 49.1 us -> 46.2 us
    pallas_call x2 -> x4, Pallas kernels: 7.6 us -> 11.2 us  [the longest x1 4.42 us: per_device(): call(output_kernel, 'space_output', [VMEM, HBM, HBM, VMEM], [(pltpu.HBM,...]
    all_to_all x1, starting transfers between devices: 8.99 us -> 5.52 us  [per_device(): frame = lax.all_to_all(normed.reshape(8, 64, WIDTH), 'z', 0, 0, tiled=True)]
    ppermute x1, waiting for transfers between devices: 1.91 us -> 0.01 us  [per_device(): kvo = lax.ppermute(kv, 'core', swap)]
    dynamic_slice x5 -> x0, local copies, waits for them, and re-layouts: 1.85 us -> none  [the longest x1 0.91 us: per_device(): wq = lax.dynamic_slice_in_dim(spatial_project, tm * 6, 6, 0)]
  transfers between devices with their start and end apart: 13 -> 13, of which waited for: 10 -> 9; matrix products, arithmetic and copies ran while one was open for 3% -> 2% of each run, Pallas kernels for 26% -> 28%
where the time goes in v5:
time: 176 us
  waiting for transfers between devices  58.3 us (33%)
  Pallas kernels  49 us (28%)
  starting transfers between devices  46.2 us (26%)
  between operations  14.3 us (8%)
  local copies, waits for them, and re-layouts  6.71 us (4%)
    all_to_all x1, waiting for transfers between devices, per_device(): frame = lax.all_to_all(normed.reshape(8, 64, WIDTH), 'z', 0, 0, tiled=True)  27.4 us
    all_to_all x1, waiting for transfers between devices, per_device(): lax.all_to_all(normed_time.reshape(8, 64, WIDTH), TM[:2], 0, 0, tiled=True)  12.6 us
    pallas_call x1, Pallas kernels, per_device(): call(weights_kernel, 'output_weights', [HBM] * 3, [(pltpu.HBM, (INNER, WI...  10.6 us
    all_to_all x1, starting transfers between devices, per_device(): ctx = lax.all_to_all(ctx.reshape(16, 32, HALF), DP[::-1], 0, 0, tiled=True)  8.58 us
    all_to_all x1, starting transfers between devices, per_device(): got = lax.all_to_all(chunk, DP, 0, 0, tiled=True)  8.29 us
    all_to_all x1, waiting for transfers between devices, per_device(): lax.all_to_all(context.reshape(16, 32, HALF), TM, 0, 0, tiled=True)  7.29 us
    all_to_all x1, starting transfers between devices, per_device(): lax.all_to_all(context.reshape(16, 32, HALF), TM, 0, 0, tiled=True)  6.58 us
    pallas_call x1, Pallas kernels, per_device(): call(temporal_kernel, 'time_attend', [VMEM, HBM], [(pltpu.VMEM, (16, 2, 1...  5.76 us
  transfers between devices with their start and end apart: 13, of which 9 were waited for; matrix products, arithmetic and copies ran while one was open for 2% of the time, Pallas kernels for 28%

profile of v5, /device:TPU:1, one launch (start us, length us, event | category | flops | bytes accessed | tf_op | source)
XLA Modules:
  0.0 175.6 jit_solution(17830707251170944574)
XLA Ops:
  7.2 3.7 %collective-permute-start = (bf16[2,2,64,1536]{3,2,1,0:T(8,128)(2,1)}, bf16[2,2,64,1536]{3,2,1,0:T(8,128)(2,1)S(1)}, u32[]{:S(2)}, u32[]{:S(2)}) collective-permute-start(bf16[2,2,64,1536]{3,2,1,0:T(8,128)(2,1)} %param.9), channel_id=1, source_target_pairs={{0,1},{1,0},{2,3},{3,2},{4,5},{5,4},{6,7},{7,6},{8,9},{9,8},{10,11... | collective-permute-start | bytes 2359304 | tf_op jit(solution)/shard_map/ppermute | solution.py:310
  10.8 1.0 copy-done.1
  11.9 1.0 copy-done.2
  12.9 0.9 copy-done.3
  13.8 1.2 weight_rows.1
  15.0 8.3 %all-to-all-start = ((bf16[16,48,384]{2,1,0:T(8,128)(2,1)}), bf16[16,48,384]{2,1,0:T(8,128)(2,1)S(1)}, u32[]{:S(2)}, u32[]{:S(2)}) async-start(bf16[16,48,384]{2,1,0:T(8,128)(2,1)} %bitcast.1), calls=%async_computation | async-start | bytes 1179648 | tf_op jit(solution)/shard_map/all_to_all | solution.py:309
  23.4 1.3 collective-permute-start.1
  24.8 1.3 collective-permute-done.1.moved_ref
  26.1 4.9 %space_norm_own.1 = (bf16[8,32,1536]{2,1,0:T(8,128)(2,1)}, bf16[8,1,32,1536]{3,2,1,0:T(8,128)(2,1)}) custom-call(s32[1]{0:T(128)} %bitcast.2.core_ref, bf16[4,2,32,1536]{3,2,1,0:T(8,128)(2,1)S(1)} %bitcast.49, bf16[4,32,1536]{2,1,0:T(8,128)(2,1)S(1)} %collective-permute-done.1.moved_ref, f32[1,1536]{1,0:T(1,128)S(1)} %reshape.97.gain_ref, ...), custom_call_target="tpu_custom_call" | custom-call | flops 1 | bytes 1 | tf_op jit(solution)/shard_map/space_norm_own/pallas_call | solution.py:321
  31.6 1.3 collective-permute-done.2.moved_ref
  32.9 4.8 %space_norm_other.1 = bf16[8,2,32,1536]{3,2,1,0:T(8,128)(2,1)} custom-call(s32[1]{0:T(128)} %bitcast.2.core_ref, s32[1]{0:T(128)} %bitcast.3.xh_ref, bf16[4,2,32,1536]{3,2,1,0:T(8,128)(2,1)S(1)} %bitcast.51, bf16[4,32,1536]{2,1,0:T(8,128)(2,1)S(1)} %collective-permute-done.2.moved_ref, f32[1,1536]{1,0:T(1,128)S(1)} %reshape.97.gain_ref, ...), custom_call_target="tpu_custom_call" | custom-call | tf_op jit(solution)/shard_map/space_norm_other/pallas_call | solution.py:333
  37.7 3.9 %all-to-all-done = bf16[16,48,384]{2,1,0:T(8,128)(2,1)S(1)} async-done(((bf16[16,48,384]{2,1,0:T(8,128)(2,1)}), bf16[16,48,384]{2,1,0:T(8,128)(2,1)S(1)}, u32[]{:S(2)}, u32[]{:S(2)}) %all-to-all-start) | async-done | bytes 589856 | tf_op jit(solution)/shard_map/all_to_all | solution.py:309
  43.0 5.5 %all-to-all-start.1 = ((bf16[8,64,1536]{2,1,0:T(8,128)(2,1)}), bf16[8,64,1536]{2,1,0:T(8,128)(2,1)S(1)}, u32[]{:S(2)}, u32[]{:S(2)}) async-start(bf16[8,64,1536]{2,1,0:T(8,128)(2,1)} %bitcast.16), calls=%async_computation.1 | async-start | bytes 3145728 | tf_op jit(solution)/shard_map/all_to_all | solution.py:362
  48.7 4.6 %collective-permute-start.3 = (bf16[3,1,96,384]{3,2,0,1:T(8,128)(2,1)S(1)}, bf16[3,1,96,384]{3,2,0,1:T(8,128)(2,1)S(1)}, u32[]{:S(2)}, u32[]{:S(2)}) collective-permute-start(bf16[3,1,96,384]{3,2,0,1:T(8,128)(2,1)S(1)} %reshape.104), channel_id=1, source_target_pairs={{0,1},{1,0},{2,3},{3,2},{4,5},{5,4},{6,7},{7,6},{8,9},{9,8},{10,11... | collective-permute-start | bytes 663560 | tf_op jit(solution)/shard_map/ppermute | solution.py:351
  53.3 4.9 %time_tokens.1.tok_ref = bf16[256,1536]{1,0:T(8,128)(2,1)} custom-call(bf16[256,1536]{1,0:T(8,128)(2,1)} %bitcast.61, bf16[1536,1536]{1,0:T(8,128)(2,1)} %constant.40.clone.order_ref.time_ref), custom_call_target="tpu_custom_call" | custom-call | tf_op jit(solution)/shard_map/time_tokens/pallas_call | solution.py:353
  59.3 27.4 %all-to-all-done.1 = bf16[8,64,1536]{2,1,0:T(8,128)(2,1)S(1)} async-done(((bf16[8,64,1536]{2,1,0:T(8,128)(2,1)}), bf16[8,64,1536]{2,1,0:T(8,128)(2,1)S(1)}, u32[]{:S(2)}, u32[]{:S(2)}) %all-to-all-start.1) | async-done | bytes 1572896 | tf_op jit(solution)/shard_map/all_to_all | solution.py:362
  86.8 2.5 %all-gather.5.cloned.1.call-done = bf16[7680,384]{1,0:T(8,128)(2,1)} async-done(((bf16[480,384]{1,0:T(8,128)(2,1)}), bf16[7680,384]{1,0:T(8,128)(2,1)}) %all-gather.5.cloned.1.call-update) | async-done | bytes 5898256 | tf_op jit(solution)/shard_map/all_gather | solution.py:352
  89.3 3.2 %space_keys_values.1.kv_ref = bf16[2,512,384]{2,1,0:T(8,128)(2,1)S(1)} custom-call(bf16[512,1536]{1,0:T(8,128)(2,1)S(1)} %bitcast.42, bf16[16,480,384]{2,1,0:T(8,128)(2,1)} %bitcast.52), custom_call_target="tpu_custom_call" | custom-call | tf_op jit(solution)/shard_map/space_keys_values/pallas_call | solution.py:366
  93.1 2.3 %space_queries.1.q_ref = bf16[512,384]{1,0:T(8,128)(2,1)S(1)} custom-call(bf16[512,1536]{1,0:T(8,128)(2,1)S(1)} %bitcast.43, bf16[16,480,384]{2,1,0:T(8,128)(2,1)} %bitcast.53), custom_call_target="tpu_custom_call" | custom-call | tf_op jit(solution)/shard_map/space_queries/pallas_call | solution.py:377
  95.3 4.2 %space_attend.1 = bf16[2,8,32,384]{3,2,1,0:T(8,128)(2,1)} custom-call(bf16[512,384]{1,0:T(8,128)(2,1)S(1)} %space_queries.1.q_ref, bf16[2,512,384]{2,1,0:T(8,128)(2,1)S(1)} %space_keys_values.1.kv_ref, bf16[2,512,384]{2,1,0:T(8,128)(2,1)S(1)} %collective-permute-done.4.kvo_ref), custom_call_target="tpu_custom_call" | custom-call | tf_op jit(solution)/shard_map/space_attend/pallas_call | solution.py:386
  99.5 8.6 %all-to-all-start.2 = ((bf16[16,32,384]{2,1,0:T(8,128)(2,1)}), bf16[16,32,384]{2,1,0:T(8,128)(2,1)S(1)}, u32[]{:S(2)}, u32[]{:S(2)}) async-start(bf16[16,32,384]{2,1,0:T(8,128)(2,1)} %bitcast.19), calls=%async_computation.2 | async-start | bytes 786432 | tf_op jit(solution)/shard_map/all_to_all | solution.py:407
  108.6 10.6 %output_weights.1 = (bf16[768,1536]{1,0:T(8,128)(2,1)}, bf16[4,768,384]{2,1,0:T(8,128)(2,1)}) custom-call(bf16[16,480,384]{2,1,0:T(8,128)(2,1)} %bitcast.54, bf16[768,768]{1,0:T(8,128)(2,1)} %constant.41.clone.inner_ref, bf16[1536,1536]{1,0:T(8,128)(2,1)} %constant.40.clone.order_ref.time_ref), custom_call_target="tpu_custom_call" | custom-call | flops 5400000000 | bytes 15000000 | tf_op jit(solution)/shard_map/output_weights/pallas_call | solution.py:390
  119.2 1.6 all-to-all-done.2
  120.8 4.4 %space_output.1 = bf16[2,256,1536]{2,1,0:T(8,128)(2,1)} custom-call(bf16[2,256,384]{2,1,0:T(8,128)(2,1)S(1)} %bitcast.45, bf16[256,1536]{1,0:T(8,128)(2,1)} %time_tokens.1.tok_ref, bf16[4,768,384]{2,1,0:T(8,128)(2,1)} %get-tuple-element.31.w_ref, f32[1,1536]{1,0:T(1,128)S(1)} %reshape.111.gain_ref), custom_call_target="tpu_custom_call" | custom-call | tf_op jit(solution)/shard_map/space_output/pallas_call | solution.py:409
  125.2 3.6 %all-to-all-start.3 = ((bf16[8,64,1536]{2,1,0:T(8,128)(2,1)}), bf16[8,64,1536]{2,1,0:T(8,128)(2,1)S(1)}, u32[]{:S(2)}, u32[]{:S(2)}) async-start(bf16[8,64,1536]{2,1,0:T(8,128)(2,1)} %bitcast.55), calls=%async_computation.3 | async-start | bytes 3145728 | tf_op jit(solution)/shard_map/all_to_all | solution.py:434
  128.8 2.7 %space_branch.1 = bf16[256,1536]{1,0:T(8,128)(2,1)S(1)} custom-call(bf16[2,256,384]{2,1,0:T(8,128)(2,1)S(1)} %bitcast.46, bf16[768,1536]{1,0:T(8,128)(2,1)} %get-tuple-element.33.w_ref), custom_call_target="tpu_custom_call" | custom-call | tf_op jit(solution)/shard_map/space_branch/pallas_call | solution.py:419
  131.6 3.0 %collective-permute-start.5 = (bf16[4,32,1536]{2,1,0:T(8,128)(2,1)S(1)}, bf16[4,32,1536]{2,1,0:T(8,128)(2,1)S(1)}, u32[]{:S(2)}, u32[]{:S(2)}) collective-permute-start(bf16[4,32,1536]{2,1,0:T(8,128)(2,1)S(1)} %get-tuple-element.37), channel_id=1, source_target_pairs={{0,16},{16,0},{1,17},{17,1},{2,18},{18,2},{3,19},{19,3},{4,20},{20... | collective-permute-start | bytes 1179656 | tf_op jit(solution)/shard_map/ppermute | solution.py:431
  134.6 12.6 %all-to-all-done.3 = bf16[8,64,1536]{2,1,0:T(8,128)(2,1)S(1)} async-done(((bf16[8,64,1536]{2,1,0:T(8,128)(2,1)}), bf16[8,64,1536]{2,1,0:T(8,128)(2,1)S(1)}, u32[]{:S(2)}, u32[]{:S(2)}) %all-to-all-start.3) | async-done | bytes 1572896 | tf_op jit(solution)/shard_map/all_to_all | solution.py:434
  147.2 5.8 %time_attend.1 = bf16[16,2,16,384]{3,2,1,0:T(8,128)(2,1)} custom-call(bf16[512,1536]{1,0:T(8,128)(2,1)S(1)} %bitcast.44, bf16[8,576,384]{2,1,0:T(8,128)(2,1)} %bitcast.56), custom_call_target="tpu_custom_call" | custom-call | tf_op jit(solution)/shard_map/time_attend/pallas_call | solution.py:435
  153.0 6.6 %all-to-all-start.4 = ((bf16[16,32,384]{2,1,0:T(8,128)(2,1)}), bf16[16,32,384]{2,1,0:T(8,128)(2,1)S(1)}, u32[]{:S(2)}, u32[]{:S(2)}) async-start(bf16[16,32,384]{2,1,0:T(8,128)(2,1)} %bitcast.29), calls=%async_computation.4 | async-start | bytes 786432 | tf_op jit(solution)/shard_map/all_to_all | solution.py:443
  159.7 1.0 copy.39
  160.6 7.3 %all-to-all-done.4 = bf16[16,32,384]{2,1,0:T(8,128)(2,1)S(1)} async-done(((bf16[16,32,384]{2,1,0:T(8,128)(2,1)}), bf16[16,32,384]{2,1,0:T(8,128)(2,1)S(1)}, u32[]{:S(2)}, u32[]{:S(2)}) %all-to-all-start.4) | async-done | bytes 393248 | tf_op jit(solution)/shard_map/all_to_all | solution.py:443
  (41 shorter events, 5.2 us)
Async XLA Ops:
  7.2 16.2 %copy-start = (bf16[2,2,64,1536]{3,2,1,0:T(8,128)(2,1)S(1)}, bf16[2,2,64,1536]{3,2,1,0:T(8,128)(2,1)}, u32[]{:S(2)}) copy-start(bf16[2,2,64,1536]{3,2,1,0:T(8,128)(2,1)} %param.9) | copy-start | bytes 2359300
  7.2 23.9 %collective-permute-start = (bf16[2,2,64,1536]{3,2,1,0:T(8,128)(2,1)}, bf16[2,2,64,1536]{3,2,1,0:T(8,128)(2,1)S(1)}, u32[]{:S(2)}, u32[]{:S(2)}) collective-permute-start(bf16[2,2,64,1536]{3,2,1,0:T(8,128)(2,1)} %param.9), channel_id=1, source_target_pairs={{0,1},{1,0},{2,3},{3,2},{4,5},{5,4},{6,7},{7,6},{8,9},{9,8},{10,11... | collective-permute-start | bytes 2359304 | tf_op jit(solution)/shard_map/ppermute | solution.py:310
  10.8 1.0 copy-start.1
  11.8 1.0 copy-start.2
  12.9 0.9 copy-start.3
  13.8 11.0 %copy-start.5 = (f32[1536]{0:T(1024)S(1)}, f32[1536]{0:T(1024)}, u32[]{:S(2)}) copy-start(f32[1536]{0:T(1024)} %param.10) | copy-start | bytes 18436
  15.0 26.6 %all-to-all-start = ((bf16[16,48,384]{2,1,0:T(8,128)(2,1)}), bf16[16,48,384]{2,1,0:T(8,128)(2,1)S(1)}, u32[]{:S(2)}, u32[]{:S(2)}) async-start(bf16[16,48,384]{2,1,0:T(8,128)(2,1)} %bitcast.1), calls=%async_computation | async-start | bytes 1179648 | tf_op jit(solution)/shard_map/all_to_all | solution.py:309
  23.3 65.9 %all-gather.5.cloned.1.call-start = ((), (), s32[]{:S(2)}) async-start(), calls=%async_computation.5 | async-start | bytes 6266880 | tf_op jit(solution)/shard_map/all_gather | solution.py:352
  23.4 2.7 %collective-permute-start.1 = (bf16[4,32,1536]{2,1,0:T(8,128)(2,1)S(1)}, bf16[4,32,1536]{2,1,0:T(8,128)(2,1)S(1)}, u32[]{:S(2)}, u32[]{:S(2)}) collective-permute-start(bf16[4,32,1536]{2,1,0:T(8,128)(2,1)S(1)} %dynamic-slice_bitcast_fusion.2), channel_id=1, source_target_pairs={{0,16},{16,0},{1,17},{17,1},{2,18},{18,2},{3,19},{19,3},{4,20},{20... | collective-permute-start | bytes 1179656 | tf_op jit(solution)/shard_map/ppermute | solution.py:313
  31.1 1.8 %collective-permute-start.2 = (bf16[4,32,1536]{2,1,0:T(8,128)(2,1)S(1)}, bf16[4,32,1536]{2,1,0:T(8,128)(2,1)S(1)}, u32[]{:S(2)}, u32[]{:S(2)}) collective-permute-start(bf16[4,32,1536]{2,1,0:T(8,128)(2,1)S(1)} %dynamic-slice_bitcast_fusion.1), channel_id=1, source_target_pairs={{0,16},{16,0},{1,17},{17,1},{2,18},{18,2},{3,19},{19,3},{4,20},{20... | collective-permute-start | bytes 1179656 | tf_op jit(solution)/shard_map/ppermute | solution.py:313
  43.0 43.8 %all-to-all-start.1 = ((bf16[8,64,1536]{2,1,0:T(8,128)(2,1)}), bf16[8,64,1536]{2,1,0:T(8,128)(2,1)S(1)}, u32[]{:S(2)}, u32[]{:S(2)}) async-start(bf16[8,64,1536]{2,1,0:T(8,128)(2,1)} %bitcast.16), calls=%async_computation.1 | async-start | bytes 3145728 | tf_op jit(solution)/shard_map/all_to_all | solution.py:362
  48.5 86.1 %all-gather.7.cloned.1.call-start = ((), (), s32[]{:S(2)}) async-start(), calls=%async_computation.6 | async-start | bytes 3981312 | tf_op jit(solution)/shard_map/all_gather | solution.py:364
  48.7 9.8 %collective-permute-start.3 = (bf16[3,1,96,384]{3,2,0,1:T(8,128)(2,1)S(1)}, bf16[3,1,96,384]{3,2,0,1:T(8,128)(2,1)S(1)}, u32[]{:S(2)}, u32[]{:S(2)}) collective-permute-start(bf16[3,1,96,384]{3,2,0,1:T(8,128)(2,1)S(1)} %reshape.104), channel_id=1, source_target_pairs={{0,1},{1,0},{2,3},{3,2},{4,5},{5,4},{6,7},{7,6},{8,9},{9,8},{10,11... | collective-permute-start | bytes 663560 | tf_op jit(solution)/shard_map/ppermute | solution.py:351
  92.5 2.8 %collective-permute-start.4 = (bf16[2,512,384]{2,1,0:T(8,128)(2,1)S(1)}, bf16[2,512,384]{2,1,0:T(8,128)(2,1)S(1)}, u32[]{:S(2)}, u32[]{:S(2)}) collective-permute-start(bf16[2,512,384]{2,1,0:T(8,128)(2,1)S(1)} %space_keys_values.1.kv_ref), channel_id=1, source_target_pairs={{0,16},{16,0},{1,17},{17,1},{2,18},{18,2},{3,19},{19,3},{4,20},{20... | collective-permute-start | bytes 2359304 | tf_op jit(solution)/shard_map/ppermute | solution.py:375
  95.3 12.8 %copy-start.4 = (f32[1536]{0:T(1024)S(1)}, f32[1536]{0:T(1024)}, u32[]{:S(2)}) copy-start(f32[1536]{0:T(1024)} %param.13) | copy-start | bytes 18436
  99.5 21.3 %all-to-all-start.2 = ((bf16[16,32,384]{2,1,0:T(8,128)(2,1)}), bf16[16,32,384]{2,1,0:T(8,128)(2,1)S(1)}, u32[]{:S(2)}, u32[]{:S(2)}) async-start(bf16[16,32,384]{2,1,0:T(8,128)(2,1)} %bitcast.19), calls=%async_computation.2 | async-start | bytes 786432 | tf_op jit(solution)/shard_map/all_to_all | solution.py:407
  125.2 22.0 %all-to-all-start.3 = ((bf16[8,64,1536]{2,1,0:T(8,128)(2,1)}), bf16[8,64,1536]{2,1,0:T(8,128)(2,1)S(1)}, u32[]{:S(2)}, u32[]{:S(2)}) async-start(bf16[8,64,1536]{2,1,0:T(8,128)(2,1)} %bitcast.55), calls=%async_computation.3 | async-start | bytes 3145728 | tf_op jit(solution)/shard_map/all_to_all | solution.py:434
  131.6 28.0 %collective-permute-start.5 = (bf16[4,32,1536]{2,1,0:T(8,128)(2,1)S(1)}, bf16[4,32,1536]{2,1,0:T(8,128)(2,1)S(1)}, u32[]{:S(2)}, u32[]{:S(2)}) collective-permute-start(bf16[4,32,1536]{2,1,0:T(8,128)(2,1)S(1)} %get-tuple-element.37), channel_id=1, source_target_pairs={{0,16},{16,0},{1,17},{17,1},{2,18},{18,2},{3,19},{19,3},{4,20},{20... | collective-permute-start | bytes 1179656 | tf_op jit(solution)/shard_map/ppermute | solution.py:431
  153.0 15.0 %all-to-all-start.4 = ((bf16[16,32,384]{2,1,0:T(8,128)(2,1)}), bf16[16,32,384]{2,1,0:T(8,128)(2,1)S(1)}, u32[]{:S(2)}, u32[]{:S(2)}) async-start(bf16[16,32,384]{2,1,0:T(8,128)(2,1)} %bitcast.29), calls=%async_computation.4 | async-start | bytes 786432 | tf_op jit(solution)/shard_map/all_to_all | solution.py:443
Sparse Core Ops, SparseCore 0:
  43.1 46.1 all-gather.4
  91.7 31.9 all-gather.6

commit v6 on v5

--- a/solution.py
+++ b/solution.py
@@ -19,6 +19,7 @@
 SCALE = math.log2(math.e) / math.sqrt(HSIZE)
 TM = ("x_lo", "y", "core")
 DP = ("z", "x_hi")
+PLANES = (0, 4, 2, 6, 1, 5, 3, 7)
 BF16 = jnp.bfloat16
 F32 = jnp.float32
 
@@ -152,9 +153,10 @@
         blocks = attend(q_ref[rows], (kv_ref[0], kvo_ref[0]), (kv_ref[1], kvo_ref[1]))
         for i, block in enumerate(blocks):
             block = block.astype(BF16).reshape(4, 2, 32, 128)
-            for xh in range(2):
-                z = slice(first // 64, first // 64 + 4)
-                out_ref[xh, z, :, i * 128 : (i + 1) * 128] = block[:, xh]
+            for k in range(4):
+                z = PLANES[first // 64 + k]
+                for xh in range(2):
+                    out_ref[xh, z, :, i * 128 : (i + 1) * 128] = block[k, xh]
 
 
 def weights_kernel(
@@ -191,6 +193,14 @@
     fetch([(out_vmem, out_ref)], sems.at[pl.ds(2, 1)])[0].wait()
 
 
+def join(ctx_ref):
+    rows = [
+        jnp.concatenate([ctx_ref[i, 32 * z : 32 * z + 32] for z in PLANES], axis=0)
+        for i in range(2)
+    ]
+    return jnp.concatenate(rows, axis=1)
+
+
 def output_kernel(
     ctx_ref, tok_ref, w_ref, gain_ref, out_ref, w_vmem, tok_vmem, out_vmem, sems
 ):
@@ -198,7 +208,7 @@
         [(w_ref.at[cb], w_vmem.at[cb]) for cb in range(4)] + [(tok_ref, tok_vmem)], sems
     )
     rows = tok_ref.shape[0]
-    ctx = jnp.concatenate([ctx_ref[0], ctx_ref[1]], axis=1)
+    ctx = join(ctx_ref)
     target = lax.broadcasted_iota(jnp.int32, (rows, rows), 0)
     source = (target % 64) // 8 * 32 + target // 64 * 8 + target % 8
     swap = (lax.broadcasted_iota(jnp.int32, (rows, rows), 1) == source).astype(BF16)
@@ -227,7 +237,7 @@
 
 def branch_kernel(ctx_ref, w_ref, out_ref, w_vmem, sems):
     copies = fetch([(w_ref, w_vmem)], sems)
-    ctx = jnp.concatenate([ctx_ref[0], ctx_ref[1]], axis=1)
+    ctx = join(ctx_ref)
     copies[0].wait()
     for cb in range(4):
         lanes = slice(cb * HALF, (cb + 1) * HALF)
@@ -359,7 +369,9 @@
         3,
         16,
     )(hbm(frames.reshape(256, WIDTH)), hbm(time_order))
-    frame = lax.all_to_all(normed.reshape(8, 64, WIDTH), "z", 0, 0, tiled=True)
+    frame = lax.all_to_all(
+        normed.reshape(8, 64, WIDTH), "z", 0, 0, axis_index_groups=[list(PLANES)], tiled=True
+    )
     w2, frame, tokens_time = lax.optimization_barrier((w2, frame, tokens_time))
     w2 = lax.all_gather(w2, TM[1:], axis=0, tiled=False)
     frame = frame.reshape(512, WIDTH)

time: 176 us -> 176 us (level)
  no operation moved by 1% of the time
where the time goes in v6:
time: 176 us
  waiting for transfers between devices  58.3 us (33%)
  Pallas kernels  49 us (28%)
  starting transfers between devices  46.2 us (26%)
  between operations  14.3 us (8%)
  local copies, waits for them, and re-layouts  6.71 us (4%)
    all_to_all x1, waiting for transfers between devices, per_device(): lax.all_to_all(normed.reshape(8, 64, WIDTH), 'z', 0, 0, axis_index_groups...  25.9 us
    all_to_all x1, waiting for transfers between devices, per_device(): lax.all_to_all(normed_time.reshape(8, 64, WIDTH), TM[:2], 0, 0, tiled=True)  12.6 us
    pallas_call x1, Pallas kernels, per_device(): call(weights_kernel, 'output_weights', [HBM] * 3, [(pltpu.HBM, (INNER, WI...  10.6 us
    all_to_all x1, starting transfers between devices, per_device(): ctx = lax.all_to_all(ctx.reshape(16, 32, HALF), DP[::-1], 0, 0, tiled=True)  8.58 us
    all_to_all x1, starting transfers between devices, per_device(): got = lax.all_to_all(chunk, DP, 0, 0, tiled=True)  8.29 us
    all_to_all x1, waiting for transfers between devices, per_device(): lax.all_to_all(context.reshape(16, 32, HALF), TM, 0, 0, tiled=True)  7.29 us
    all_to_all x1, starting transfers between devices, per_device(): lax.all_to_all(context.reshape(16, 32, HALF), TM, 0, 0, tiled=True)  6.58 us
    pallas_call x1, Pallas kernels, per_device(): call(temporal_kernel, 'time_attend', [VMEM, HBM], [(pltpu.VMEM, (16, 2, 1...  5.76 us
  transfers between devices with their start and end apart: 13, of which 9 were waited for; matrix products, arithmetic and copies ran while one was open for 2% of the time, Pallas kernels for 28%

profile of v6, /device:TPU:1, one launch (start us, length us, event | category | flops | bytes accessed | tf_op | source)
XLA Modules:
  0.0 175.6 jit_solution(1067549029527976613)
XLA Ops:
  7.2 3.7 %collective-permute-start = (bf16[2,2,64,1536]{3,2,1,0:T(8,128)(2,1)}, bf16[2,2,64,1536]{3,2,1,0:T(8,128)(2,1)S(1)}, u32[]{:S(2)}, u32[]{:S(2)}) collective-permute-start(bf16[2,2,64,1536]{3,2,1,0:T(8,128)(2,1)} %param.9), channel_id=1, source_target_pairs={{0,1},{1,0},{2,3},{3,2},{4,5},{5,4},{6,7},{7,6},{8,9},{9,8},{10,11... | collective-permute-start | bytes 2359304 | tf_op jit(solution)/shard_map/ppermute | solution.py:320
  10.8 1.0 copy-done.1
  11.9 1.0 copy-done.2
  12.9 0.9 copy-done.3
  13.8 1.2 weight_rows.1
  15.0 8.3 %all-to-all-start = ((bf16[16,48,384]{2,1,0:T(8,128)(2,1)}), bf16[16,48,384]{2,1,0:T(8,128)(2,1)S(1)}, u32[]{:S(2)}, u32[]{:S(2)}) async-start(bf16[16,48,384]{2,1,0:T(8,128)(2,1)} %bitcast.1), calls=%async_computation | async-start | bytes 1179648 | tf_op jit(solution)/shard_map/all_to_all | solution.py:319
  23.4 1.3 collective-permute-start.1
  24.8 1.3 collective-permute-done.1.moved_ref
  26.1 4.9 %space_norm_own.1 = (bf16[8,32,1536]{2,1,0:T(8,128)(2,1)}, bf16[8,1,32,1536]{3,2,1,0:T(8,128)(2,1)}) custom-call(s32[1]{0:T(128)} %bitcast.2.core_ref, bf16[4,2,32,1536]{3,2,1,0:T(8,128)(2,1)S(1)} %bitcast.49, bf16[4,32,1536]{2,1,0:T(8,128)(2,1)S(1)} %collective-permute-done.1.moved_ref, f32[1,1536]{1,0:T(1,128)S(1)} %reshape.97.gain_ref, ...), custom_call_target="tpu_custom_call" | custom-call | flops 1 | bytes 1 | tf_op jit(solution)/shard_map/space_norm_own/pallas_call | solution.py:331
  31.6 1.3 collective-permute-done.2.moved_ref
  32.9 4.8 %space_norm_other.1 = bf16[8,2,32,1536]{3,2,1,0:T(8,128)(2,1)} custom-call(s32[1]{0:T(128)} %bitcast.2.core_ref, s32[1]{0:T(128)} %bitcast.3.xh_ref, bf16[4,2,32,1536]{3,2,1,0:T(8,128)(2,1)S(1)} %bitcast.51, bf16[4,32,1536]{2,1,0:T(8,128)(2,1)S(1)} %collective-permute-done.2.moved_ref, f32[1,1536]{1,0:T(1,128)S(1)} %reshape.97.gain_ref, ...), custom_call_target="tpu_custom_call" | custom-call | tf_op jit(solution)/shard_map/space_norm_other/pallas_call | solution.py:343
  37.7 3.9 %all-to-all-done = bf16[16,48,384]{2,1,0:T(8,128)(2,1)S(1)} async-done(((bf16[16,48,384]{2,1,0:T(8,128)(2,1)}), bf16[16,48,384]{2,1,0:T(8,128)(2,1)S(1)}, u32[]{:S(2)}, u32[]{:S(2)}) %all-to-all-start) | async-done | bytes 589856 | tf_op jit(solution)/shard_map/all_to_all | solution.py:319
  43.0 5.5 %all-to-all-start.1 = ((bf16[8,64,1536]{2,1,0:T(8,128)(2,1)}), bf16[8,64,1536]{2,1,0:T(8,128)(2,1)S(1)}, u32[]{:S(2)}, u32[]{:S(2)}) async-start(bf16[8,64,1536]{2,1,0:T(8,128)(2,1)} %bitcast.16), calls=%async_computation.1 | async-start | bytes 3145728 | tf_op jit(solution)/shard_map/all_to_all | solution.py:372
  48.7 4.6 %collective-permute-start.3 = (bf16[3,1,96,384]{3,2,0,1:T(8,128)(2,1)S(1)}, bf16[3,1,96,384]{3,2,0,1:T(8,128)(2,1)S(1)}, u32[]{:S(2)}, u32[]{:S(2)}) collective-permute-start(bf16[3,1,96,384]{3,2,0,1:T(8,128)(2,1)S(1)} %reshape.104), channel_id=1, source_target_pairs={{0,1},{1,0},{2,3},{3,2},{4,5},{5,4},{6,7},{7,6},{8,9},{9,8},{10,11... | collective-permute-start | bytes 663560 | tf_op jit(solution)/shard_map/ppermute | solution.py:361
  53.3 4.9 %time_tokens.1.tok_ref = bf16[256,1536]{1,0:T(8,128)(2,1)} custom-call(bf16[256,1536]{1,0:T(8,128)(2,1)} %bitcast.61, bf16[1536,1536]{1,0:T(8,128)(2,1)} %constant.40.clone.order_ref.time_ref), custom_call_target="tpu_custom_call" | custom-call | tf_op jit(solution)/shard_map/time_tokens/pallas_call | solution.py:363
  59.3 25.9 %all-to-all-done.1 = bf16[8,64,1536]{2,1,0:T(8,128)(2,1)S(1)} async-done(((bf16[8,64,1536]{2,1,0:T(8,128)(2,1)}), bf16[8,64,1536]{2,1,0:T(8,128)(2,1)S(1)}, u32[]{:S(2)}, u32[]{:S(2)}) %all-to-all-start.1) | async-done | bytes 1572896 | tf_op jit(solution)/shard_map/all_to_all | solution.py:372
  85.3 4.0 %all-gather.5.cloned.1.call-done = bf16[7680,384]{1,0:T(8,128)(2,1)} async-done(((bf16[480,384]{1,0:T(8,128)(2,1)}), bf16[7680,384]{1,0:T(8,128)(2,1)}) %all-gather.5.cloned.1.call-update) | async-done | bytes 5898256 | tf_op jit(solution)/shard_map/all_gather | solution.py:362
  89.3 3.2 %space_keys_values.1.kv_ref = bf16[2,512,384]{2,1,0:T(8,128)(2,1)S(1)} custom-call(bf16[512,1536]{1,0:T(8,128)(2,1)S(1)} %bitcast.42, bf16[16,480,384]{2,1,0:T(8,128)(2,1)} %bitcast.52), custom_call_target="tpu_custom_call" | custom-call | tf_op jit(solution)/shard_map/space_keys_values/pallas_call | solution.py:378
  93.1 2.3 %space_queries.1.q_ref = bf16[512,384]{1,0:T(8,128)(2,1)S(1)} custom-call(bf16[512,1536]{1,0:T(8,128)(2,1)S(1)} %bitcast.43, bf16[16,480,384]{2,1,0:T(8,128)(2,1)} %bitcast.53), custom_call_target="tpu_custom_call" | custom-call | tf_op jit(solution)/shard_map/space_queries/pallas_call | solution.py:389
  95.3 4.2 %space_attend.1 = bf16[2,8,32,384]{3,2,1,0:T(8,128)(2,1)} custom-call(bf16[512,384]{1,0:T(8,128)(2,1)S(1)} %space_queries.1.q_ref, bf16[2,512,384]{2,1,0:T(8,128)(2,1)S(1)} %space_keys_values.1.kv_ref, bf16[2,512,384]{2,1,0:T(8,128)(2,1)S(1)} %collective-permute-done.4.kvo_ref), custom_call_target="tpu_custom_call" | custom-call | tf_op jit(solution)/shard_map/space_attend/pallas_call | solution.py:398
  99.5 8.6 %all-to-all-start.2 = ((bf16[16,32,384]{2,1,0:T(8,128)(2,1)}), bf16[16,32,384]{2,1,0:T(8,128)(2,1)S(1)}, u32[]{:S(2)}, u32[]{:S(2)}) async-start(bf16[16,32,384]{2,1,0:T(8,128)(2,1)} %bitcast.19), calls=%async_computation.2 | async-start | bytes 786432 | tf_op jit(solution)/shard_map/all_to_all | solution.py:419
  108.6 10.6 %output_weights.1 = (bf16[768,1536]{1,0:T(8,128)(2,1)}, bf16[4,768,384]{2,1,0:T(8,128)(2,1)}) custom-call(bf16[16,480,384]{2,1,0:T(8,128)(2,1)} %bitcast.54, bf16[768,768]{1,0:T(8,128)(2,1)} %constant.41.clone.inner_ref, bf16[1536,1536]{1,0:T(8,128)(2,1)} %constant.40.clone.order_ref.time_ref), custom_call_target="tpu_custom_call" | custom-call | flops 5400000000 | bytes 15000000 | tf_op jit(solution)/shard_map/output_weights/pallas_call | solution.py:402
  119.2 1.6 all-to-all-done.2
  120.8 4.4 %space_output.1 = bf16[2,256,1536]{2,1,0:T(8,128)(2,1)} custom-call(bf16[2,256,384]{2,1,0:T(8,128)(2,1)S(1)} %bitcast.45, bf16[256,1536]{1,0:T(8,128)(2,1)} %time_tokens.1.tok_ref, bf16[4,768,384]{2,1,0:T(8,128)(2,1)} %get-tuple-element.31.w_ref, f32[1,1536]{1,0:T(1,128)S(1)} %reshape.111.gain_ref), custom_call_target="tpu_custom_call" | custom-call | tf_op jit(solution)/shard_map/space_output/pallas_call | solution.py:421
  125.2 3.6 %all-to-all-start.3 = ((bf16[8,64,1536]{2,1,0:T(8,128)(2,1)}), bf16[8,64,1536]{2,1,0:T(8,128)(2,1)S(1)}, u32[]{:S(2)}, u32[]{:S(2)}) async-start(bf16[8,64,1536]{2,1,0:T(8,128)(2,1)} %bitcast.55), calls=%async_computation.3 | async-start | bytes 3145728 | tf_op jit(solution)/shard_map/all_to_all | solution.py:446
  128.8 2.7 %space_branch.1 = bf16[256,1536]{1,0:T(8,128)(2,1)S(1)} custom-call(bf16[2,256,384]{2,1,0:T(8,128)(2,1)S(1)} %bitcast.46, bf16[768,1536]{1,0:T(8,128)(2,1)} %get-tuple-element.33.w_ref), custom_call_target="tpu_custom_call" | custom-call | tf_op jit(solution)/shard_map/space_branch/pallas_call | solution.py:431
  131.6 3.0 %collective-permute-start.5 = (bf16[4,32,1536]{2,1,0:T(8,128)(2,1)S(1)}, bf16[4,32,1536]{2,1,0:T(8,128)(2,1)S(1)}, u32[]{:S(2)}, u32[]{:S(2)}) collective-permute-start(bf16[4,32,1536]{2,1,0:T(8,128)(2,1)S(1)} %get-tuple-element.37), channel_id=1, source_target_pairs={{0,16},{16,0},{1,17},{17,1},{2,18},{18,2},{3,19},{19,3},{4,20},{20... | collective-permute-start | bytes 1179656 | tf_op jit(solution)/shard_map/ppermute | solution.py:443
  134.6 12.6 %all-to-all-done.3 = bf16[8,64,1536]{2,1,0:T(8,128)(2,1)S(1)} async-done(((bf16[8,64,1536]{2,1,0:T(8,128)(2,1)}), bf16[8,64,1536]{2,1,0:T(8,128)(2,1)S(1)}, u32[]{:S(2)}, u32[]{:S(2)}) %all-to-all-start.3) | async-done | bytes 1572896 | tf_op jit(solution)/shard_map/all_to_all | solution.py:446
  147.2 5.8 %time_attend.1 = bf16[16,2,16,384]{3,2,1,0:T(8,128)(2,1)} custom-call(bf16[512,1536]{1,0:T(8,128)(2,1)S(1)} %bitcast.44, bf16[8,576,384]{2,1,0:T(8,128)(2,1)} %bitcast.56), custom_call_target="tpu_custom_call" | custom-call | tf_op jit(solution)/shard_map/time_attend/pallas_call | solution.py:447
  153.0 6.6 %all-to-all-start.4 = ((bf16[16,32,384]{2,1,0:T(8,128)(2,1)}), bf16[16,32,384]{2,1,0:T(8,128)(2,1)S(1)}, u32[]{:S(2)}, u32[]{:S(2)}) async-start(bf16[16,32,384]{2,1,0:T(8,128)(2,1)} %bitcast.29), calls=%async_computation.4 | async-start | bytes 786432 | tf_op jit(solution)/shard_map/all_to_all | solution.py:455
  159.7 1.0 copy.39
  160.6 7.3 %all-to-all-done.4 = bf16[16,32,384]{2,1,0:T(8,128)(2,1)S(1)} async-done(((bf16[16,32,384]{2,1,0:T(8,128)(2,1)}), bf16[16,32,384]{2,1,0:T(8,128)(2,1)S(1)}, u32[]{:S(2)}, u32[]{:S(2)}) %all-to-all-start.4) | async-done | bytes 393248 | tf_op jit(solution)/shard_map/all_to_all | solution.py:455
  (41 shorter events, 5.2 us)
Async XLA Ops:
  7.2 16.2 %copy-start = (bf16[2,2,64,1536]{3,2,1,0:T(8,128)(2,1)S(1)}, bf16[2,2,64,1536]{3,2,1,0:T(8,128)(2,1)}, u32[]{:S(2)}) copy-start(bf16[2,2,64,1536]{3,2,1,0:T(8,128)(2,1)} %param.9) | copy-start | bytes 2359300
  7.2 23.9 %collective-permute-start = (bf16[2,2,64,1536]{3,2,1,0:T(8,128)(2,1)}, bf16[2,2,64,1536]{3,2,1,0:T(8,128)(2,1)S(1)}, u32[]{:S(2)}, u32[]{:S(2)}) collective-permute-start(bf16[2,2,64,1536]{3,2,1,0:T(8,128)(2,1)} %param.9), channel_id=1, source_target_pairs={{0,1},{1,0},{2,3},{3,2},{4,5},{5,4},{6,7},{7,6},{8,9},{9,8},{10,11... | collective-permute-start | bytes 2359304 | tf_op jit(solution)/shard_map/ppermute | solution.py:320
  10.8 1.0 copy-start.1
  11.8 1.0 copy-start.2
  12.9 0.9 copy-start.3
  13.8 11.0 %copy-start.5 = (f32[1536]{0:T(1024)S(1)}, f32[1536]{0:T(1024)}, u32[]{:S(2)}) copy-start(f32[1536]{0:T(1024)} %param.10) | copy-start | bytes 18436
  15.0 26.6 %all-to-all-start = ((bf16[16,48,384]{2,1,0:T(8,128)(2,1)}), bf16[16,48,384]{2,1,0:T(8,128)(2,1)S(1)}, u32[]{:S(2)}, u32[]{:S(2)}) async-start(bf16[16,48,384]{2,1,0:T(8,128)(2,1)} %bitcast.1), calls=%async_computation | async-start | bytes 1179648 | tf_op jit(solution)/shard_map/all_to_all | solution.py:319
  23.3 65.9 %all-gather.5.cloned.1.call-start = ((), (), s32[]{:S(2)}) async-start(), calls=%async_computation.5 | async-start | bytes 6266880 | tf_op jit(solution)/shard_map/all_gather | solution.py:362
  23.4 2.7 %collective-permute-start.1 = (bf16[4,32,1536]{2,1,0:T(8,128)(2,1)S(1)}, bf16[4,32,1536]{2,1,0:T(8,128)(2,1)S(1)}, u32[]{:S(2)}, u32[]{:S(2)}) collective-permute-start(bf16[4,32,1536]{2,1,0:T(8,128)(2,1)S(1)} %dynamic-slice_bitcast_fusion.2), channel_id=1, source_target_pairs={{0,16},{16,0},{1,17},{17,1},{2,18},{18,2},{3,19},{19,3},{4,20},{20... | collective-permute-start | bytes 1179656 | tf_op jit(solution)/shard_map/ppermute | solution.py:323
  31.1 1.8 %collective-permute-start.2 = (bf16[4,32,1536]{2,1,0:T(8,128)(2,1)S(1)}, bf16[4,32,1536]{2,1,0:T(8,128)(2,1)S(1)}, u32[]{:S(2)}, u32[]{:S(2)}) collective-permute-start(bf16[4,32,1536]{2,1,0:T(8,128)(2,1)S(1)} %dynamic-slice_bitcast_fusion.1), channel_id=1, source_target_pairs={{0,16},{16,0},{1,17},{17,1},{2,18},{18,2},{3,19},{19,3},{4,20},{20... | collective-permute-start | bytes 1179656 | tf_op jit(solution)/shard_map/ppermute | solution.py:323
  43.0 42.3 %all-to-all-start.1 = ((bf16[8,64,1536]{2,1,0:T(8,128)(2,1)}), bf16[8,64,1536]{2,1,0:T(8,128)(2,1)S(1)}, u32[]{:S(2)}, u32[]{:S(2)}) async-start(bf16[8,64,1536]{2,1,0:T(8,128)(2,1)} %bitcast.16), calls=%async_computation.1 | async-start | bytes 3145728 | tf_op jit(solution)/shard_map/all_to_all | solution.py:372
  48.5 86.1 %all-gather.7.cloned.1.call-start = ((), (), s32[]{:S(2)}) async-start(), calls=%async_computation.6 | async-start | bytes 3981312 | tf_op jit(solution)/shard_map/all_gather | solution.py:376
  48.7 9.8 %collective-permute-start.3 = (bf16[3,1,96,384]{3,2,0,1:T(8,128)(2,1)S(1)}, bf16[3,1,96,384]{3,2,0,1:T(8,128)(2,1)S(1)}, u32[]{:S(2)}, u32[]{:S(2)}) collective-permute-start(bf16[3,1,96,384]{3,2,0,1:T(8,128)(2,1)S(1)} %reshape.104), channel_id=1, source_target_pairs={{0,1},{1,0},{2,3},{3,2},{4,5},{5,4},{6,7},{7,6},{8,9},{9,8},{10,11... | collective-permute-start | bytes 663560 | tf_op jit(solution)/shard_map/ppermute | solution.py:361
  92.5 2.8 %collective-permute-start.4 = (bf16[2,512,384]{2,1,0:T(8,128)(2,1)S(1)}, bf16[2,512,384]{2,1,0:T(8,128)(2,1)S(1)}, u32[]{:S(2)}, u32[]{:S(2)}) collective-permute-start(bf16[2,512,384]{2,1,0:T(8,128)(2,1)S(1)} %space_keys_values.1.kv_ref), channel_id=1, source_target_pairs={{0,16},{16,0},{1,17},{17,1},{2,18},{18,2},{3,19},{19,3},{4,20},{20... | collective-permute-start | bytes 2359304 | tf_op jit(solution)/shard_map/ppermute | solution.py:387
  95.3 12.8 %copy-start.4 = (f32[1536]{0:T(1024)S(1)}, f32[1536]{0:T(1024)}, u32[]{:S(2)}) copy-start(f32[1536]{0:T(1024)} %param.13) | copy-start | bytes 18436
  99.5 21.3 %all-to-all-start.2 = ((bf16[16,32,384]{2,1,0:T(8,128)(2,1)}), bf16[16,32,384]{2,1,0:T(8,128)(2,1)S(1)}, u32[]{:S(2)}, u32[]{:S(2)}) async-start(bf16[16,32,384]{2,1,0:T(8,128)(2,1)} %bitcast.19), calls=%async_computation.2 | async-start | bytes 786432 | tf_op jit(solution)/shard_map/all_to_all | solution.py:419
  125.2 22.0 %all-to-all-start.3 = ((bf16[8,64,1536]{2,1,0:T(8,128)(2,1)}), bf16[8,64,1536]{2,1,0:T(8,128)(2,1)S(1)}, u32[]{:S(2)}, u32[]{:S(2)}) async-start(bf16[8,64,1536]{2,1,0:T(8,128)(2,1)} %bitcast.55), calls=%async_computation.3 | async-start | bytes 3145728 | tf_op jit(solution)/shard_map/all_to_all | solution.py:446
  131.6 28.0 %collective-permute-start.5 = (bf16[4,32,1536]{2,1,0:T(8,128)(2,1)S(1)}, bf16[4,32,1536]{2,1,0:T(8,128)(2,1)S(1)}, u32[]{:S(2)}, u32[]{:S(2)}) collective-permute-start(bf16[4,32,1536]{2,1,0:T(8,128)(2,1)S(1)} %get-tuple-element.37), channel_id=1, source_target_pairs={{0,16},{16,0},{1,17},{17,1},{2,18},{18,2},{3,19},{19,3},{4,20},{20... | collective-permute-start | bytes 1179656 | tf_op jit(solution)/shard_map/ppermute | solution.py:443
  153.0 15.0 %all-to-all-start.4 = ((bf16[16,32,384]{2,1,0:T(8,128)(2,1)}), bf16[16,32,384]{2,1,0:T(8,128)(2,1)S(1)}, u32[]{:S(2)}, u32[]{:S(2)}) async-start(bf16[16,32,384]{2,1,0:T(8,128)(2,1)} %bitcast.29), calls=%async_computation.4 | async-start | bytes 786432 | tf_op jit(solution)/shard_map/all_to_all | solution.py:455
Sparse Core Ops, SparseCore 0:
  43.1 46.1 all-gather.4
  91.7 31.9 all-gather.6

commit v7 on v6

--- a/solution.py
+++ b/solution.py
@@ -20,6 +20,7 @@
 TM = ("x_lo", "y", "core")
 DP = ("z", "x_hi")
 PLANES = (0, 4, 2, 6, 1, 5, 3, 7)
+SHARDS = [2 * z + x for z in PLANES for x in range(2)]
 BF16 = jnp.bfloat16
 F32 = jnp.float32
 
@@ -34,7 +35,7 @@
 
 def one_hot(shape, order):
     size = math.prod(shape)
-    source = np.arange(size).reshape(shape).transpose(order).reshape(-1)
+    source = np.arange(size).reshape(shape)[SHARDS].transpose(order).reshape(-1)
     return (np.arange(size)[:, None] == source[None]).astype(jnp.bfloat16)
 
 
@@ -316,7 +317,7 @@
         12,
     )(tm.reshape(1).astype(jnp.int32), spatial_project, spatial_output, temporal_project)
     chunk = chunk.reshape(16, 48, HALF)
-    got = lax.all_to_all(chunk, DP, 0, 0, tiled=True)
+    got = lax.all_to_all(chunk, DP, 0, 0, axis_index_groups=[SHARDS], tiled=True)
     across = lax.ppermute(tokens, "x_hi", swap)
 
     def moved(block):
@@ -415,7 +416,8 @@
         24,
         cost=pl.CostEstimate(flops=5_400_000_000, bytes_accessed=15_000_000, transcendentals=0),
     )(hbm(w1), hbm(inner_order), hbm(time_order))
-    gain = time_gain.reshape(16, 4, 2, 2, 6).transpose(1, 2, 3, 0, 4).reshape(1, WIDTH)
+    gain = time_gain.reshape(16, 4, 2, 2, 6)
+    gain = jnp.concatenate([gain[d : d + 1] for d in SHARDS]).transpose(1, 2, 3, 0, 4).reshape(1, WIDTH)
     ctx = lax.all_to_all(ctx.reshape(16, 32, HALF), DP[::-1], 0, 0, tiled=True)
     ctx = ctx.reshape(2, 256, HALF)
     (normed_time,) = call(

time: 176 us -> 181 us (1.028)
  local copies, waits for them, and re-layouts: 6.71 us -> 12.2 us
  starting transfers between devices: 46.2 us -> 41 us
  waiting for transfers between devices: 58.3 us -> 62.7 us
    slice x0 -> x33, local copies, waits for them, and re-layouts: none -> 4.95 us  [per_device(): gain[d:d + 1]]
    all_to_all x1, waiting for transfers between devices: 12.6 us -> 16.9 us  [per_device(): lax.all_to_all(normed_time.reshape(8, 64, WIDTH), TM[:2], 0, 0, tiled=True)]
    ppermute x1, starting transfers between devices: 3.03 us -> 0.85 us  [per_device(): back = lax.ppermute(theirs, 'core', swap)]
    all_to_all x1, starting transfers between devices: 6.58 us -> 4.44 us  [per_device(): lax.all_to_all(context.reshape(16, 32, HALF), TM, 0, 0, tiled=True)]
  transfers between devices with their start and end apart: 13 -> 13, of which waited for: 9 -> 8; matrix products, arithmetic and copies ran while one was open for 2% -> 4% of each run, Pallas kernels for 28% -> 27%
where the time goes in v7:
time: 181 us; the launch traced here: 180 us
  waiting for transfers between devices  62.7 us (35%)
  Pallas kernels  49 us (27%)
  starting transfers between devices  41 us (23%)
  between operations  14.5 us (8%)
  local copies, waits for them, and re-layouts  12.2 us (7%)
    all_to_all x1, waiting for transfers between devices, per_device(): lax.all_to_all(normed.reshape(8, 64, WIDTH), 'z', 0, 0, axis_index_groups...  26.8 us
    all_to_all x1, waiting for transfers between devices, per_device(): lax.all_to_all(normed_time.reshape(8, 64, WIDTH), TM[:2], 0, 0, tiled=True)  16.9 us
    pallas_call x1, Pallas kernels, per_device(): call(weights_kernel, 'output_weights', [HBM] * 3, [(pltpu.HBM, (INNER, WI...  10.6 us
    all_to_all x1, starting transfers between devices, per_device(): ctx = lax.all_to_all(ctx.reshape(16, 32, HALF), DP[::-1], 0, 0, tiled=True)  8.59 us
    all_to_all x1, starting transfers between devices, per_device(): lax.all_to_all(chunk, DP, 0, 0, axis_index_groups=[SHARDS], tiled=True)  8.29 us
    all_to_all x1, waiting for transfers between devices, per_device(): lax.all_to_all(context.reshape(16, 32, HALF), TM, 0, 0, tiled=True)  7.29 us
    pallas_call x1, Pallas kernels, per_device(): call(temporal_kernel, 'time_attend', [VMEM, HBM], [(pltpu.VMEM, (16, 2, 1...  5.76 us
    all_to_all x1, waiting for transfers between devices, per_device(): lax.all_to_all(chunk, DP, 0, 0, axis_index_groups=[SHARDS], tiled=True)  5.63 us
  transfers between devices with their start and end apart: 13, of which 8 were waited for; matrix products, arithmetic and copies ran while one was open for 4% of the time, Pallas kernels for 27%

profile of v7, /device:TPU:1, one launch (start us, length us, event | category | flops | bytes accessed | tf_op | source)
XLA Modules:
  0.0 180.3 jit_solution(12351104850679873093)
XLA Ops:
  7.2 3.7 %collective-permute-start = (bf16[2,2,64,1536]{3,2,1,0:T(8,128)(2,1)}, bf16[2,2,64,1536]{3,2,1,0:T(8,128)(2,1)S(1)}, u32[]{:S(2)}, u32[]{:S(2)}) collective-permute-start(bf16[2,2,64,1536]{3,2,1,0:T(8,128)(2,1)} %param.9), channel_id=1, source_target_pairs={{0,1},{1,0},{2,3},{3,2},{4,5},{5,4},{6,7},{7,6},{8,9},{9,8},{10,11... | collective-permute-start | bytes 2359304 | tf_op jit(solution)/shard_map/ppermute | solution.py:321
  10.8 1.0 copy-done.1
  11.9 1.0 copy-done.2
  12.9 0.9 copy-done.3
  13.8 1.2 weight_rows.1
  15.0 8.3 %all-to-all-start = ((bf16[16,48,384]{2,1,0:T(8,128)(2,1)}), bf16[16,48,384]{2,1,0:T(8,128)(2,1)S(1)}, u32[]{:S(2)}, u32[]{:S(2)}) async-start(bf16[16,48,384]{2,1,0:T(8,128)(2,1)} %bitcast.1), calls=%async_computation | async-start | bytes 1179648 | tf_op jit(solution)/shard_map/all_to_all | solution.py:320
  23.4 1.3 collective-permute-start.1
  24.8 1.3 collective-permute-done.1.moved_ref
  26.1 4.9 %space_norm_own.1 = (bf16[8,32,1536]{2,1,0:T(8,128)(2,1)}, bf16[8,1,32,1536]{3,2,1,0:T(8,128)(2,1)}) custom-call(s32[1]{0:T(128)} %bitcast.2.core_ref, bf16[4,2,32,1536]{3,2,1,0:T(8,128)(2,1)S(1)} %bitcast.49, bf16[4,32,1536]{2,1,0:T(8,128)(2,1)S(1)} %collective-permute-done.1.moved_ref, f32[1,1536]{1,0:T(1,128)S(1)} %reshape.239.gain_ref, ...), custom_call_target="tpu_custom_call" | custom-call | flops 1 | bytes 1 | tf_op jit(solution)/shard_map/space_norm_own/pallas_call | solution.py:332
  31.6 1.3 collective-permute-done.2.moved_ref
  32.9 4.8 %space_norm_other.1 = bf16[8,2,32,1536]{3,2,1,0:T(8,128)(2,1)} custom-call(s32[1]{0:T(128)} %bitcast.2.core_ref, s32[1]{0:T(128)} %bitcast.3.xh_ref, bf16[4,2,32,1536]{3,2,1,0:T(8,128)(2,1)S(1)} %bitcast.51, bf16[4,32,1536]{2,1,0:T(8,128)(2,1)S(1)} %collective-permute-done.2.moved_ref, f32[1,1536]{1,0:T(1,128)S(1)} %reshape.239.gain_ref, ...), custom_call_target="tpu_custom_call" | custom-call | tf_op jit(solution)/shard_map/space_norm_other/pallas_call | solution.py:344
  37.7 5.6 %all-to-all-done = bf16[16,48,384]{2,1,0:T(8,128)(2,1)S(1)} async-done(((bf16[16,48,384]{2,1,0:T(8,128)(2,1)}), bf16[16,48,384]{2,1,0:T(8,128)(2,1)S(1)}, u32[]{:S(2)}, u32[]{:S(2)}) %all-to-all-start) | async-done | bytes 589856 | tf_op jit(solution)/shard_map/all_to_all | solution.py:320
  44.7 5.5 %all-to-all-start.1 = ((bf16[8,64,1536]{2,1,0:T(8,128)(2,1)}), bf16[8,64,1536]{2,1,0:T(8,128)(2,1)S(1)}, u32[]{:S(2)}, u32[]{:S(2)}) async-start(bf16[8,64,1536]{2,1,0:T(8,128)(2,1)} %bitcast.16), calls=%async_computation.1 | async-start | bytes 3145728 | tf_op jit(solution)/shard_map/all_to_all | solution.py:373
  50.4 3.7 %collective-permute-start.3 = (bf16[3,1,96,384]{3,2,0,1:T(8,128)(2,1)S(1)}, bf16[3,1,96,384]{3,2,0,1:T(8,128)(2,1)S(1)}, u32[]{:S(2)}, u32[]{:S(2)}) collective-permute-start(bf16[3,1,96,384]{3,2,0,1:T(8,128)(2,1)S(1)} %reshape.246), channel_id=1, source_target_pairs={{0,1},{1,0},{2,3},{3,2},{4,5},{5,4},{6,7},{7,6},{8,9},{9,8},{10,11... | collective-permute-start | bytes 663560 | tf_op jit(solution)/shard_map/ppermute | solution.py:362
  54.1 4.9 %time_tokens.1.tok_ref = bf16[256,1536]{1,0:T(8,128)(2,1)} custom-call(bf16[256,1536]{1,0:T(8,128)(2,1)} %bitcast.61, bf16[1536,1536]{1,0:T(8,128)(2,1)} %constant.40.clone.order_ref.time_ref), custom_call_target="tpu_custom_call" | custom-call | tf_op jit(solution)/shard_map/time_tokens/pallas_call | solution.py:364
  59.4 0.8 copy.38
  60.2 26.8 %all-to-all-done.1 = bf16[8,64,1536]{2,1,0:T(8,128)(2,1)S(1)} async-done(((bf16[8,64,1536]{2,1,0:T(8,128)(2,1)}), bf16[8,64,1536]{2,1,0:T(8,128)(2,1)S(1)}, u32[]{:S(2)}, u32[]{:S(2)}) %all-to-all-start.1) | async-done | bytes 1572896 | tf_op jit(solution)/shard_map/all_to_all | solution.py:373
  87.0 3.1 %all-gather.5.cloned.1.call-done = bf16[7680,384]{1,0:T(8,128)(2,1)} async-done(((bf16[480,384]{1,0:T(8,128)(2,1)}), bf16[7680,384]{1,0:T(8,128)(2,1)}) %all-gather.5.cloned.1.call-update) | async-done | bytes 5898256 | tf_op jit(solution)/shard_map/all_gather | solution.py:363
  90.1 3.2 %space_keys_values.1.kv_ref = bf16[2,512,384]{2,1,0:T(8,128)(2,1)S(1)} custom-call(bf16[512,1536]{1,0:T(8,128)(2,1)S(1)} %bitcast.42, bf16[16,480,384]{2,1,0:T(8,128)(2,1)} %bitcast.52), custom_call_target="tpu_custom_call" | custom-call | tf_op jit(solution)/shard_map/space_keys_values/pallas_call | solution.py:379
  93.9 2.3 %space_queries.1.q_ref = bf16[512,384]{1,0:T(8,128)(2,1)S(1)} custom-call(bf16[512,1536]{1,0:T(8,128)(2,1)S(1)} %bitcast.43, bf16[16,480,384]{2,1,0:T(8,128)(2,1)} %bitcast.53), custom_call_target="tpu_custom_call" | custom-call | tf_op jit(solution)/shard_map/space_queries/pallas_call | solution.py:390
  96.2 4.2 %space_attend.1 = bf16[2,8,32,384]{3,2,1,0:T(8,128)(2,1)} custom-call(bf16[512,384]{1,0:T(8,128)(2,1)S(1)} %space_queries.1.q_ref, bf16[2,512,384]{2,1,0:T(8,128)(2,1)S(1)} %space_keys_values.1.kv_ref, bf16[2,512,384]{2,1,0:T(8,128)(2,1)S(1)} %collective-permute-done.4.kvo_ref), custom_call_target="tpu_custom_call" | custom-call | tf_op jit(solution)/shard_map/space_attend/pallas_call | solution.py:399
  100.4 8.6 %all-to-all-start.2 = ((bf16[16,32,384]{2,1,0:T(8,128)(2,1)}), bf16[16,32,384]{2,1,0:T(8,128)(2,1)S(1)}, u32[]{:S(2)}, u32[]{:S(2)}) async-start(bf16[16,32,384]{2,1,0:T(8,128)(2,1)} %bitcast.19), calls=%async_computation.2 | async-start | bytes 786432 | tf_op jit(solution)/shard_map/all_to_all | solution.py:421
  115.0 10.6 %output_weights.1 = (bf16[768,1536]{1,0:T(8,128)(2,1)}, bf16[4,768,384]{2,1,0:T(8,128)(2,1)}) custom-call(bf16[16,480,384]{2,1,0:T(8,128)(2,1)} %bitcast.54, bf16[768,768]{1,0:T(8,128)(2,1)} %constant.41.clone.inner_ref, bf16[1536,1536]{1,0:T(8,128)(2,1)} %constant.40.clone.order_ref.time_ref), custom_call_target="tpu_custom_call" | custom-call | flops 5400000000 | bytes 15000000 | tf_op jit(solution)/shard_map/output_weights/pallas_call | solution.py:403
  125.6 4.4 %space_output.1 = bf16[2,256,1536]{2,1,0:T(8,128)(2,1)} custom-call(bf16[2,256,384]{2,1,0:T(8,128)(2,1)S(1)} %bitcast.45, bf16[256,1536]{1,0:T(8,128)(2,1)} %time_tokens.1.tok_ref, bf16[4,768,384]{2,1,0:T(8,128)(2,1)} %get-tuple-element.31.w_ref, f32[1,1536]{1,0:T(1,128)S(1)} %reshape.252.gain_ref), custom_call_target="tpu_custom_call" | custom-call | tf_op jit(solution)/shard_map/space_output/pallas_call | solution.py:423
  130.0 3.6 %all-to-all-start.3 = ((bf16[8,64,1536]{2,1,0:T(8,128)(2,1)}), bf16[8,64,1536]{2,1,0:T(8,128)(2,1)S(1)}, u32[]{:S(2)}, u32[]{:S(2)}) async-start(bf16[8,64,1536]{2,1,0:T(8,128)(2,1)} %bitcast.55), calls=%async_computation.3 | async-start | bytes 3145728 | tf_op jit(solution)/shard_map/all_to_all | solution.py:448
  133.6 2.7 %space_branch.1 = bf16[256,1536]{1,0:T(8,128)(2,1)S(1)} custom-call(bf16[2,256,384]{2,1,0:T(8,128)(2,1)S(1)} %bitcast.46, bf16[768,1536]{1,0:T(8,128)(2,1)} %get-tuple-element.33.w_ref), custom_call_target="tpu_custom_call" | custom-call | tf_op jit(solution)/shard_map/space_branch/pallas_call | solution.py:433
  136.4 0.8 collective-permute-start.5
  137.2 16.9 %all-to-all-done.3 = bf16[8,64,1536]{2,1,0:T(8,128)(2,1)S(1)} async-done(((bf16[8,64,1536]{2,1,0:T(8,128)(2,1)}), bf16[8,64,1536]{2,1,0:T(8,128)(2,1)S(1)}, u32[]{:S(2)}, u32[]{:S(2)}) %all-to-all-start.3) | async-done | bytes 1572896 | tf_op jit(solution)/shard_map/all_to_all | solution.py:448
  154.1 5.8 %time_attend.1 = bf16[16,2,16,384]{3,2,1,0:T(8,128)(2,1)} custom-call(bf16[512,1536]{1,0:T(8,128)(2,1)S(1)} %bitcast.44, bf16[8,576,384]{2,1,0:T(8,128)(2,1)} %bitcast.56), custom_call_target="tpu_custom_call" | custom-call | tf_op jit(solution)/shard_map/time_attend/pallas_call | solution.py:449
  159.9 4.4 %all-to-all-start.4 = ((bf16[16,32,384]{2,1,0:T(8,128)(2,1)}), bf16[16,32,384]{2,1,0:T(8,128)(2,1)S(1)}, u32[]{:S(2)}, u32[]{:S(2)}) async-start(bf16[16,32,384]{2,1,0:T(8,128)(2,1)} %bitcast.29), calls=%async_computation.4 | async-start | bytes 786432 | tf_op jit(solution)/shard_map/all_to_all | solution.py:457
  164.5 1.0 copy.56
  165.4 7.3 %all-to-all-done.4 = bf16[16,32,384]{2,1,0:T(8,128)(2,1)S(1)} async-done(((bf16[16,32,384]{2,1,0:T(8,128)(2,1)}), bf16[16,32,384]{2,1,0:T(8,128)(2,1)S(1)}, u32[]{:S(2)}, u32[]{:S(2)}) %all-to-all-start.4) | async-done | bytes 393248 | tf_op jit(solution)/shard_map/all_to_all | solution.py:457
  (74 shorter events, 9.9 us)
Async XLA Ops:
  7.2 16.2 %copy-start = (bf16[2,2,64,1536]{3,2,1,0:T(8,128)(2,1)S(1)}, bf16[2,2,64,1536]{3,2,1,0:T(8,128)(2,1)}, u32[]{:S(2)}) copy-start(bf16[2,2,64,1536]{3,2,1,0:T(8,128)(2,1)} %param.9) | copy-start | bytes 2359300
  7.2 23.9 %collective-permute-start = (bf16[2,2,64,1536]{3,2,1,0:T(8,128)(2,1)}, bf16[2,2,64,1536]{3,2,1,0:T(8,128)(2,1)S(1)}, u32[]{:S(2)}, u32[]{:S(2)}) collective-permute-start(bf16[2,2,64,1536]{3,2,1,0:T(8,128)(2,1)} %param.9), channel_id=1, source_target_pairs={{0,1},{1,0},{2,3},{3,2},{4,5},{5,4},{6,7},{7,6},{8,9},{9,8},{10,11... | collective-permute-start | bytes 2359304 | tf_op jit(solution)/shard_map/ppermute | solution.py:321
  10.8 1.0 copy-start.1
  11.8 1.0 copy-start.2
  12.9 0.9 copy-start.3
  13.8 11.0 %copy-start.4 = (f32[1536]{0:T(1024)S(1)}, f32[1536]{0:T(1024)}, u32[]{:S(2)}) copy-start(f32[1536]{0:T(1024)} %param.10) | copy-start | bytes 18436
  15.0 28.3 %all-to-all-start = ((bf16[16,48,384]{2,1,0:T(8,128)(2,1)}), bf16[16,48,384]{2,1,0:T(8,128)(2,1)S(1)}, u32[]{:S(2)}, u32[]{:S(2)}) async-start(bf16[16,48,384]{2,1,0:T(8,128)(2,1)} %bitcast.1), calls=%async_computation | async-start | bytes 1179648 | tf_op jit(solution)/shard_map/all_to_all | solution.py:320
  23.3 66.8 %all-gather.5.cloned.1.call-start = ((), (), s32[]{:S(2)}) async-start(), calls=%async_computation.5 | async-start | bytes 6266880 | tf_op jit(solution)/shard_map/all_gather | solution.py:363
  23.4 2.7 %collective-permute-start.1 = (bf16[4,32,1536]{2,1,0:T(8,128)(2,1)S(1)}, bf16[4,32,1536]{2,1,0:T(8,128)(2,1)S(1)}, u32[]{:S(2)}, u32[]{:S(2)}) collective-permute-start(bf16[4,32,1536]{2,1,0:T(8,128)(2,1)S(1)} %dynamic-slice_bitcast_fusion.2), channel_id=1, source_target_pairs={{0,16},{16,0},{1,17},{17,1},{2,18},{18,2},{3,19},{19,3},{4,20},{20... | collective-permute-start | bytes 1179656 | tf_op jit(solution)/shard_map/ppermute | solution.py:324
  31.1 1.8 %collective-permute-start.2 = (bf16[4,32,1536]{2,1,0:T(8,128)(2,1)S(1)}, bf16[4,32,1536]{2,1,0:T(8,128)(2,1)S(1)}, u32[]{:S(2)}, u32[]{:S(2)}) collective-permute-start(bf16[4,32,1536]{2,1,0:T(8,128)(2,1)S(1)} %dynamic-slice_bitcast_fusion.1), channel_id=1, source_target_pairs={{0,16},{16,0},{1,17},{17,1},{2,18},{18,2},{3,19},{19,3},{4,20},{20... | collective-permute-start | bytes 1179656 | tf_op jit(solution)/shard_map/ppermute | solution.py:324
  44.7 42.3 %all-to-all-start.1 = ((bf16[8,64,1536]{2,1,0:T(8,128)(2,1)}), bf16[8,64,1536]{2,1,0:T(8,128)(2,1)S(1)}, u32[]{:S(2)}, u32[]{:S(2)}) async-start(bf16[8,64,1536]{2,1,0:T(8,128)(2,1)} %bitcast.16), calls=%async_computation.1 | async-start | bytes 3145728 | tf_op jit(solution)/shard_map/all_to_all | solution.py:373
  50.2 87.0 %all-gather.7.cloned.1.call-start = ((), (), s32[]{:S(2)}) async-start(), calls=%async_computation.6 | async-start | bytes 3981312 | tf_op jit(solution)/shard_map/all_gather | solution.py:377
  50.4 8.9 %collective-permute-start.3 = (bf16[3,1,96,384]{3,2,0,1:T(8,128)(2,1)S(1)}, bf16[3,1,96,384]{3,2,0,1:T(8,128)(2,1)S(1)}, u32[]{:S(2)}, u32[]{:S(2)}) collective-permute-start(bf16[3,1,96,384]{3,2,0,1:T(8,128)(2,1)S(1)} %reshape.246), channel_id=1, source_target_pairs={{0,1},{1,0},{2,3},{3,2},{4,5},{5,4},{6,7},{7,6},{8,9},{9,8},{10,11... | collective-permute-start | bytes 663560 | tf_op jit(solution)/shard_map/ppermute | solution.py:362
  93.4 2.8 %collective-permute-start.4 = (bf16[2,512,384]{2,1,0:T(8,128)(2,1)S(1)}, bf16[2,512,384]{2,1,0:T(8,128)(2,1)S(1)}, u32[]{:S(2)}, u32[]{:S(2)}) collective-permute-start(bf16[2,512,384]{2,1,0:T(8,128)(2,1)S(1)} %space_keys_values.1.kv_ref), channel_id=1, source_target_pairs={{0,16},{16,0},{1,17},{17,1},{2,18},{18,2},{3,19},{19,3},{4,20},{20... | collective-permute-start | bytes 2359304 | tf_op jit(solution)/shard_map/ppermute | solution.py:388
  96.2 12.8 %copy-start.5 = (f32[1536]{0:T(1024)S(1)}, f32[1536]{0:T(1024)}, u32[]{:S(2)}) copy-start(f32[1536]{0:T(1024)} %param.13) | copy-start | bytes 18436
  100.4 25.2 %all-to-all-start.2 = ((bf16[16,32,384]{2,1,0:T(8,128)(2,1)}), bf16[16,32,384]{2,1,0:T(8,128)(2,1)S(1)}, u32[]{:S(2)}, u32[]{:S(2)}) async-start(bf16[16,32,384]{2,1,0:T(8,128)(2,1)} %bitcast.19), calls=%async_computation.2 | async-start | bytes 786432 | tf_op jit(solution)/shard_map/all_to_all | solution.py:421
  130.0 24.1 %all-to-all-start.3 = ((bf16[8,64,1536]{2,1,0:T(8,128)(2,1)}), bf16[8,64,1536]{2,1,0:T(8,128)(2,1)S(1)}, u32[]{:S(2)}, u32[]{:S(2)}) async-start(bf16[8,64,1536]{2,1,0:T(8,128)(2,1)} %bitcast.55), calls=%async_computation.3 | async-start | bytes 3145728 | tf_op jit(solution)/shard_map/all_to_all | solution.py:448
  136.4 28.0 %collective-permute-start.5 = (bf16[4,32,1536]{2,1,0:T(8,128)(2,1)S(1)}, bf16[4,32,1536]{2,1,0:T(8,128)(2,1)S(1)}, u32[]{:S(2)}, u32[]{:S(2)}) collective-permute-start(bf16[4,32,1536]{2,1,0:T(8,128)(2,1)S(1)} %get-tuple-element.37), channel_id=1, source_target_pairs={{0,16},{16,0},{1,17},{17,1},{2,18},{18,2},{3,19},{19,3},{4,20},{20... | collective-permute-start | bytes 1179656 | tf_op jit(solution)/shard_map/ppermute | solution.py:445
  159.9 12.8 %all-to-all-start.4 = ((bf16[16,32,384]{2,1,0:T(8,128)(2,1)}), bf16[16,32,384]{2,1,0:T(8,128)(2,1)S(1)}, u32[]{:S(2)}, u32[]{:S(2)}) async-start(bf16[16,32,384]{2,1,0:T(8,128)(2,1)} %bitcast.29), calls=%async_computation.4 | async-start | bytes 786432 | tf_op jit(solution)/shard_map/all_to_all | solution.py:457
Sparse Core Ops, SparseCore 0:
  44.8 45.2 all-gather.4
  92.5 31.9 all-gather.6
